TPU v7x, 32 devices: a whole 2x2x4 slice. The times are simulated.
32 devices in a mesh: dp: 8 (over z, x), replica: 4 (over y, core).
Axes of the slice: x: 2, y: 2, z: 4, core: 2. Of those that a mesh axis runs over, the one named last changes fastest.
Arguments:
- grad_parts: bfloat16 [64, 1024, 512], P('dp', 'replica'), may hold values from -1.1953125 to 1.1953125
- master_weight: float32 [8192, 512], P(('dp', 'replica')), may hold values from -0.0625 to 0.0625
- moment_one: float32 [8192, 512], P(('dp', 'replica')), may hold values from -1.8 to 1.8
- moment_two: float32 [8192, 512], P(('dp', 'replica')), may hold values from 0.05 to 2
- queries: bfloat16 [4, 1024, 4096], P('replica', 'dp'), may hold values from -5 to 5
- keys_in: bfloat16 [4, 1024, 512], P('replica', 'dp'), may hold values from -5 to 5
- hidden: bfloat16 [4, 1024, 8192], P('replica', 'dp'), may hold values from -6 to 6
- segment_ids: int32 [4, 1024], P('replica', 'dp'), may hold values from 0 to 4, never falling along the last dimension, each value on 1 to 384 neighbouring positions
- packed_len: int32 [4], P('replica'), may hold values from 512 to 1024
Outputs:
- new_master: float32 [8192, 512], P(('dp', 'replica'))
- new_first: float32 [8192, 512], P(('dp', 'replica'))
- new_second: float32 [8192, 512], P(('dp', 'replica'))
- attended: bfloat16 [4, 1024, 4096], P('replica', 'dp')
Inputs may be any that keep to these rules, and one draw needn't show every extreme that they name: `segment_ids`: on each replica the numbers never fall along positions, and each prompt covers at most 384 positions, one exactly that many.
All inputs are finite; a program needn't handle non-finite values.
Results may differ from a plain program's by a relative error of at most 0.009.
Values may be sent and summed in bfloat16 or wider, within the bound.
No kernel may reach another device: no remote copies, remote signals or barrier semaphores. Data moves between devices by JAX's collectives and lax.ppermute only.
A program may use at most 64 MiB of HBM per device.

v0:
```python
import jax
import jax.numpy as jnp
from jax import lax
from jax.sharding import PartitionSpec as P

HD = 128


beta_one = 0.9
beta_two = 0.95
bias_one = 1.0 - 0.9**10
bias_two = 1.0 - 0.95**10
adam_eps = 1e-08
learn_rate = 0.002
weight_decay = 0.1


def passed_along(block, axis, distance):
    devices = range(lax.axis_size(axis))
    route = [(i - distance, i) for i in devices if i - distance in devices]
    return lax.ppermute(block, axis, route)


def adam_update(grad_sum, master, moment_first, moment_second):
    first_new = beta_one * moment_first + (1.0 - beta_one) * grad_sum
    second_new = beta_two * moment_second + (1.0 - beta_two) * grad_sum * grad_sum
    step_dir = (
        first_new / bias_one / (jnp.sqrt(second_new / bias_two) + adam_eps) + weight_decay * master
    )
    master_new = master - learn_rate * step_dir
    return (master_new, first_new, second_new, master_new.astype(jnp.bfloat16))


def prefill(queries, keys_in, value_states, segment_ids, packed_len):
    local_len = queries.shape[1]
    heads_kv = keys_in.shape[2] // HD
    groups = queries.shape[2] // keys_in.shape[2]
    device_pos = lax.axis_index("dp")
    seg_here = segment_ids[0].astype(jnp.bfloat16)
    steps_back = jnp.arange(local_len, dtype=jnp.int32)
    key_list = []
    value_list = []
    seg_list = []
    valid_list = []
    pos_list = []
    for offset in (3, 2, 1):
        moved_keys, moved_values, moved_segs = passed_along(
            (keys_in[0], value_states, seg_here), "dp", offset
        )
        key_list.append(moved_keys)
        value_list.append(moved_values)
        seg_list.append(moved_segs)
        valid_list.append(jnp.broadcast_to(device_pos >= offset, (local_len,)))
        pos_list.append((device_pos - offset) * local_len + steps_back)
    key_list.append(keys_in[0])
    value_list.append(value_states)
    seg_list.append(seg_here)
    valid_list.append(jnp.ones((local_len,), jnp.bool_))
    query_pos = device_pos * local_len + steps_back
    pos_list.append(query_pos)
    all_keys = jnp.concatenate(key_list, axis=0).reshape(4 * local_len, heads_kv, HD)
    all_values = jnp.concatenate(value_list, axis=0).reshape(4 * local_len, heads_kv, HD)
    seg_keys = jnp.concatenate(seg_list, axis=0)
    key_valid = jnp.concatenate(valid_list, axis=0)
    key_pos = jnp.concatenate(pos_list, axis=0)
    allowed = (
        (seg_here[:, None] == seg_keys[None, :])
        & (key_pos[None, :] <= query_pos[:, None])
        & key_valid[None, :]
    )
    query_heads = queries[0].reshape(local_len, heads_kv, groups, HD)
    scores = jnp.einsum(
        "qhgd,khd->hgqk", query_heads, all_keys, preferred_element_type=jnp.float32
    ) * HD ** (-0.5)
    scores = jnp.where(allowed, scores, -jnp.inf)
    row_max = jnp.max(scores, axis=-1, keepdims=True)
    weights = jnp.where(allowed, jnp.exp(scores - row_max), 0.0)
    totals = jnp.sum(weights, axis=-1, keepdims=True)
    rounded = weights.astype(jnp.bfloat16)
    mixed_out = jnp.einsum(
        "hgqk,khd->qhgd", rounded, all_values, preferred_element_type=jnp.float32
    )
    mixed_out = mixed_out / jnp.transpose(totals, (2, 0, 1, 3))
    mixed_out = mixed_out.reshape(local_len, heads_kv * groups * HD)
    query_live = query_pos < packed_len[0]
    return jnp.where(query_live[:, None], mixed_out, 0.0).astype(jnp.bfloat16)[None]


def on_device(
    grad_parts,
    master_weight,
    moment_one,
    moment_two,
    queries,
    keys_in,
    hidden,
    segment_ids,
    packed_len,
):
    grad_terms = grad_parts.astype(jnp.float32)
    grad_sum = lax.psum_scatter(
        grad_terms.astype(jnp.bfloat16), "dp", scatter_dimension=0, tiled=True
    ).astype(jnp.float32)[0]
    new_master, new_first, new_second, rounded_rows = adam_update(
        grad_sum, master_weight, moment_one, moment_two
    )
    hidden_rows = hidden[0]
    group_rows = lax.all_gather(rounded_rows, "replica", axis=0, tiled=True)
    projected = jnp.dot(
        hidden_rows,
        lax.all_gather(group_rows, "dp", axis=0, tiled=True),
        preferred_element_type=jnp.float32,
    )
    value_states = projected.astype(jnp.bfloat16)
    attended = prefill(queries, keys_in, value_states, segment_ids, packed_len)
    return (new_master, new_first, new_second, attended)


def solution(mesh):
    in_specs = (
        P("dp", "replica", None),
        P(("dp", "replica"), None),
        P(("dp", "replica"), None),
        P(("dp", "replica"), None),
        P("replica", "dp", None),
        P("replica", "dp", None),
        P("replica", "dp", None),
        P("replica", "dp"),
        P("replica"),
    )
    out_specs = (
        P(("dp", "replica"), None),
        P(("dp", "replica"), None),
        P(("dp", "replica"), None),
        P("replica", "dp", None),
    )
    return jax.shard_map(
        on_device, mesh=mesh, in_specs=in_specs, out_specs=out_specs, check_vma=False
    )
```

profile of v0, /device:TPU:0, one launch (start us, length us, event | category | flops | bytes accessed | tf_op | source)
XLA Modules:
  0.0 272.8 jit_solution(7231010512074524962)
XLA Ops:
  7.2 0.0 copy-start
  7.2 0.0 reduce-scatter.2.cloned.1.call-start
  7.2 0.7 reduce-scatter.2.cloned.1.call-update
  7.9 0.0 all-gather.3.cloned.1.call-start
  8.0 74.4 %reduce-scatter.2.cloned.1.call-done = bf16[1,256,512]{2,1,0:T(8,128)(2,1)} async-done(((bf16[8,256,512]{2,1,0:T(8,128)(2,1)}), bf16[1,256,512]{2,1,0:T(8,128)(2,1)}) %reduce-scatter.2.cloned.1.call-update) | async-done | bytes 262160 | tf_op jit(solution)/shard_map/reduce_scatter | solution.py:101
  82.4 2.9 %fusion.30 = (bf16[256,512]{1,0:T(8,128)(2,1)}, f32[256,512]{1,0:T(8,128)}, f32[256,512]{1,0:T(8,128)}, f32[256,512]{1,0:T(8,128)}) fusion(f32[256,512]{1,0:T(8,128)} %param.10, bf16[1,256,512]{2,1,0:T(8,128)(2,1)} %reduce-scatter.2.cloned.1.call-done, f32[256,512]{1,0:T(8,128)} %param.11, f32[256,512]{1,0:T(8,128)} %param.12), kind=kLoop, calls=%fused_computation.44 | loop fusion | flops 2228224 | bytes 3670016 | tf_op jit(solution)/shard_map/convert_element_type | solution.py:31
  85.4 0.0 all-gather.3.cloned.1.call-update
  85.4 0.0 all-gather.5.cloned.1.call-start
  85.4 15.9 %all-gather.3.cloned.1.call-done = bf16[1024,512]{1,0:T(8,128)(2,1)} async-done(((bf16[256,512]{1,0:T(8,128)(2,1)}), bf16[1024,512]{1,0:T(8,128)(2,1)}) %all-gather.3.cloned.1.call-update) | async-done | bytes 1048592 | tf_op jit(solution)/shard_map/all_gather | solution.py:108
  101.3 0.0 all-gather.5.cloned.1.call-update
  101.3 0.7 convert_bitcast_fusion
  102.0 3.9 %collective-permute-start.5 = (bf16[128]{0:T(256)(128)(2,1)S(1)}, bf16[128]{0:T(256)(128)(2,1)}, u32[]{:S(2)}, u32[]{:S(2)}) collective-permute-start(bf16[128]{0:T(256)(128)(2,1)S(1)} %convert_bitcast_fusion), channel_id=1, source_target_pairs={{0,4},{4,8},{8,12},{12,16},{16,20},{20,24},{24,28},{1,5},{5,9},{9,... | collective-permute-start | bytes 776 | tf_op jit(solution)/shard_map/ppermute | solution.py:21
  105.9 3.4 %collective-permute-start.4 = (bf16[128]{0:T(256)(128)(2,1)S(1)}, bf16[128]{0:T(256)(128)(2,1)}, u32[]{:S(2)}, u32[]{:S(2)}) collective-permute-start(bf16[128]{0:T(256)(128)(2,1)S(1)} %convert_bitcast_fusion), channel_id=1, source_target_pairs={{0,8},{4,12},{8,16},{12,20},{16,24},{20,28},{1,9},{5,13},{9,17},{1... | collective-permute-start | bytes 776 | tf_op jit(solution)/shard_map/ppermute | solution.py:21
  109.3 4.3 %collective-permute-start.3 = (bf16[128]{0:T(256)(128)(2,1)S(1)}, bf16[128]{0:T(256)(128)(2,1)}, u32[]{:S(2)}, u32[]{:S(2)}) collective-permute-start(bf16[128]{0:T(256)(128)(2,1)S(1)} %convert_bitcast_fusion), channel_id=1, source_target_pairs={{0,12},{4,16},{8,20},{12,24},{16,28},{1,13},{5,17},{9,21},{13,25},... | collective-permute-start | bytes 776 | tf_op jit(solution)/shard_map/ppermute | solution.py:21
  113.6 1.7 copy.17
  115.3 3.4 %collective-permute-start.8 = (bf16[128,512]{0,1:T(8,128)(2,1)}, bf16[128,512]{0,1:T(8,128)(2,1)S(1)}, u32[]{:S(2)}, u32[]{:S(2)}) collective-permute-start(bf16[128,512]{0,1:T(8,128)(2,1)} %bitcast.9), channel_id=1, source_target_pairs={{0,4},{4,8},{8,12},{12,16},{16,20},{20,24},{24,28},{1,5},{5,9},{9,... | collective-permute-start | bytes 393224 | tf_op jit(solution)/shard_map/ppermute | solution.py:21
  118.7 1.3 collective-permute-start.7
  120.7 0.5 broadcast_compare_fusion
  121.2 1.0 copy.22
  122.3 1.4 copy.31
  123.7 0.0 collective-permute-done.5
  123.7 2.7 collective-permute-start.6
  126.4 0.0 collective-permute-done.4
  126.4 0.0 collective-permute-done.3
  126.4 0.7 pad_maximum_fusion.1
  127.1 0.9 and_and_fusion
  128.0 0.0 collective-permute-done.8
  128.0 0.0 copy-start.3
  128.0 0.7 copy-done.3
  128.7 1.0 copy.21
  129.7 0.0 collective-permute-done.7
  129.7 0.0 copy-start.2
  129.7 0.6 copy-done.2
  130.4 1.0 copy.20
  131.4 0.9 collective-permute-done.6
  132.3 1.7 copy.19
  133.9 5.4 %fusion.17 = f32[4,512,128,8]{2,1,3,0:T(8,128)} fusion(bf16[128,4,8,128]{3,2,1,0:T(8,128)(2,1)S(1)} %bitcast.60, bf16[128,4,128]{2,0,1:T(8,128)(2,1)S(1)} %copy.22, bf16[128,4,128]{2,0,1:T(8,128)(2,1)S(1)} %copy.21, bf16[128,4,128]{2,0,1:T(8,128)(2,1)S(1)} %copy.20, bf16[128,4,128]{2,0,1:T(8,128)(2,1)} %copy.19), kind=kOutput, calls=%fused_computation.15 | convolution fusion | flops 538968064 | bytes 9961472 | tf_op jit(solution)/shard_map/qhgd,khd->hgqk/dot_general | solution.py:72
  139.4 0.0 copy-start.4
  139.4 100.1 %all-gather.5.cloned.1.call-done = bf16[8192,512]{1,0:T(8,128)(2,1)} async-done(((bf16[1024,512]{1,0:T(8,128)(2,1)}), bf16[8192,512]{1,0:T(8,128)(2,1)}) %all-gather.5.cloned.1.call-update) | async-done | bytes 8388624 | tf_op jit(solution)/shard_map/all_gather | solution.py:111
  239.5 0.0 copy-done
  239.5 0.0 copy-start.1
  239.5 4.8 %fusion.14 = bf16[128,512]{1,0:T(8,128)(2,1)S(1)} fusion(bf16[8192,512]{1,0:T(8,128)(2,1)} %all-gather.5.cloned.1.call-done, bf16[1,128,8192]{2,1,0:T(8,128)(2,1)S(1)} %copy-done), kind=kOutput, calls=%fused_computation.14 | convolution fusion | flops 1073807360 | bytes 10616832 | tf_op jit(solution)/shard_map/dot_general | solution.py:109
  244.3 2.5 collective-permute-start.2
  246.8 1.5 collective-permute-start.1
  248.2 5.2 %collective-permute-start = (bf16[128,512]{1,0:T(8,128)(2,1)S(1)}, bf16[128,512]{1,0:T(8,128)(2,1)S(1)}, u32[]{:S(2)}, u32[]{:S(2)}) collective-permute-start(bf16[128,512]{1,0:T(8,128)(2,1)S(1)} %fusion.14), channel_id=1, source_target_pairs={{0,12},{4,16},{8,20},{12,24},{16,28},{1,13},{5,17},{9,21},{13,25},... | collective-permute-start | bytes 393224 | tf_op jit(solution)/shard_map/ppermute | solution.py:21
  253.5 0.0 copy-done.4
  253.5 0.0 copy-done.1
  253.5 5.9 %fusion.33 = (f32[4,8,128]{2,1,0:T(8,128)S(1)}, bf16[4,8,128,512]{2,3,1,0:T(8,128)(2,1)}) fusion(f32[4,512,128,8]{2,1,3,0:T(8,128)S(1)} %copy-done.1, pred[128,512]{0,1:T(8,128)(4,1)S(1)} %copy-done.4), kind=kOutput, calls=%fused_computation.45 | output fusion | flops 16777728 | bytes 12664832 | tf_op jit(solution)/shard_map/sub | solution.py:77
  259.3 0.0 collective-permute-done.2
  259.3 0.0 collective-permute-done.1
  259.3 0.0 collective-permute-done
  259.4 0.2 copy.30
  259.6 0.0 copy-start.5
  259.6 3.9 %bitcast_divide_fusion = bf16[128,4,8,128]{0,3,2,1:T(8,128)(2,1)} fusion(bf16[512,4,128,1]{0,2,3,1:T(8,128)(2,1)S(1)} %bitcast.63, bf16[4,8,128,512]{2,3,1,0:T(8,128)(2,1)} %get-tuple-element.9, f32[128,4,8]{0,2,1:T(8,128)S(1)} %bitcast.66), kind=kOutput, calls=%fused_computation.9 | convolution fusion | flops 537919488 | bytes 5783552 | tf_op jit(solution)/shard_map/hgqk,khd->qhgd/dot_general | solution.py:80
  263.5 1.5 copy.26
  265.0 0.0 copy-done.5
  265.0 1.2 select_convert_fusion
  (10 shorter events, 0.1 us)
Async XLA Ops:
  7.2 232.3 %copy-start = (bf16[1,128,8192]{2,1,0:T(8,128)(2,1)S(1)}, bf16[1,128,8192]{2,1,0:T(8,128)(2,1)}, u32[]{:S(2)}) copy-start(bf16[1,128,8192]{2,1,0:T(8,128)(2,1)} %param.15) | copy-start | bytes 6291460
  7.2 75.2 %reduce-scatter.2.cloned.1.call-start = ((), (), s32[]{:S(2)}) async-start(), calls=%async_computation.1 | async-start | bytes 2359296 | tf_op jit(solution)/shard_map/reduce_scatter | solution.py:101
  7.9 93.4 %all-gather.3.cloned.1.call-start = ((), (), s32[]{:S(2)}) async-start(), calls=%async_computation.2 | async-start | bytes 1310720 | tf_op jit(solution)/shard_map/all_gather | solution.py:108
  85.4 154.1 %all-gather.5.cloned.1.call-start = ((), (), s32[]{:S(2)}) async-start(), calls=%async_computation.3 | async-start | bytes 9437184 | tf_op jit(solution)/shard_map/all_gather | solution.py:111
  102.0 21.7 %collective-permute-start.5 = (bf16[128]{0:T(256)(128)(2,1)S(1)}, bf16[128]{0:T(256)(128)(2,1)}, u32[]{:S(2)}, u32[]{:S(2)}) collective-permute-start(bf16[128]{0:T(256)(128)(2,1)S(1)} %convert_bitcast_fusion), channel_id=1, source_target_pairs={{0,4},{4,8},{8,12},{12,16},{16,20},{20,24},{24,28},{1,5},{5,9},{9,... | collective-permute-start | bytes 776 | tf_op jit(solution)/shard_map/ppermute | solution.py:21
  105.9 20.5 %collective-permute-start.4 = (bf16[128]{0:T(256)(128)(2,1)S(1)}, bf16[128]{0:T(256)(128)(2,1)}, u32[]{:S(2)}, u32[]{:S(2)}) collective-permute-start(bf16[128]{0:T(256)(128)(2,1)S(1)} %convert_bitcast_fusion), channel_id=1, source_target_pairs={{0,8},{4,12},{8,16},{12,20},{16,24},{20,28},{1,9},{5,13},{9,17},{1... | collective-permute-start | bytes 776 | tf_op jit(solution)/shard_map/ppermute | solution.py:21
  109.3 17.1 %collective-permute-start.3 = (bf16[128]{0:T(256)(128)(2,1)S(1)}, bf16[128]{0:T(256)(128)(2,1)}, u32[]{:S(2)}, u32[]{:S(2)}) collective-permute-start(bf16[128]{0:T(256)(128)(2,1)S(1)} %convert_bitcast_fusion), channel_id=1, source_target_pairs={{0,12},{4,16},{8,20},{12,24},{16,28},{1,13},{5,17},{9,21},{13,25},... | collective-permute-start | bytes 776 | tf_op jit(solution)/shard_map/ppermute | solution.py:21
  115.3 12.7 %collective-permute-start.8 = (bf16[128,512]{0,1:T(8,128)(2,1)}, bf16[128,512]{0,1:T(8,128)(2,1)S(1)}, u32[]{:S(2)}, u32[]{:S(2)}) collective-permute-start(bf16[128,512]{0,1:T(8,128)(2,1)} %bitcast.9), channel_id=1, source_target_pairs={{0,4},{4,8},{8,12},{12,16},{16,20},{20,24},{24,28},{1,5},{5,9},{9,... | collective-permute-start | bytes 393224 | tf_op jit(solution)/shard_map/ppermute | solution.py:21
  118.7 11.0 %collective-permute-start.7 = (bf16[128,512]{0,1:T(8,128)(2,1)}, bf16[128,512]{0,1:T(8,128)(2,1)S(1)}, u32[]{:S(2)}, u32[]{:S(2)}) collective-permute-start(bf16[128,512]{0,1:T(8,128)(2,1)} %bitcast.9), channel_id=1, source_target_pairs={{0,8},{4,12},{8,16},{12,20},{16,24},{20,28},{1,9},{5,13},{9,17},{1... | collective-permute-start | bytes 393224 | tf_op jit(solution)/shard_map/ppermute | solution.py:21
  123.7 8.5 %collective-permute-start.6 = (bf16[128,512]{0,1:T(8,128)(2,1)}, bf16[128,512]{0,1:T(8,128)(2,1)}, u32[]{:S(2)}, u32[]{:S(2)}) collective-permute-start(bf16[128,512]{0,1:T(8,128)(2,1)} %bitcast.9), channel_id=1, source_target_pairs={{0,12},{4,16},{8,20},{12,24},{16,28},{1,13},{5,17},{9,21},{13,25},... | collective-permute-start | bytes 393224 | tf_op jit(solution)/shard_map/ppermute | solution.py:21
  128.0 0.7 copy-start.3
  129.7 0.7 copy-start.2
  139.4 114.1 %copy-start.4 = (pred[128,512]{0,1:T(8,128)(4,1)S(1)}, pred[128,512]{0,1:T(8,128)(4,1)}, u32[]{:S(2)}) copy-start(pred[128,512]{0,1:T(8,128)(4,1)} %and_and_fusion) | copy-start | bytes 196612
  239.5 14.0 %copy-start.1 = (f32[4,512,128,8]{2,1,3,0:T(8,128)S(1)}, f32[4,512,128,8]{2,1,3,0:T(8,128)}, u32[]{:S(2)}) copy-start(f32[4,512,128,8]{2,1,3,0:T(8,128)} %fusion.17) | copy-start | bytes 25165828
  244.3 15.0 %collective-permute-start.2 = (bf16[128,512]{1,0:T(8,128)(2,1)S(1)}, bf16[128,512]{1,0:T(8,128)(2,1)S(1)}, u32[]{:S(2)}, u32[]{:S(2)}) collective-permute-start(bf16[128,512]{1,0:T(8,128)(2,1)S(1)} %fusion.14), channel_id=1, source_target_pairs={{0,4},{4,8},{8,12},{12,16},{16,20},{20,24},{24,28},{1,5},{5,9},{9,... | collective-permute-start | bytes 393224 | tf_op jit(solution)/shard_map/ppermute | solution.py:21
  246.8 12.6 %collective-permute-start.1 = (bf16[128,512]{1,0:T(8,128)(2,1)S(1)}, bf16[128,512]{1,0:T(8,128)(2,1)S(1)}, u32[]{:S(2)}, u32[]{:S(2)}) collective-permute-start(bf16[128,512]{1,0:T(8,128)(2,1)S(1)} %fusion.14), channel_id=1, source_target_pairs={{0,8},{4,12},{8,16},{12,20},{16,24},{20,28},{1,9},{5,13},{9,17},{1... | collective-permute-start | bytes 393224 | tf_op jit(solution)/shard_map/ppermute | solution.py:21
  248.2 11.1 %collective-permute-start = (bf16[128,512]{1,0:T(8,128)(2,1)S(1)}, bf16[128,512]{1,0:T(8,128)(2,1)S(1)}, u32[]{:S(2)}, u32[]{:S(2)}) collective-permute-start(bf16[128,512]{1,0:T(8,128)(2,1)S(1)} %fusion.14), channel_id=1, source_target_pairs={{0,12},{4,16},{8,20},{12,24},{16,28},{1,13},{5,17},{9,21},{13,25},... | collective-permute-start | bytes 393224 | tf_op jit(solution)/shard_map/ppermute | solution.py:21
  259.6 5.4 %copy-start.5 = (pred[128]{0:T(512)(128)(4,1)S(1)}, pred[128]{0:T(512)(128)(4,1)}, u32[]{:S(2)}) copy-start(pred[128]{0:T(512)(128)(4,1)} %broadcast_compare_fusion) | copy-start | bytes 388
Sparse Core Ops, SparseCore 0:
  11.5 70.8 reduce-scatter.1
  85.5 15.7 all-gather.2
  103.4 136.0 all-gather.4
where the time goes:
time: 273 us
  waiting for transfers between devices  192 us (70%)
  starting transfers between devices  28.2 us (10%)
  between operations  14.6 us (5%)
  matrix products  14.1 us (5%)
  other arithmetic  12.9 us (5%)
  local copies, waits for them, and re-layouts  10.9 us (4%)
    all_gather x1, waiting for transfers between devices, on_device(): lax.all_gather(group_rows, 'dp', axis=0, tiled=True)  100 us
    reduce_scatter x1, waiting for transfers between devices, on_device(): lax.psum_scatter(grad_terms.astype(jnp.bfloat16), 'dp', scatter_dimension...  74.4 us
    ppermute x9, starting transfers between devices, passed_along(): return lax.ppermute(block, axis, route)  28.1 us
    all_gather x1, waiting for transfers between devices, on_device(): group_rows = lax.all_gather(rounded_rows, 'replica', axis=0, tiled=True)  15.9 us
    sub x1, other arithmetic, prefill(): weights = jnp.where(allowed, jnp.exp(scores - row_max), 0.0)  5.85 us
  transfers between devices with their start and end apart: 12, of which 4 were waited for; matrix products, arithmetic and copies ran while one was open for 8% of the time, Pallas kernels for 0%

commit v1 on v0

v1 whole, which is shorter than its diff:
```python
import jax
import jax.numpy as jnp
from jax import lax
from jax.experimental import pallas as pl
from jax.experimental.pallas import tpu as pltpu
from jax.sharding import PartitionSpec as P

HD = 128
ALL = ("dp", "replica")

beta_one = 0.9
beta_two = 0.95
bias_one = 1.0 - 0.9**10
bias_two = 1.0 - 0.95**10
adam_eps = 1e-08
learn_rate = 0.002
weight_decay = 0.1


def bits_of(count):
    return [1 << j for j in range(count.bit_length() - 1)]


def swapped(block, mask):
    total = lax.axis_size("dp") * lax.axis_size("replica")
    return lax.ppermute(block, ALL, [(i, i ^ mask) for i in range(total)])


def passed_along(block, distance):
    devices = range(lax.axis_size("dp"))
    route = [(i - distance, i) for i in devices if i - distance in devices]
    return lax.ppermute(block, "dp", route)


def adam_update(grad_sum, master, moment_first, moment_second):
    first_new = beta_one * moment_first + (1.0 - beta_one) * grad_sum
    second_new = beta_two * moment_second + (1.0 - beta_two) * grad_sum * grad_sum
    step_dir = (
        first_new / bias_one / (jnp.sqrt(second_new / bias_two) + adam_eps) + weight_decay * master
    )
    master_new = master - learn_rate * step_dir
    return (master_new, first_new, second_new)


def summed_to_owner(terms, order):
    n_dp, rows, columns = terms.shape
    names = bits_of(n_dp)[::-1]
    me = lax.axis_index("dp")
    n_replica = lax.axis_size("replica")
    held = terms.reshape((2,) * len(names) + (rows, columns))
    for step, bit in enumerate(order):
        axis = names.index(bit)
        names = names[:axis] + names[axis + 1 :]
        mine = (me // bit) % 2
        away = lax.dynamic_index_in_dim(held, 1 - mine, axis, keepdims=False)
        kept = lax.dynamic_index_in_dim(held, mine, axis, keepdims=False)
        came = swapped(away, bit * n_replica)
        held = kept.astype(jnp.float32) + came.astype(jnp.float32)
        if step < len(order) - 1:
            held = held.astype(jnp.bfloat16)
    return held


def gathered(rows, order):
    n_replica = lax.axis_size("replica")
    held, labels = rows, [0]
    for bit in order[:-1]:
        held = jnp.concatenate([held, swapped(held, bit * n_replica)], axis=0)
        labels = labels + [label ^ bit for label in labels]
    last = swapped(held, order[-1] * n_replica)
    return held, last, labels + [label ^ order[-1] for label in labels]


def packed_columns(hidden_rows, picks, width):
    tokens = hidden_rows.shape[0]
    offsets, blocks = picks.shape
    if width % HD:
        cut = hidden_rows.reshape(tokens, -1, width)
        taken = jnp.take(cut, picks.reshape(-1), axis=1).reshape(tokens, offsets, blocks * width)
        return jnp.transpose(taken, (1, 0, 2))

    def kernel(picks_ref, source_ref, out_ref, sems):
        copies = []
        for m in range(offsets):
            for o in range(blocks):
                start = pl.multiple_of(picks_ref[m, o] * width, width)
                copies.append(
                    pltpu.make_async_copy(
                        source_ref.at[:, pl.ds(start, width)],
                        out_ref.at[m, :, pl.ds(o * width, width)],
                        sems.at[m, o],
                    )
                )
        for copy in copies:
            copy.start()
        for copy in copies:
            copy.wait()

    return pl.pallas_call(
        kernel,
        out_shape=jax.ShapeDtypeStruct((offsets, tokens, blocks * width), hidden_rows.dtype),
        in_specs=[
            pl.BlockSpec(memory_space=pltpu.SMEM),
            pl.BlockSpec(memory_space=pl.ANY),
        ],
        out_specs=pl.BlockSpec(memory_space=pl.ANY),
        scratch_shapes=[pltpu.SemaphoreType.DMA((offsets, blocks))],
        cost_estimate=pl.CostEstimate(
            flops=0, bytes_accessed=4 * hidden_rows.size, transcendentals=0
        ),
        name="pack_hidden",
    )(picks, hidden_rows)


def attention_weights(place, queries, seg_column, key_blocks):
    tokens = queries.shape[1]
    heads_kv = key_blocks[0].shape[1] // HD
    groups = queries.shape[2] // (heads_kv * HD)
    spans = len(key_blocks)
    padded = key_blocks[0].shape[0]
    keys_all = spans * tokens

    def kernel(place_ref, q_ref, seg_ref, *rest):
        key_refs, out_ref = rest[:-1], rest[-1]
        here, used = place_ref[0], place_ref[1]
        keys = jnp.concatenate([ref[0:tokens, :] for ref in key_refs], axis=0)
        seg_keys = jnp.concatenate(
            [ref[tokens : tokens + 16, :].astype(jnp.float32)[0:1, :] for ref in key_refs], axis=1
        )
        row = lax.broadcasted_iota(jnp.int32, (tokens, keys_all), 0)
        column = lax.broadcasted_iota(jnp.int32, (tokens, keys_all), 1)
        offset = column - (spans - 1) * tokens
        allowed = (
            (seg_ref[...] == seg_keys) & (offset <= row) & (offset + here * tokens >= 0)
        )
        live = (here * tokens + lax.broadcasted_iota(jnp.int32, (tokens, 1), 0)) < used
        for j in range(groups):
            scores = lax.dot_general(
                q_ref[0, :, j * HD : (j + 1) * HD],
                keys,
                (((1,), (1,)), ((), ())),
                preferred_element_type=jnp.float32,
            ) * HD ** (-0.5)
            scores = jnp.where(allowed, scores, -1e30)
            weights = jnp.exp(scores - jnp.max(scores, axis=-1, keepdims=True))
            totals = jnp.sum(weights, axis=-1, keepdims=True)
            scale = jnp.where(live, 1.0 / totals, 0.0)
            out_ref[0, j * tokens : (j + 1) * tokens, :] = (weights * scale).astype(jnp.bfloat16)

    key_spec = pl.BlockSpec((padded, HD), lambda g: (0, g))
    return pl.pallas_call(
        kernel,
        grid=(heads_kv,),
        out_shape=jax.ShapeDtypeStruct((heads_kv, groups * tokens, keys_all), jnp.bfloat16),
        in_specs=[
            pl.BlockSpec(memory_space=pltpu.SMEM),
            pl.BlockSpec((1, tokens, groups * HD), lambda g: (0, 0, g)),
            pl.BlockSpec((tokens, 1), lambda g: (0, 0)),
        ]
        + [key_spec] * spans,
        out_specs=pl.BlockSpec((1, groups * tokens, keys_all), lambda g: (g, 0, 0)),
        cost_estimate=pl.CostEstimate(
            flops=2 * heads_kv * groups * tokens * keys_all * HD,
            bytes_accessed=2 * heads_kv * groups * tokens * (keys_all + HD),
            transcendentals=heads_kv * groups * tokens * keys_all,
        ),
        name="attention_weights",
    )(place, queries, seg_column, *key_blocks)


def weighted_values(weights, value_parts):
    heads_kv, rows, keys_all = weights.shape
    spans = len(value_parts[0])
    tokens = keys_all // spans
    groups = rows // tokens
    part_heads = value_parts[0][0].shape[1] // HD
    parts = len(value_parts)

    def kernel(w_ref, *rest):
        value_refs, out_ref = rest[:-1], rest[-1]
        g = pl.program_id(0)
        for part in range(parts):

            @pl.when(g // part_heads == part)
            def _():
                refs = value_refs[part * spans : (part + 1) * spans]
                values = jnp.concatenate([ref[...] for ref in refs], axis=0)
                mixed = jnp.dot(w_ref[0], values, preferred_element_type=jnp.float32)
                for j in range(groups):
                    out_ref[0, :, j * HD : (j + 1) * HD] = mixed[
                        j * tokens : (j + 1) * tokens, :
                    ].astype(jnp.bfloat16)

    in_specs = [pl.BlockSpec((1, rows, keys_all), lambda g: (g, 0, 0))]
    for _ in range(parts * spans):
        in_specs.append(pl.BlockSpec((tokens, HD), lambda g: (0, g % part_heads)))
    return pl.pallas_call(
        kernel,
        grid=(heads_kv,),
        out_shape=jax.ShapeDtypeStruct((1, tokens, heads_kv * groups * HD), jnp.bfloat16),
        in_specs=in_specs,
        out_specs=pl.BlockSpec((1, tokens, groups * HD), lambda g: (0, 0, g)),
        cost_estimate=pl.CostEstimate(
            flops=2 * heads_kv * rows * keys_all * HD,
            bytes_accessed=2 * heads_kv * rows * keys_all,
            transcendentals=0,
        ),
        name="weighted_values",
    )(weights, *[block for part in value_parts for block in part])


def on_device(
    grad_parts,
    master_weight,
    moment_one,
    moment_two,
    queries,
    keys_in,
    hidden,
    segment_ids,
    packed_len,
):
    n_dp, n_replica = lax.axis_size("dp"), lax.axis_size("replica")
    dp, replica = lax.axis_index("dp"), lax.axis_index("replica")
    tokens = queries.shape[1]
    rows, columns = master_weight.shape
    half = columns // 2
    bits = bits_of(n_dp)
    orders = [bits, [bits[1], bits[0]] + bits[2:]]

    first_parts = []
    sums = []
    for part, order in enumerate(orders):
        sums.append(summed_to_owner(grad_parts[:, :, part * half : (part + 1) * half], order))
    new_master, new_first, new_second = adam_update(
        jnp.concatenate(sums, axis=1), master_weight, moment_one, moment_two
    )
    weight_parts = []
    for part, order in enumerate(orders):
        cut = slice(part * half, (part + 1) * half)
        updated = adam_update(
            sums[part], master_weight[:, cut], moment_one[:, cut], moment_two[:, cut]
        )[0].astype(jnp.bfloat16)
        weight_parts.append(gathered(updated, order[::-1]))

    labels = weight_parts[0][2]
    assert sorted(labels) == list(range(n_dp))
    owner = dp ^ jnp.arange(n_dp, dtype=jnp.int32)
    offsets = jnp.arange(n_replica, dtype=jnp.int32)
    picks = owner[None, :] * n_replica + (replica ^ offsets)[:, None]
    packed = packed_columns(hidden[0], picks, rows)
    token_rows = [packed[0]] + [swapped(packed[m], m) for m in range(1, n_replica)]
    token_rows = jnp.concatenate(token_rows, axis=0)

    seg_row = jnp.tile(segment_ids.astype(jnp.bfloat16), (16, columns // tokens))
    key_own = jnp.concatenate([keys_in[0], seg_row], axis=0)
    key_blocks = [passed_along(key_own, d) for d in (3, 2, 1)] + [key_own]
    place = jnp.stack([dp.astype(jnp.int32), packed_len[0]])
    seg_column = segment_ids.astype(jnp.float32).reshape(tokens, 1)
    weights = attention_weights(place, queries, seg_column, key_blocks)

    value_parts = []
    for held, last, labels in weight_parts:
        early = len(labels) // 2

        def columns_of(picked):
            return jnp.concatenate(
                [token_rows[:, o * rows : (o + 1) * rows] for o in picked], axis=1
            )

        partial = jnp.dot(
            columns_of(labels[:early]), held, preferred_element_type=jnp.float32
        ) + jnp.dot(columns_of(labels[early:]), last, preferred_element_type=jnp.float32)
        partial = partial.reshape(n_replica, tokens, half)
        for bit in bits_of(n_replica):
            partial = partial.reshape(-1, 2, tokens, half)
            came = swapped(partial[:, 1].astype(jnp.bfloat16), bit)
            partial = partial[:, 0] + came.astype(jnp.float32)
        value = partial[0].astype(jnp.bfloat16)
        value_parts.append([passed_along(value, d) for d in (3, 2, 1)] + [value])
    attended = weighted_values(weights, value_parts)
    return (new_master, new_first, new_second, attended)


def solution(mesh):
    in_specs = (
        P("dp", "replica", None),
        P(("dp", "replica"), None),
        P(("dp", "replica"), None),
        P(("dp", "replica"), None),
        P("replica", "dp", None),
        P("replica", "dp", None),
        P("replica", "dp", None),
        P("replica", "dp"),
        P("replica"),
    )
    out_specs = (
        P(("dp", "replica"), None),
        P(("dp", "replica"), None),
        P(("dp", "replica"), None),
        P("replica", "dp", None),
    )
    return jax.shard_map(
        on_device, mesh=mesh, in_specs=in_specs, out_specs=out_specs, check_vma=False
    )
```

time: 273 us -> 187 us (0.68)
  waiting for transfers between devices: 192 us -> 43.8 us
  Pallas kernels: 0 us -> 77 us
  starting transfers between devices: 28.2 us -> 47.9 us
  between operations: 14.6 us -> 1.83 us
  matrix products: 14.1 us -> 1.77 us
  local copies, waits for them, and re-layouts: 10.9 us -> 5.71 us
  other arithmetic: 12.9 us -> 8.51 us
    all_gather x2 -> x0, waiting for transfers between devices: 116 us -> none  [the longest x1 100 us: on_device(): lax.all_gather(group_rows, 'dp', axis=0, tiled=True)]
    pallas_call x0 -> x3, Pallas kernels: none -> 77 us  [the longest x1 65.6 us: packed_columns(): pl.pallas_call(kernel, out_shape=jax.ShapeDtypeStruct((offsets, tokens, b...]
    reduce_scatter x1 -> x0, waiting for transfers between devices: 74.4 us -> none  [on_device(): lax.psum_scatter(grad_terms.astype(jnp.bfloat16), 'dp', scatter_dimension...]
    ppermute x9 -> x28, waiting for transfers between devices: 0.91 us -> 43.8 us  [the longest x19 43.3 us: swapped(): return lax.ppermute(block, ALL, [(i, i ^ mask) for i in range(total)])]
    ppermute x9 -> x28, starting transfers between devices: 28.1 us -> 47.9 us  [the longest x9 30.3 us: passed_along(): return lax.ppermute(block, 'dp', route)]
    dot_general x3 -> x4, matrix products: 14.1 us -> 1.77 us  [the longest x2 0.9 us: on_device(): jnp.dot(columns_of(labels[:early]), held, preferred_element_type=jnp.floa...]
    concatenate x4 -> x0, local copies, waits for them, and re-layouts: 4.74 us -> none  [prefill(): jnp.concatenate(key_list, axis=0).reshape(4 * local_len, heads_kv, HD)]
    sub x1, other arithmetic: 5.85 us -> 1.4 us  [adam_update(): master_new = master - learn_rate * step_dir]
  transfers between devices with their start and end apart: 12 -> 28, of which waited for: 4 -> 10; matrix products, arithmetic and copies ran while one was open for 8% -> 7% of each run, Pallas kernels for 0% -> 39%
where the time goes in v1:
time: 187 us
  Pallas kernels  77 us (41%)
  starting transfers between devices  47.9 us (26%)
  waiting for transfers between devices  43.8 us (23%)
  other arithmetic  8.51 us (5%)
  local copies, waits for them, and re-layouts  5.71 us (3%)
    pallas_call x1, Pallas kernels, packed_columns(): pl.pallas_call(kernel, out_shape=jax.ShapeDtypeStruct((offsets, tokens, b...  65.6 us
    ppermute x19, waiting for transfers between devices, swapped(): return lax.ppermute(block, ALL, [(i, i ^ mask) for i in range(total)])  43.3 us
    ppermute x9, starting transfers between devices, passed_along(): return lax.ppermute(block, 'dp', route)  30.3 us
    ppermute x19, starting transfers between devices, swapped(): return lax.ppermute(block, ALL, [(i, i ^ mask) for i in range(total)])  17.6 us
    pallas_call x1, Pallas kernels, attention_weights(): pl.pallas_call(kernel, grid=(heads_kv,), out_shape=jax.ShapeDtypeStruct((...  6.4 us
    pallas_call x1, Pallas kernels, weighted_values(): pl.pallas_call(kernel, grid=(heads_kv,), out_shape=jax.ShapeDtypeStruct((...  5 us
  transfers between devices with their start and end apart: 28, of which 10 were waited for; matrix products, arithmetic and copies ran while one was open for 7% of the time, Pallas kernels for 39%

profile of v1, /device:TPU:0, one launch (start us, length us, event | category | flops | bytes accessed | tf_op | source)
XLA Modules:
  0.0 186.5 jit_solution(915490090031190606)
XLA Ops:
  0.6 1.3 convert_bitcast_fusion
  2.0 0.9 pad_maximum_fusion.15.rest_3_
  2.9 6.5 %collective-permute-start.6 = (bf16[144,512]{1,0:T(8,128)(2,1)S(1)}, bf16[144,512]{1,0:T(8,128)(2,1)}, u32[]{:S(2)}, u32[]{:S(2)}) collective-permute-start(bf16[144,512]{1,0:T(8,128)(2,1)S(1)} %pad_maximum_fusion.15.rest_3_), channel_id=1, source_target_pairs={{0,12},{4,16},{8,20},{12,24},{16,28},{1,13},{5,17},{9,21},{13,25},... | collective-permute-start | bytes 442376 | tf_op jit(solution)/shard_map/ppermute | solution.py:32
  9.4 4.1 %collective-permute-start.7 = (bf16[144,512]{1,0:T(8,128)(2,1)S(1)}, bf16[144,512]{1,0:T(8,128)(2,1)}, u32[]{:S(2)}, u32[]{:S(2)}) collective-permute-start(bf16[144,512]{1,0:T(8,128)(2,1)S(1)} %pad_maximum_fusion.15.rest_3_), channel_id=1, source_target_pairs={{0,8},{4,12},{8,16},{12,20},{16,24},{20,28},{1,9},{5,13},{9,17},{1... | collective-permute-start | bytes 442376 | tf_op jit(solution)/shard_map/ppermute | solution.py:32
  13.5 3.5 %collective-permute-start.8 = (bf16[144,512]{1,0:T(8,128)(2,1)S(1)}, bf16[144,512]{1,0:T(8,128)(2,1)}, u32[]{:S(2)}, u32[]{:S(2)}) collective-permute-start(bf16[144,512]{1,0:T(8,128)(2,1)S(1)} %pad_maximum_fusion.15.rest_3_), channel_id=1, source_target_pairs={{0,4},{4,8},{8,12},{12,16},{16,20},{20,24},{24,28},{1,5},{5,9},{9,... | collective-permute-start | bytes 442376 | tf_op jit(solution)/shard_map/ppermute | solution.py:32
  17.0 1.7 fusion.53
  18.7 0.1 constant_dynamic-slice_fusion.1
  18.9 0.1 collective-permute-start.3
  18.9 0.8 dynamic-slice_bitcast_fusion
  19.8 0.2 collective-permute-start
  20.0 0.7 broadcast_add_fusion.picks_ref
  20.7 65.6 %pack_hidden.1 = bf16[4,128,2048]{2,1,0:T(8,128)(2,1)} custom-call(s32[4,8]{1,0:T(4,128)} %broadcast_add_fusion.picks_ref, bf16[128,8192]{1,0:T(8,128)(2,1)} %bitcast.105), custom_call_target="tpu_custom_call" | custom-call | bytes 4194304 | tf_op jit(solution)/shard_map/pack_hidden/pallas_call | solution.py:99
  86.3 0.1 fusion.16
  86.5 1.9 collective-permute-start.4
  88.4 0.1 fusion.17
  88.5 2.1 %collective-permute-start.1 = (bf16[2,256,256]{2,1,0:T(8,128)(2,1)S(1)}, bf16[2,256,256]{2,1,0:T(8,128)(2,1)S(1)}, u32[]{:S(2)}, u32[]{:S(2)}) collective-permute-start(bf16[2,256,256]{2,1,0:T(8,128)(2,1)S(1)} %dynamic-slice_bitcast_fusion.2), channel_id=1, source_target_pairs={{0,8},{1,9},{2,10},{3,11},{4,12},{5,13},{6,14},{7,15},{8,0},{9,1},... | collective-permute-start | bytes 786440 | tf_op jit(solution)/shard_map/ppermute | solution.py:26
  90.6 3.0 %collective-permute-done.4 = bf16[2,256,256]{2,1,0:T(8,128)(2,1)S(1)} collective-permute-done((bf16[2,256,256]{2,1,0:T(8,128)(2,1)S(1)}, bf16[2,256,256]{2,1,0:T(8,128)(2,1)S(1)}, u32[]{:S(2)}, u32[]{:S(2)}) %collective-permute-start.4) | collective-permute-done | bytes 262176 | tf_op jit(solution)/shard_map/ppermute | solution.py:26
  93.5 0.1 fusion.19
  93.6 0.1 collective-permute-start.5
  93.7 3.3 %collective-permute-done.1 = bf16[2,256,256]{2,1,0:T(8,128)(2,1)S(1)} collective-permute-done((bf16[2,256,256]{2,1,0:T(8,128)(2,1)S(1)}, bf16[2,256,256]{2,1,0:T(8,128)(2,1)S(1)}, u32[]{:S(2)}, u32[]{:S(2)}) %collective-permute-start.1) | collective-permute-done | bytes 262176 | tf_op jit(solution)/shard_map/ppermute | solution.py:26
  97.0 0.1 fusion.20
  97.1 0.1 collective-permute-start.2
  97.2 1.2 slice_bitcast_fusion.3
  99.1 0.7 copy.16.seg_ref
  99.8 1.5 collective-permute-start.10
  101.3 1.9 %collective-permute-done.5 = bf16[256,256]{1,0:T(8,128)(2,1)} collective-permute-done((bf16[256,256]{1,0:T(8,128)(2,1)S(1)}, bf16[256,256]{1,0:T(8,128)(2,1)}, u32[]{:S(2)}, u32[]{:S(2)}) %collective-permute-start.5) | collective-permute-done | bytes 131104 | tf_op jit(solution)/shard_map/ppermute | solution.py:26
  103.2 3.2 %collective-permute-done.2 = bf16[256,256]{1,0:T(8,128)(2,1)} collective-permute-done((bf16[256,256]{1,0:T(8,128)(2,1)S(1)}, bf16[256,256]{1,0:T(8,128)(2,1)}, u32[]{:S(2)}, u32[]{:S(2)}) %collective-permute-start.2) | collective-permute-done | bytes 131104 | tf_op jit(solution)/shard_map/ppermute | solution.py:26
  106.4 1.5 subtract_convert_fusion.1
  107.9 0.1 collective-permute-start.20
  107.9 0.6 pad_add_fusion.place_ref
  108.6 6.4 %attention_weights.1.w_ref = bf16[4,1024,512]{2,1,0:T(8,128)(2,1)} custom-call(s32[2]{0:T(128)} %pad_add_fusion.place_ref, bf16[1,128,4096]{2,1,0:T(8,128)(2,1)} %q_ref.1, f32[128,1]{1,0:T(8,128)} %copy.16.seg_ref, bf16[144,512]{1,0:T(8,128)(2,1)} %collective-permute-done.6.rest_0_, bf16[144,512]{1,0:T(8,128)(2,1)} %collective-permute-done.7.rest_1_, ...), custom_call_target="tpu_custom_call" | custom-call | flops 536870912 | bytes 5242880 | tf_op jit(solution)/shard_map/attention_weights/pallas_call | solution.py:151
  115.0 2.9 %collective-permute-start.12 = (bf16[256,256]{1,0:T(8,128)(2,1)S(1)}, bf16[256,256]{1,0:T(8,128)(2,1)S(1)}, u32[]{:S(2)}, u32[]{:S(2)}) collective-permute-start(bf16[256,256]{1,0:T(8,128)(2,1)S(1)} %get-tuple-element.6), channel_id=1, source_target_pairs={{0,16},{1,17},{2,18},{3,19},{4,20},{5,21},{6,22},{7,23},{8,24},{9,... | collective-permute-start | bytes 393224 | tf_op jit(solution)/shard_map/ppermute | solution.py:26
  117.9 1.7 collective-permute-start.21
  119.6 1.5 collective-permute-done.11
  121.1 1.6 pad_maximum_fusion
  122.7 3.4 %collective-permute-done.21 = bf16[512,256]{1,0:T(8,128)(2,1)S(1)} collective-permute-done((bf16[512,256]{1,0:T(8,128)(2,1)S(1)}, bf16[512,256]{1,0:T(8,128)(2,1)S(1)}, u32[]{:S(2)}, u32[]{:S(2)}) %collective-permute-start.21) | collective-permute-done | bytes 262176 | tf_op jit(solution)/shard_map/ppermute | solution.py:26
  126.1 0.1 collective-permute-start.22
  126.3 2.1 %collective-permute-start.13 = (bf16[512,256]{1,0:T(8,128)(2,1)S(1)}, bf16[512,256]{1,0:T(8,128)(2,1)S(1)}, u32[]{:S(2)}, u32[]{:S(2)}) collective-permute-start(bf16[512,256]{1,0:T(8,128)(2,1)S(1)} %pad_maximum_fusion.13), channel_id=1, source_target_pairs={{0,8},{1,9},{2,10},{3,11},{4,12},{5,13},{6,14},{7,15},{8,0},{9,1},... | collective-permute-start | bytes 786440 | tf_op jit(solution)/shard_map/ppermute | solution.py:26
  128.3 0.1 fusion.52
  128.5 16.3 %collective-permute-done.13 = bf16[512,256]{1,0:T(8,128)(2,1)S(1)} collective-permute-done((bf16[512,256]{1,0:T(8,128)(2,1)S(1)}, bf16[512,256]{1,0:T(8,128)(2,1)S(1)}, u32[]{:S(2)}, u32[]{:S(2)}) %collective-permute-start.13) | collective-permute-done | bytes 262176 | tf_op jit(solution)/shard_map/ppermute | solution.py:26
  144.7 1.8 collective-permute-start.14
  146.5 0.4 fusion.1
  147.0 0.4 convolution_add_fusion
  147.4 0.1 collective-permute-start.23
  147.5 9.3 %collective-permute-done.14 = bf16[1024,256]{1,0:T(8,128)(2,1)S(1)} collective-permute-done((bf16[1024,256]{1,0:T(8,128)(2,1)S(1)}, bf16[1024,256]{1,0:T(8,128)(2,1)S(1)}, u32[]{:S(2)}, u32[]{:S(2)}) %collective-permute-start.14) | collective-permute-done | bytes 524320 | tf_op jit(solution)/shard_map/ppermute | solution.py:26
  156.8 0.4 fusion
  157.2 0.4 convolution_add_fusion.1
  157.7 0.1 collective-permute-start.15
  157.9 1.6 collective-permute-start.24
  159.5 1.3 collective-permute-start.16
  160.8 1.6 collective-permute-done.24
  162.5 3.7 %collective-permute-start.25 = (bf16[128,256]{1,0:T(8,128)(2,1)S(1)}, bf16[128,256]{1,0:T(8,128)(2,1)S(1)}, u32[]{:S(2)}, u32[]{:S(2)}) collective-permute-start(bf16[128,256]{1,0:T(8,128)(2,1)S(1)} %fusion.45.rest_7_), channel_id=1, source_target_pairs={{0,12},{4,16},{8,20},{12,24},{16,28},{1,13},{5,17},{9,21},{13,25},... | collective-permute-start | bytes 196616 | tf_op jit(solution)/shard_map/ppermute | solution.py:32
  166.2 2.8 %collective-permute-start.26 = (bf16[128,256]{1,0:T(8,128)(2,1)S(1)}, bf16[128,256]{1,0:T(8,128)(2,1)S(1)}, u32[]{:S(2)}, u32[]{:S(2)}) collective-permute-start(bf16[128,256]{1,0:T(8,128)(2,1)S(1)} %fusion.45.rest_7_), channel_id=1, source_target_pairs={{0,8},{4,12},{8,16},{12,20},{16,24},{20,28},{1,9},{5,13},{9,17},{1... | collective-permute-start | bytes 196616 | tf_op jit(solution)/shard_map/ppermute | solution.py:32
  169.0 3.7 %collective-permute-start.27 = (bf16[128,256]{1,0:T(8,128)(2,1)S(1)}, bf16[128,256]{1,0:T(8,128)(2,1)S(1)}, u32[]{:S(2)}, u32[]{:S(2)}) collective-permute-start(bf16[128,256]{1,0:T(8,128)(2,1)S(1)} %fusion.45.rest_7_), channel_id=1, source_target_pairs={{0,4},{4,8},{8,12},{12,16},{16,20},{20,24},{24,28},{1,5},{5,9},{9,... | collective-permute-start | bytes 196616 | tf_op jit(solution)/shard_map/ppermute | solution.py:32
  172.8 1.6 collective-permute-start.17
  174.4 1.6 collective-permute-start.18
  176.0 2.7 %collective-permute-start.19 = (bf16[128,256]{1,0:T(8,128)(2,1)S(1)}, bf16[128,256]{1,0:T(8,128)(2,1)S(1)}, u32[]{:S(2)}, u32[]{:S(2)}) collective-permute-start(bf16[128,256]{1,0:T(8,128)(2,1)S(1)} %fusion.43.rest_3_), channel_id=1, source_target_pairs={{0,4},{4,8},{8,12},{12,16},{16,20},{20,24},{24,28},{1,5},{5,9},{9,... | collective-permute-start | bytes 196616 | tf_op jit(solution)/shard_map/ppermute | solution.py:32
  178.8 1.4 multiply_subtract_fusion
  180.3 0.4 collective-permute-done.19.rest_2_
  180.7 0.1 copy-done.8
  180.8 0.0 copy-done.9
  180.8 0.0 copy-done.10
  180.9 0.6 copy-done.12
  181.5 5.0 %weighted_values.1 = bf16[1,128,4096]{2,1,0:T(8,128)(2,1)} custom-call(bf16[4,1024,512]{2,1,0:T(8,128)(2,1)} %attention_weights.1.w_ref, bf16[128,256]{1,0:T(8,128)(2,1)} %copy-done.10, bf16[128,256]{1,0:T(8,128)(2,1)} %copy-done.11, bf16[128,256]{1,0:T(8,128)(2,1)} %copy-done.12, bf16[128,256]{1,0:T(8,128)(2,1)} %copy-done.6, bf16[128,256]{1,0:T(8,128)(2,1)} %copy-done.7, ...), custom_call_target="tpu_custom_call" | custom-call | flops 536870912 | bytes 4194304 | tf_op jit(solution)/shard_map/weighted_values/pallas_call | solution.py:197
  (65 shorter events, 0.5 us)
Async XLA Ops:
  2.9 15.8 %copy-start.4 = (bf16[144,512]{1,0:T(8,128)(2,1)}, bf16[144,512]{1,0:T(8,128)(2,1)S(1)}, u32[]{:S(2)}) copy-start(bf16[144,512]{1,0:T(8,128)(2,1)S(1)} %pad_maximum_fusion.15.rest_3_) | copy-start | bytes 442372
  2.9 96.9 %collective-permute-start.6 = (bf16[144,512]{1,0:T(8,128)(2,1)S(1)}, bf16[144,512]{1,0:T(8,128)(2,1)}, u32[]{:S(2)}, u32[]{:S(2)}) collective-permute-start(bf16[144,512]{1,0:T(8,128)(2,1)S(1)} %pad_maximum_fusion.15.rest_3_), channel_id=1, source_target_pairs={{0,12},{4,16},{8,20},{12,24},{16,28},{1,13},{5,17},{9,21},{13,25},... | collective-permute-start | bytes 442376 | tf_op jit(solution)/shard_map/ppermute | solution.py:32
  9.4 98.4 %collective-permute-start.7 = (bf16[144,512]{1,0:T(8,128)(2,1)S(1)}, bf16[144,512]{1,0:T(8,128)(2,1)}, u32[]{:S(2)}, u32[]{:S(2)}) collective-permute-start(bf16[144,512]{1,0:T(8,128)(2,1)S(1)} %pad_maximum_fusion.15.rest_3_), channel_id=1, source_target_pairs={{0,8},{4,12},{8,16},{12,20},{16,24},{20,28},{1,9},{5,13},{9,17},{1... | collective-permute-start | bytes 442376 | tf_op jit(solution)/shard_map/ppermute | solution.py:32
  13.5 95.0 %collective-permute-start.8 = (bf16[144,512]{1,0:T(8,128)(2,1)S(1)}, bf16[144,512]{1,0:T(8,128)(2,1)}, u32[]{:S(2)}, u32[]{:S(2)}) collective-permute-start(bf16[144,512]{1,0:T(8,128)(2,1)S(1)} %pad_maximum_fusion.15.rest_3_), channel_id=1, source_target_pairs={{0,4},{4,8},{8,12},{12,16},{16,20},{20,24},{24,28},{1,5},{5,9},{9,... | collective-permute-start | bytes 442376 | tf_op jit(solution)/shard_map/ppermute | solution.py:32
  18.9 67.5 %collective-permute-start.3 = (bf16[2,2,256,256]{3,2,0,1:T(8,128)(2,1)S(1)}, bf16[2,2,256,256]{3,2,0,1:T(8,128)(2,1)S(1)}, u32[]{:S(2)}, u32[]{:S(2)}) collective-permute-start(bf16[2,2,256,256]{3,2,0,1:T(8,128)(2,1)S(1)} %bitcast.106), channel_id=1, source_target_pairs={{0,8},{1,9},{2,10},{3,11},{4,12},{5,13},{6,14},{7,15},{8,0},{9,1},... | collective-permute-start | bytes 1572872 | tf_op jit(solution)/shard_map/ppermute | solution.py:26
  19.8 68.6 %collective-permute-start = (bf16[2,2,256,256]{3,2,1,0:T(8,128)(2,1)}, bf16[2,2,256,256]{3,2,1,0:T(8,128)(2,1)S(1)}, u32[]{:S(2)}, u32[]{:S(2)}) collective-permute-start(bf16[2,2,256,256]{3,2,1,0:T(8,128)(2,1)} %dynamic-slice_bitcast_fusion), channel_id=1, source_target_pairs={{0,4},{1,5},{2,6},{3,7},{4,0},{5,1},{6,2},{7,3},{8,12},{9,13},{10,... | collective-permute-start | bytes 1572872 | tf_op jit(solution)/shard_map/ppermute | solution.py:26
  86.5 10.7 %copy-start = (bf16[4,128,2048]{2,1,0:T(8,128)(2,1)S(1)}, bf16[4,128,2048]{2,1,0:T(8,128)(2,1)}, u32[]{:S(2)}) copy-start(bf16[4,128,2048]{2,1,0:T(8,128)(2,1)} %pack_hidden.1) | copy-start | bytes 6291460
  86.5 7.0 %collective-permute-start.4 = (bf16[2,256,256]{2,1,0:T(8,128)(2,1)S(1)}, bf16[2,256,256]{2,1,0:T(8,128)(2,1)S(1)}, u32[]{:S(2)}, u32[]{:S(2)}) collective-permute-start(bf16[2,256,256]{2,1,0:T(8,128)(2,1)S(1)} %dynamic-slice_bitcast_fusion.1), channel_id=1, source_target_pairs={{0,4},{1,5},{2,6},{3,7},{4,0},{5,1},{6,2},{7,3},{8,12},{9,13},{10,... | collective-permute-start | bytes 786440 | tf_op jit(solution)/shard_map/ppermute | solution.py:26
  88.5 8.5 %collective-permute-start.1 = (bf16[2,256,256]{2,1,0:T(8,128)(2,1)S(1)}, bf16[2,256,256]{2,1,0:T(8,128)(2,1)S(1)}, u32[]{:S(2)}, u32[]{:S(2)}) collective-permute-start(bf16[2,256,256]{2,1,0:T(8,128)(2,1)S(1)} %dynamic-slice_bitcast_fusion.2), channel_id=1, source_target_pairs={{0,8},{1,9},{2,10},{3,11},{4,12},{5,13},{6,14},{7,15},{8,0},{9,1},... | collective-permute-start | bytes 786440 | tf_op jit(solution)/shard_map/ppermute | solution.py:26
  93.6 9.6 %collective-permute-start.5 = (bf16[256,256]{1,0:T(8,128)(2,1)S(1)}, bf16[256,256]{1,0:T(8,128)(2,1)}, u32[]{:S(2)}, u32[]{:S(2)}) collective-permute-start(bf16[256,256]{1,0:T(8,128)(2,1)S(1)} %dynamic-slice_bitcast_fusion.3), channel_id=1, source_target_pairs={{0,16},{1,17},{2,18},{3,19},{4,20},{5,21},{6,22},{7,23},{8,24},{9,... | collective-permute-start | bytes 393224 | tf_op jit(solution)/shard_map/ppermute | solution.py:26
  97.1 2.0 %copy-start.13 = (f32[128,1]{0,1:T(1,128)S(1)}, f32[128,1]{0,1:T(1,128)}, u32[]{:S(2)}) copy-start(f32[128,1]{0,1:T(1,128)} %get-tuple-element.30) | copy-start | bytes 1540
  97.1 9.3 %copy-start.1 = (f32[256,512]{1,0:T(8,128)S(1)}, f32[256,512]{1,0:T(8,128)}, u32[]{:S(2)}) copy-start(f32[256,512]{1,0:T(8,128)} %param.10) | copy-start | bytes 1572868
  97.1 9.3 %copy-start.2 = (f32[256,512]{1,0:T(8,128)S(1)}, f32[256,512]{1,0:T(8,128)}, u32[]{:S(2)}) copy-start(f32[256,512]{1,0:T(8,128)} %param.12) | copy-start | bytes 1572868
  97.1 9.3 %copy-start.3 = (f32[256,512]{1,0:T(8,128)S(1)}, f32[256,512]{1,0:T(8,128)}, u32[]{:S(2)}) copy-start(f32[256,512]{1,0:T(8,128)} %param.11) | copy-start | bytes 1572868
  97.1 9.2 %collective-permute-start.2 = (bf16[256,256]{1,0:T(8,128)(2,1)S(1)}, bf16[256,256]{1,0:T(8,128)(2,1)}, u32[]{:S(2)}, u32[]{:S(2)}) collective-permute-start(bf16[256,256]{1,0:T(8,128)(2,1)S(1)} %dynamic-slice_bitcast_fusion.4), channel_id=1, source_target_pairs={{0,16},{1,17},{2,18},{3,19},{4,20},{5,21},{6,22},{7,23},{8,24},{9,... | collective-permute-start | bytes 393224 | tf_op jit(solution)/shard_map/ppermute | solution.py:26
  99.8 19.9 %collective-permute-start.10 = (bf16[128,2048]{1,0:T(8,128)(2,1)}, bf16[128,2048]{1,0:T(8,128)(2,1)}, u32[]{:S(2)}, u32[]{:S(2)}) collective-permute-start(bf16[128,2048]{1,0:T(8,128)(2,1)} %get-tuple-element.21), channel_id=1, source_target_pairs={{0,2},{1,3},{2,0},{3,1},{4,6},{5,7},{6,4},{7,5},{8,10},{9,11},{10,... | collective-permute-start | bytes 1572872 | tf_op jit(solution)/shard_map/ppermute | solution.py:26
  103.2 17.9 %collective-permute-start.11 = (bf16[128,2048]{1,0:T(8,128)(2,1)}, bf16[128,2048]{1,0:T(8,128)(2,1)}, u32[]{:S(2)}, u32[]{:S(2)}) collective-permute-start(bf16[128,2048]{1,0:T(8,128)(2,1)} %get-tuple-element.20), channel_id=1, source_target_pairs={{0,3},{1,2},{2,1},{3,0},{4,7},{5,6},{6,5},{7,4},{8,11},{9,10},{10,... | collective-permute-start | bytes 1572872 | tf_op jit(solution)/shard_map/ppermute | solution.py:26
  106.4 14.7 %collective-permute-start.9 = (bf16[128,2048]{1,0:T(8,128)(2,1)}, bf16[128,2048]{1,0:T(8,128)(2,1)}, u32[]{:S(2)}, u32[]{:S(2)}) collective-permute-start(bf16[128,2048]{1,0:T(8,128)(2,1)} %get-tuple-element.22), channel_id=1, source_target_pairs={{0,1},{1,0},{2,3},{3,2},{4,5},{5,4},{6,7},{7,6},{8,9},{9,8},{10,11... | collective-permute-start | bytes 1572872 | tf_op jit(solution)/shard_map/ppermute | solution.py:26
  107.9 10.0 %collective-permute-start.20 = (bf16[256,256]{1,0:T(8,128)(2,1)S(1)}, bf16[256,256]{1,0:T(8,128)(2,1)S(1)}, u32[]{:S(2)}, u32[]{:S(2)}) collective-permute-start(bf16[256,256]{1,0:T(8,128)(2,1)S(1)} %get-tuple-element.25), channel_id=1, source_target_pairs={{0,16},{1,17},{2,18},{3,19},{4,20},{5,21},{6,22},{7,23},{8,24},{9,... | collective-permute-start | bytes 393224 | tf_op jit(solution)/shard_map/ppermute | solution.py:26
  115.0 11.3 %collective-permute-start.12 = (bf16[256,256]{1,0:T(8,128)(2,1)S(1)}, bf16[256,256]{1,0:T(8,128)(2,1)S(1)}, u32[]{:S(2)}, u32[]{:S(2)}) collective-permute-start(bf16[256,256]{1,0:T(8,128)(2,1)S(1)} %get-tuple-element.6), channel_id=1, source_target_pairs={{0,16},{1,17},{2,18},{3,19},{4,20},{5,21},{6,22},{7,23},{8,24},{9,... | collective-permute-start | bytes 393224 | tf_op jit(solution)/shard_map/ppermute | solution.py:26
  117.9 8.2 %collective-permute-start.21 = (bf16[512,256]{1,0:T(8,128)(2,1)S(1)}, bf16[512,256]{1,0:T(8,128)(2,1)S(1)}, u32[]{:S(2)}, u32[]{:S(2)}) collective-permute-start(bf16[512,256]{1,0:T(8,128)(2,1)S(1)} %pad_maximum_fusion.14), channel_id=1, source_target_pairs={{0,4},{1,5},{2,6},{3,7},{4,0},{5,1},{6,2},{7,3},{8,12},{9,13},{10,... | collective-permute-start | bytes 786440 | tf_op jit(solution)/shard_map/ppermute | solution.py:26
  126.1 20.4 %collective-permute-start.22 = (bf16[1024,256]{1,0:T(8,128)(2,1)S(1)}, bf16[1024,256]{1,0:T(8,128)(2,1)S(1)}, u32[]{:S(2)}, u32[]{:S(2)}) collective-permute-start(bf16[1024,256]{1,0:T(8,128)(2,1)S(1)} %pad_maximum_fusion.12), channel_id=1, source_target_pairs={{0,8},{1,9},{2,10},{3,11},{4,12},{5,13},{6,14},{7,15},{8,0},{9,1},... | collective-permute-start | bytes 1572872 | tf_op jit(solution)/shard_map/ppermute | solution.py:26
  126.3 18.5 %collective-permute-start.13 = (bf16[512,256]{1,0:T(8,128)(2,1)S(1)}, bf16[512,256]{1,0:T(8,128)(2,1)S(1)}, u32[]{:S(2)}, u32[]{:S(2)}) collective-permute-start(bf16[512,256]{1,0:T(8,128)(2,1)S(1)} %pad_maximum_fusion.13), channel_id=1, source_target_pairs={{0,8},{1,9},{2,10},{3,11},{4,12},{5,13},{6,14},{7,15},{8,0},{9,1},... | collective-permute-start | bytes 786440 | tf_op jit(solution)/shard_map/ppermute | solution.py:26
  144.7 12.0 %collective-permute-start.14 = (bf16[1024,256]{1,0:T(8,128)(2,1)S(1)}, bf16[1024,256]{1,0:T(8,128)(2,1)S(1)}, u32[]{:S(2)}, u32[]{:S(2)}) collective-permute-start(bf16[1024,256]{1,0:T(8,128)(2,1)S(1)} %pad_maximum_fusion.11), channel_id=1, source_target_pairs={{0,4},{1,5},{2,6},{3,7},{4,0},{5,1},{6,2},{7,3},{8,12},{9,13},{10,... | collective-permute-start | bytes 1572872 | tf_op jit(solution)/shard_map/ppermute | solution.py:26
  147.4 10.3 %collective-permute-start.23 = (bf16[2,128,256]{2,1,0:T(8,128)(2,1)S(1)}, bf16[2,128,256]{2,1,0:T(8,128)(2,1)S(1)}, u32[]{:S(2)}, u32[]{:S(2)}) collective-permute-start(bf16[2,128,256]{2,1,0:T(8,128)(2,1)S(1)} %fusion.38), channel_id=1, source_target_pairs={{0,1},{1,0},{2,3},{3,2},{4,5},{5,4},{6,7},{7,6},{8,9},{9,8},{10,11... | collective-permute-start | bytes 393224 | tf_op jit(solution)/shard_map/ppermute | solution.py:26
  157.7 1.8 collective-permute-start.15
  157.9 4.6 %collective-permute-start.24 = (bf16[1,128,256]{2,1,0:T(8,128)(2,1)S(1)}, bf16[1,128,256]{2,1,0:T(8,128)(2,1)S(1)}, u32[]{:S(2)}, u32[]{:S(2)}) collective-permute-start(bf16[1,128,256]{2,1,0:T(8,128)(2,1)S(1)} %fusion.46), channel_id=1, source_target_pairs={{0,2},{1,3},{2,0},{3,1},{4,6},{5,7},{6,4},{7,5},{8,10},{9,11},{10,... | collective-permute-start | bytes 196616 | tf_op jit(solution)/shard_map/ppermute | solution.py:26
  159.5 13.2 %collective-permute-start.16 = (bf16[1,128,256]{2,1,0:T(8,128)(2,1)S(1)}, bf16[1,128,256]{2,1,0:T(8,128)(2,1)S(1)}, u32[]{:S(2)}, u32[]{:S(2)}) collective-permute-start(bf16[1,128,256]{2,1,0:T(8,128)(2,1)S(1)} %fusion.44), channel_id=1, source_target_pairs={{0,2},{1,3},{2,0},{3,1},{4,6},{5,7},{6,4},{7,5},{8,10},{9,11},{10,... | collective-permute-start | bytes 196616 | tf_op jit(solution)/shard_map/ppermute | solution.py:26
  162.5 18.2 %copy-start.5 = (bf16[128,256]{1,0:T(8,128)(2,1)}, bf16[128,256]{1,0:T(8,128)(2,1)S(1)}, u32[]{:S(2)}) copy-start(bf16[128,256]{1,0:T(8,128)(2,1)S(1)} %fusion.45.rest_7_) | copy-start | bytes 196612
  162.5 13.6 %collective-permute-start.25 = (bf16[128,256]{1,0:T(8,128)(2,1)S(1)}, bf16[128,256]{1,0:T(8,128)(2,1)S(1)}, u32[]{:S(2)}, u32[]{:S(2)}) collective-permute-start(bf16[128,256]{1,0:T(8,128)(2,1)S(1)} %fusion.45.rest_7_), channel_id=1, source_target_pairs={{0,12},{4,16},{8,20},{12,24},{16,28},{1,13},{5,17},{9,21},{13,25},... | collective-permute-start | bytes 196616 | tf_op jit(solution)/shard_map/ppermute | solution.py:32
  166.2 14.0 %collective-permute-start.26 = (bf16[128,256]{1,0:T(8,128)(2,1)S(1)}, bf16[128,256]{1,0:T(8,128)(2,1)S(1)}, u32[]{:S(2)}, u32[]{:S(2)}) collective-permute-start(bf16[128,256]{1,0:T(8,128)(2,1)S(1)} %fusion.45.rest_7_), channel_id=1, source_target_pairs={{0,8},{4,12},{8,16},{12,20},{16,24},{20,28},{1,9},{5,13},{9,17},{1... | collective-permute-start | bytes 196616 | tf_op jit(solution)/shard_map/ppermute | solution.py:32
  169.0 11.2 %collective-permute-start.27 = (bf16[128,256]{1,0:T(8,128)(2,1)S(1)}, bf16[128,256]{1,0:T(8,128)(2,1)S(1)}, u32[]{:S(2)}, u32[]{:S(2)}) collective-permute-start(bf16[128,256]{1,0:T(8,128)(2,1)S(1)} %fusion.45.rest_7_), channel_id=1, source_target_pairs={{0,4},{4,8},{8,12},{12,16},{16,20},{20,24},{24,28},{1,5},{5,9},{9,... | collective-permute-start | bytes 196616 | tf_op jit(solution)/shard_map/ppermute | solution.py:32
  172.8 7.9 %copy-start.6 = (bf16[128,256]{1,0:T(8,128)(2,1)}, bf16[128,256]{1,0:T(8,128)(2,1)S(1)}, u32[]{:S(2)}) copy-start(bf16[128,256]{1,0:T(8,128)(2,1)S(1)} %fusion.43.rest_3_) | copy-start | bytes 196612
  172.8 7.4 %collective-permute-start.17 = (bf16[128,256]{1,0:T(8,128)(2,1)S(1)}, bf16[128,256]{1,0:T(8,128)(2,1)S(1)}, u32[]{:S(2)}, u32[]{:S(2)}) collective-permute-start(bf16[128,256]{1,0:T(8,128)(2,1)S(1)} %fusion.43.rest_3_), channel_id=1, source_target_pairs={{0,12},{4,16},{8,20},{12,24},{16,28},{1,13},{5,17},{9,21},{13,25},... | collective-permute-start | bytes 196616 | tf_op jit(solution)/shard_map/ppermute | solution.py:32
  174.4 5.9 %collective-permute-start.18 = (bf16[128,256]{1,0:T(8,128)(2,1)S(1)}, bf16[128,256]{1,0:T(8,128)(2,1)S(1)}, u32[]{:S(2)}, u32[]{:S(2)}) collective-permute-start(bf16[128,256]{1,0:T(8,128)(2,1)S(1)} %fusion.43.rest_3_), channel_id=1, source_target_pairs={{0,8},{4,12},{8,16},{12,20},{16,24},{20,28},{1,9},{5,13},{9,17},{1... | collective-permute-start | bytes 196616 | tf_op jit(solution)/shard_map/ppermute | solution.py:32
  176.0 4.7 %copy-start.7 = (bf16[128,256]{1,0:T(8,128)(2,1)}, bf16[128,256]{1,0:T(8,128)(2,1)S(1)}, u32[]{:S(2)}) copy-start(bf16[128,256]{1,0:T(8,128)(2,1)S(1)} %collective-permute-done.25.rest_4_) | copy-start | bytes 196612
  176.0 4.6 %collective-permute-start.19 = (bf16[128,256]{1,0:T(8,128)(2,1)S(1)}, bf16[128,256]{1,0:T(8,128)(2,1)S(1)}, u32[]{:S(2)}, u32[]{:S(2)}) collective-permute-start(bf16[128,256]{1,0:T(8,128)(2,1)S(1)} %fusion.43.rest_3_), channel_id=1, source_target_pairs={{0,4},{4,8},{8,12},{12,16},{16,20},{20,24},{24,28},{1,5},{5,9},{9,... | collective-permute-start | bytes 196616 | tf_op jit(solution)/shard_map/ppermute | solution.py:32
  180.2 0.6 copy-start.8
  180.2 0.6 copy-start.9
  180.2 0.7 copy-start.10
  180.2 0.7 copy-start.11
  180.9 0.6 copy-start.12

commit v2 on v1

v2 whole, which is shorter than its diff:
```python
import jax
import jax.numpy as jnp
from jax import lax
from jax.experimental import pallas as pl
from jax.experimental.pallas import tpu as pltpu
from jax.sharding import PartitionSpec as P

HD = 128
ALL = ("dp", "replica")
STREAMS = 2

beta_one = 0.9
beta_two = 0.95
bias_one = 1.0 - 0.9**10
bias_two = 1.0 - 0.95**10
adam_eps = 1e-08
learn_rate = 0.002
weight_decay = 0.1


def bits_of(count):
    return [1 << j for j in range(count.bit_length() - 1)]


def swapped(block, mask):
    total = lax.axis_size("dp") * lax.axis_size("replica")
    return lax.ppermute(block, ALL, [(i, i ^ mask) for i in range(total)])


def passed_along(block, distance):
    n_dp = lax.axis_size("dp")
    return lax.ppermute(block, "dp", [(i, (i + distance) % n_dp) for i in range(n_dp)])


def adam_update(grad_sum, master, moment_first, moment_second):
    first_new = beta_one * moment_first + (1.0 - beta_one) * grad_sum
    second_new = beta_two * moment_second + (1.0 - beta_two) * grad_sum * grad_sum
    step_dir = (
        first_new / bias_one / (jnp.sqrt(second_new / bias_two) + adam_eps) + weight_decay * master
    )
    master_new = master - learn_rate * step_dir
    return (master_new, first_new, second_new)


def tied(*values):
    return lax.optimization_barrier(values)


def packed_columns(hidden_rows, picks, width):
    tokens = hidden_rows.shape[0]
    offsets, blocks = picks.shape
    if width % HD:
        cut = hidden_rows.reshape(tokens, -1, width)
        taken = jnp.take(cut, picks.reshape(-1), axis=1).reshape(tokens, offsets, blocks * width)
        return [taken[:, m] for m in range(offsets)]

    def kernel(picks_ref, source_ref, *out_refs):
        for m in range(offsets):
            for o in range(blocks):
                start = pl.multiple_of(picks_ref[m, o] * width, width)
                out_refs[m][:, o * width : (o + 1) * width] = source_ref[:, pl.ds(start, width)]

    return pl.pallas_call(
        kernel,
        out_shape=[
            jax.ShapeDtypeStruct((tokens, blocks * width), hidden_rows.dtype)
            for _ in range(offsets)
        ],
        in_specs=[
            pl.BlockSpec(memory_space=pltpu.SMEM),
            pl.BlockSpec(memory_space=pltpu.VMEM),
        ],
        out_specs=[pl.BlockSpec(memory_space=pltpu.VMEM)] * offsets,
        compiler_params=pltpu.CompilerParams(vmem_limit_bytes=16 * 2**20),
        cost_estimate=pl.CostEstimate(
            flops=0, bytes_accessed=4 * hidden_rows.size, transcendentals=0
        ),
        name="pack_hidden",
    )(picks, hidden_rows)


def projected(token_blocks, pieces, width, before):
    count = len(token_blocks)
    tokens = token_blocks[0].shape[0]
    columns = pieces[0][0].shape[1]
    depth = sum(piece.shape[0] for piece, _ in pieces)

    def total_of(token_ref, weight_refs):
        total = None
        for weight_ref, (_, places) in zip(weight_refs, pieces):
            for i, place in enumerate(places):
                term = jnp.dot(
                    token_ref[:, place * width : (place + 1) * width],
                    weight_ref[i * width : (i + 1) * width, :],
                    preferred_element_type=jnp.float32,
                )
                total = term if total is None else total + term
        return total

    def first_kernel(*refs):
        for m in range(count):
            refs[-1][m] = total_of(refs[m], refs[count:-1])

    def last_kernel(*refs):
        kept_ref, away_ref = refs[-2], refs[-1]
        for m in range(count):
            total = refs[count][m] + total_of(refs[m], refs[count + 1 : -2])
            if m % 2:
                away_ref[m // 2] = total.astype(jnp.bfloat16)
            else:
                kept_ref[m // 2] = total

    cost = pl.CostEstimate(
        flops=2 * count * tokens * depth * columns,
        bytes_accessed=2 * count * tokens * depth,
        transcendentals=0,
    )
    params = pltpu.CompilerParams(vmem_limit_bytes=24 * 2**20)
    weights = [piece for piece, _ in pieces]
    if before is None:
        return pl.pallas_call(
            first_kernel,
            out_shape=jax.ShapeDtypeStruct((count, tokens, columns), jnp.float32),
            compiler_params=params,
            cost_estimate=cost,
            name="projected_first",
        )(*token_blocks, *weights)
    return pl.pallas_call(
        last_kernel,
        out_shape=(
            jax.ShapeDtypeStruct((count // 2, tokens, columns), jnp.float32),
            jax.ShapeDtypeStruct((count // 2, tokens, columns), jnp.bfloat16),
        ),
        compiler_params=params,
        cost_estimate=cost,
        name="projected_last",
    )(*token_blocks, before, *weights)


def attention_weights(place, queries, seg_column, key_blocks):
    tokens = queries.shape[1]
    heads_kv = key_blocks[0].shape[1] // HD
    groups = queries.shape[2] // (heads_kv * HD)
    spans = len(key_blocks)
    padded = key_blocks[0].shape[0]
    keys_all = spans * tokens

    def kernel(place_ref, q_ref, seg_ref, *rest):
        key_refs, out_ref = rest[:-1], rest[-1]
        here, used = place_ref[0], place_ref[1]
        keys = jnp.concatenate([ref[0:tokens, :] for ref in key_refs], axis=0)
        seg_keys = jnp.concatenate(
            [ref[tokens : tokens + 16, :].astype(jnp.float32)[0:1, :] for ref in key_refs], axis=1
        )
        row = lax.broadcasted_iota(jnp.int32, (tokens, keys_all), 0)
        column = lax.broadcasted_iota(jnp.int32, (tokens, keys_all), 1)
        offset = column - (spans - 1) * tokens
        allowed = (
            (seg_ref[...] == seg_keys) & (offset <= row) & (offset + here * tokens >= 0)
        )
        live = (here * tokens + lax.broadcasted_iota(jnp.int32, (tokens, 1), 0)) < used
        for j in range(groups):
            scores = lax.dot_general(
                q_ref[0, :, j * HD : (j + 1) * HD],
                keys,
                (((1,), (1,)), ((), ())),
                preferred_element_type=jnp.float32,
            ) * HD ** (-0.5)
            scores = jnp.where(allowed, scores, -1e30)
            weights = jnp.exp(scores - jnp.max(scores, axis=-1, keepdims=True))
            totals = jnp.sum(weights, axis=-1, keepdims=True)
            scale = jnp.where(live, 1.0 / totals, 0.0)
            out_ref[0, j * tokens : (j + 1) * tokens, :] = (weights * scale).astype(jnp.bfloat16)

    key_spec = pl.BlockSpec((padded, HD), lambda g: (0, g))
    return pl.pallas_call(
        kernel,
        grid=(heads_kv,),
        out_shape=jax.ShapeDtypeStruct((heads_kv, groups * tokens, keys_all), jnp.bfloat16),
        in_specs=[
            pl.BlockSpec(memory_space=pltpu.SMEM),
            pl.BlockSpec((1, tokens, groups * HD), lambda g: (0, 0, g)),
            pl.BlockSpec((tokens, 1), lambda g: (0, 0)),
        ]
        + [key_spec] * spans,
        out_specs=pl.BlockSpec((1, groups * tokens, keys_all), lambda g: (g, 0, 0)),
        cost_estimate=pl.CostEstimate(
            flops=2 * heads_kv * groups * tokens * keys_all * HD,
            bytes_accessed=2 * heads_kv * groups * tokens * (keys_all + HD),
            transcendentals=heads_kv * groups * tokens * keys_all,
        ),
        name="attention_weights",
    )(place, queries, seg_column, *key_blocks)


def weighted_values(weights, value_blocks):
    heads_kv, rows, keys_all = weights.shape
    tokens, columns = value_blocks[0].shape
    groups = rows // tokens

    def kernel(w_ref, *rest):
        value_refs, out_ref = rest[:-1], rest[-1]
        values = jnp.concatenate([ref[...] for ref in value_refs], axis=0)
        mixed = jnp.dot(w_ref[0], values, preferred_element_type=jnp.float32)
        for j in range(groups):
            out_ref[0, :, j * HD : (j + 1) * HD] = mixed[j * tokens : (j + 1) * tokens, :].astype(
                jnp.bfloat16
            )

    return pl.pallas_call(
        kernel,
        grid=(heads_kv,),
        out_shape=jax.ShapeDtypeStruct((1, tokens, heads_kv * groups * HD), jnp.bfloat16),
        in_specs=[pl.BlockSpec((1, rows, keys_all), lambda g: (g, 0, 0))]
        + [pl.BlockSpec((tokens, HD), lambda g: (0, g))] * len(value_blocks),
        out_specs=pl.BlockSpec((1, tokens, groups * HD), lambda g: (0, 0, g)),
        compiler_params=pltpu.CompilerParams(vmem_limit_bytes=16 * 2**20),
        cost_estimate=pl.CostEstimate(
            flops=2 * heads_kv * rows * keys_all * HD,
            bytes_accessed=2 * heads_kv * rows * keys_all,
            transcendentals=0,
        ),
        name="weighted_values",
    )(weights, *value_blocks)


def on_device(
    grad_parts,
    master_weight,
    moment_one,
    moment_two,
    queries,
    keys_in,
    hidden,
    segment_ids,
    packed_len,
):
    n_dp, n_replica = lax.axis_size("dp"), lax.axis_size("replica")
    dp, replica = lax.axis_index("dp"), lax.axis_index("replica")
    tokens = queries.shape[1]
    rows, columns = master_weight.shape
    bits = bits_of(n_dp)
    orders = [bits, [bits[1], bits[0]] + bits[2:]] * (STREAMS // 2)
    width = columns // STREAMS
    cuts = [slice(part * width, (part + 1) * width) for part in range(STREAMS)]
    steps = len(bits)

    owner = dp ^ jnp.arange(n_dp, dtype=jnp.int32)
    offsets = jnp.arange(n_replica, dtype=jnp.int32)
    picks = owner[None, :] * n_replica + (replica ^ offsets)[:, None]

    seg_row = jnp.tile(segment_ids.astype(jnp.bfloat16), (16, columns // tokens))
    key_own = jnp.concatenate([keys_in[0], seg_row], axis=0)
    place = jnp.stack([dp.astype(jnp.int32), packed_len[0]])
    seg_column = segment_ids.astype(jnp.float32).reshape(tokens, 1)

    names = bits[::-1]
    held = [
        grad_parts[:, :, cut].reshape((2,) * len(names) + (rows, width)) for cut in cuts
    ]
    axes = [list(names) for _ in cuts]
    for step in range(steps):
        came = []
        for part, order in enumerate(orders):
            bit = order[step]
            axis = axes[part].index(bit)
            axes[part].pop(axis)
            mine = (dp // bit) % 2
            leaving = lax.dynamic_index_in_dim(held[part], 1 - mine, axis, keepdims=False)
            held[part] = lax.dynamic_index_in_dim(held[part], mine, axis, keepdims=False)
            came.append(swapped(leaving, bit * n_replica))
        if step == 0:
            packed = packed_columns(hidden[0], picks, rows)
            came[0], *packed = tied(came[0], *packed)
            token_blocks = [packed[0]] + [swapped(packed[m], m) for m in range(1, n_replica)]
        if step == 1:
            came[0], token_blocks[2] = tied(came[0], token_blocks[2])
            key_blocks = [passed_along(key_own, d) for d in (3, 2, 1)] + [key_own]
        for part in range(STREAMS):
            held[part] = held[part].astype(jnp.float32) + came[part].astype(jnp.float32)
            if step < steps - 1:
                held[part] = held[part].astype(jnp.bfloat16)

    fresh = []
    labels = [[0] for _ in cuts]
    for part, cut in enumerate(cuts):
        updated = adam_update(
            held[part], master_weight[:, cut], moment_one[:, cut], moment_two[:, cut]
        )
        fresh.append(updated[0].astype(jnp.bfloat16))
    new_master, new_first, new_second = adam_update(
        jnp.concatenate(held, axis=1), master_weight, moment_one, moment_two
    )
    for step in range(steps):
        came = [
            swapped(rows_here, order[-1 - step] * n_replica)
            for rows_here, order in zip(fresh, orders)
        ]
        if step == 0:
            came[0], *token_blocks = tied(came[0], *token_blocks)
        if step == 1:
            came[1], *key_blocks = tied(came[1], *key_blocks)
            weights = attention_weights(place, queries, seg_column, key_blocks)
        if step == steps - 1:
            came[0], weights = tied(came[0], weights)
            break
        for part, order in enumerate(orders):
            fresh[part] = jnp.concatenate([fresh[part], came[part]], axis=0)
            labels[part] = labels[part] + [label ^ order[-1 - step] for label in labels[part]]

    sent = []
    for part, order in enumerate(orders):
        before = projected(token_blocks, [(fresh[part], labels[part])], rows, None)
        last = [label ^ order[0] for label in labels[part]]
        kept, leaving = projected(token_blocks, [(came[part], last)], rows, before)
        sent.append(kept + swapped(leaving, 1).astype(jnp.float32))
    partial = jnp.concatenate(sent, axis=2)
    for bit in bits_of(n_replica)[1:]:
        partial = partial.reshape(-1, 2, tokens, columns)
        came = swapped(partial[:, 1].astype(jnp.bfloat16), bit)
        partial = partial[:, 0] + came.astype(jnp.float32)
    value = partial[0].astype(jnp.bfloat16)
    value_blocks = [passed_along(value, d) for d in (3, 2, 1)] + [value]
    attended = weighted_values(weights, value_blocks)
    return (new_master, new_first, new_second, attended)


def solution(mesh):
    in_specs = (
        P("dp", "replica", None),
        P(("dp", "replica"), None),
        P(("dp", "replica"), None),
        P(("dp", "replica"), None),
        P("replica", "dp", None),
        P("replica", "dp", None),
        P("replica", "dp", None),
        P("replica", "dp"),
        P("replica"),
    )
    out_specs = (
        P(("dp", "replica"), None),
        P(("dp", "replica"), None),
        P(("dp", "replica"), None),
        P("replica", "dp", None),
    )
    return jax.shard_map(
        on_device, mesh=mesh, in_specs=in_specs, out_specs=out_specs, check_vma=False
    )
```

time: 187 us -> 118 us (0.63)
  Pallas kernels: 77 us -> 14.8 us
  starting transfers between devices: 47.9 us -> 26.6 us
  waiting for transfers between devices: 43.8 us -> 53.9 us
  local copies, waits for them, and re-layouts: 5.71 us -> 12 us
    pallas_call x1 -> x5, Pallas kernels: 65.6 us -> 5.54 us  [the longest x2 2.99 us: projected(): pl.pallas_call(last_kernel, out_shape=(jax.ShapeDtypeStruct((count // 2,...]
    ppermute x9 -> x6, starting transfers between devices: 30.3 us -> 6.61 us  [passed_along(): lax.ppermute(block, 'dp', [(i, (i + distance) % n_dp) for i in range(n_dp)])]
    ppermute x9 -> x6, waiting for transfers between devices: 0.44 us -> 17.5 us  [passed_along(): lax.ppermute(block, 'dp', [(i, (i + distance) % n_dp) for i in range(n_dp)])]
    ppermute x19 -> x18, waiting for transfers between devices: 43.3 us -> 36.4 us  [swapped(): return lax.ppermute(block, ALL, [(i, i ^ mask) for i in range(total)])]
    dynamic_slice x2 -> x4, local copies, waits for them, and re-layouts: 0.11 us -> 4.6 us  [the longest x2 2.92 us: on_device(): lax.dynamic_index_in_dim(held[part], mine, axis, keepdims=False)]
    convert_element_type x5, other arithmetic: 1.84 us -> 5.15 us  [the longest x4 2.7 us: on_device(): held[part] = held[part].astype(jnp.bfloat16)]
    ppermute x19 -> x18, starting transfers between devices: 17.6 us -> 20 us  [swapped(): return lax.ppermute(block, ALL, [(i, i ^ mask) for i in range(total)])]
    unnamed x28 -> x34, local copies, waits for them, and re-layouts: 0.9 us -> 3.19 us
  transfers between devices with their start and end apart: 28 -> 24, of which waited for: 10 -> 13; matrix products, arithmetic and copies ran while one was open for 7% -> 11% of each run, Pallas kernels for 39% -> 10%
where the time goes in v2:
time: 118 us
  waiting for transfers between devices  53.9 us (46%)
  starting transfers between devices  26.6 us (23%)
  Pallas kernels  14.8 us (13%)
  local copies, waits for them, and re-layouts  12 us (10%)
  other arithmetic  8.86 us (8%)
  between operations  1.66 us (1%)
    ppermute x18, waiting for transfers between devices, swapped(): return lax.ppermute(block, ALL, [(i, i ^ mask) for i in range(total)])  36.4 us
    ppermute x18, starting transfers between devices, swapped(): return lax.ppermute(block, ALL, [(i, i ^ mask) for i in range(total)])  20 us
    ppermute x6, waiting for transfers between devices, passed_along(): lax.ppermute(block, 'dp', [(i, (i + distance) % n_dp) for i in range(n_dp)])  17.5 us
    ppermute x6, starting transfers between devices, passed_along(): lax.ppermute(block, 'dp', [(i, (i + distance) % n_dp) for i in range(n_dp)])  6.61 us
    pallas_call x1, Pallas kernels, attention_weights(): pl.pallas_call(kernel, grid=(heads_kv,), out_shape=jax.ShapeDtypeStruct((...  6.39 us
    unnamed x34, local copies, waits for them, and re-layouts  3.19 us
    pallas_call x2, Pallas kernels, projected(): pl.pallas_call(last_kernel, out_shape=(jax.ShapeDtypeStruct((count // 2,...  2.99 us
    dynamic_slice x2, local copies, waits for them, and re-layouts, on_device(): lax.dynamic_index_in_dim(held[part], mine, axis, keepdims=False)  2.92 us
  transfers between devices with their start and end apart: 24, of which 13 were waited for; matrix products, arithmetic and copies ran while one was open for 11% of the time, Pallas kernels for 10%

profile of v2, /device:TPU:0, one launch (start us, length us, event | category | flops | bytes accessed | tf_op | source)
XLA Modules:
  0.0 117.8 jit_solution(11745515624570552994)
XLA Ops:
  0.7 2.7 %fusion.22 = (bf16[8,256,256]{2,1,0:T(8,128)(2,1)}, bf16[8,256,256]{2,1,0:T(8,128)(2,1)S(1)}) fusion(bf16[8,256,512]{2,1,0:T(8,128)(2,1)} %param.9), kind=kLoop, calls=%fused_computation.64 | loop fusion | bytes 4194304 | tf_op jit(solution)/shard_map/slice | solution.py:259
  3.3 0.9 constant_dynamic-slice_fusion.1
  4.2 0.9 copy.29
  5.1 3.0 %collective-permute-start.4 = (bf16[2,2,256,256]{3,2,0,1:T(8,128)(2,1)}, bf16[2,2,256,256]{3,2,0,1:T(8,128)(2,1)}, u32[]{:S(2)}, u32[]{:S(2)}) collective-permute-start(bf16[2,2,256,256]{3,2,0,1:T(8,128)(2,1)} %bitcast.61), channel_id=1, source_target_pairs={{0,8},{1,9},{2,10},{3,11},{4,12},{5,13},{6,14},{7,15},{8,0},{9,1},... | collective-permute-start | bytes 1572872 | tf_op jit(solution)/shard_map/ppermute | solution.py:27
  8.1 2.1 %constant_dynamic-slice_fusion.3 = (bf16[2,2,1,256,256]{4,3,2,1,0:T(8,128)(2,1)}, bf16[2,2,1,256,256]{4,3,2,1,0:T(8,128)(2,1)S(1)}) fusion(bf16[2,2,2,256,256]{4,3,2,1,0:T(8,128)(2,1)} %bitcast.64, s32[]{:T(128)S(6)} %select_n.61, s32[]{:T(128)S(6)} %select_n.62), kind=kLoop, calls=%fused_computation.56 | loop fusion | bytes 2097160 | tf_op jit(solution)/shard_map/jit(dynamic_index_in_dim)/dynamic_slice | solution.py:270
  10.2 0.8 copy.30
  11.0 1.5 %collective-permute-start = (bf16[2,2,256,256]{3,2,0,1:T(8,128)(2,1)}, bf16[2,2,256,256]{3,2,0,1:T(8,128)(2,1)}, u32[]{:S(2)}, u32[]{:S(2)}) collective-permute-start(bf16[2,2,256,256]{3,2,0,1:T(8,128)(2,1)} %bitcast.62), channel_id=1, source_target_pairs={{0,4},{1,5},{2,6},{3,7},{4,0},{5,1},{6,2},{7,3},{8,12},{9,13},{10,... | collective-permute-start | bytes 1572872 | tf_op jit(solution)/shard_map/ppermute | solution.py:27
  12.5 0.1 broadcast_add_fusion.picks_ref
  12.6 1.6 %pack_hidden.1 = (bf16[128,2048]{1,0:T(8,128)(2,1)S(1)}, bf16[128,2048]{1,0:T(8,128)(2,1)}, bf16[128,2048]{1,0:T(8,128)(2,1)S(1)}, bf16[128,2048]{1,0:T(8,128)(2,1)S(1)}) custom-call(s32[4,8]{1,0:T(4,128)S(1)} %broadcast_add_fusion.picks_ref, bf16[128,8192]{1,0:T(8,128)(2,1)S(1)} %bitcast.63), custom_call_target="tpu_custom_call" | custom-call | bytes 4194304 | tf_op jit(solution)/shard_map/pack_hidden/pallas_call | solution.py:63
  14.2 6.1 %collective-permute-done.4 = bf16[2,2,256,256]{3,2,0,1:T(8,128)(2,1)} collective-permute-done((bf16[2,2,256,256]{3,2,0,1:T(8,128)(2,1)}, bf16[2,2,256,256]{3,2,0,1:T(8,128)(2,1)}, u32[]{:S(2)}, u32[]{:S(2)}) %collective-permute-start.4) | collective-permute-done | bytes 524320 | tf_op jit(solution)/shard_map/ppermute | solution.py:27
  20.3 1.3 %fusion = bf16[2,2,256,256]{3,2,0,1:T(8,128)(2,1)S(1)} fusion(bf16[2,2,256,256]{3,2,0,1:T(8,128)(2,1)} %collective-permute-done.4, bf16[2,1,2,256,256]{4,3,2,1,0:T(8,128)(2,1)} %get-tuple-element.71), kind=kLoop, calls=%fused_computation.1 | loop fusion | flops 1048576 | bytes 1572864 | tf_op jit(solution)/shard_map/convert_element_type | solution.py:282
  21.7 1.7 %collective-permute-start.5 = (bf16[2,256,256]{2,1,0:T(8,128)(2,1)S(1)}, bf16[2,256,256]{2,1,0:T(8,128)(2,1)S(1)}, u32[]{:S(2)}, u32[]{:S(2)}) collective-permute-start(bf16[2,256,256]{2,1,0:T(8,128)(2,1)S(1)} %dynamic-slice_bitcast_fusion), channel_id=1, source_target_pairs={{0,4},{1,5},{2,6},{3,7},{4,0},{5,1},{6,2},{7,3},{8,12},{9,13},{10,... | collective-permute-start | bytes 786440 | tf_op jit(solution)/shard_map/ppermute | solution.py:27
  23.4 2.1 %collective-permute-done = bf16[2,2,256,256]{3,2,0,1:T(8,128)(2,1)} collective-permute-done((bf16[2,2,256,256]{3,2,0,1:T(8,128)(2,1)}, bf16[2,2,256,256]{3,2,0,1:T(8,128)(2,1)}, u32[]{:S(2)}, u32[]{:S(2)}) %collective-permute-start) | collective-permute-done | bytes 524320 | tf_op jit(solution)/shard_map/ppermute | solution.py:27
  25.6 1.7 %collective-permute-start.2 = (bf16[128,2048]{1,0:T(8,128)(2,1)S(1)}, bf16[128,2048]{1,0:T(8,128)(2,1)S(1)}, u32[]{:S(2)}, u32[]{:S(2)}) collective-permute-start(bf16[128,2048]{1,0:T(8,128)(2,1)S(1)} %get-tuple-element.36), channel_id=1, source_target_pairs={{0,2},{1,3},{2,0},{3,1},{4,6},{5,7},{6,4},{7,5},{8,10},{9,11},{10,... | collective-permute-start | bytes 1572872 | tf_op jit(solution)/shard_map/ppermute | solution.py:27
  27.2 1.2 %fusion.1 = bf16[2,2,256,256]{3,2,0,1:T(8,128)(2,1)S(1)} fusion(bf16[2,2,256,256]{3,2,0,1:T(8,128)(2,1)} %collective-permute-done, bf16[2,2,1,256,256]{4,3,2,1,0:T(8,128)(2,1)S(1)} %copy-done.8), kind=kLoop, calls=%fused_computation.3 | loop fusion | flops 1048576 | bytes 1572864 | tf_op jit(solution)/shard_map/convert_element_type | solution.py:282
  28.5 0.1 collective-permute-start.1
  28.6 1.6 %collective-permute-done.5 = bf16[2,256,256]{2,1,0:T(8,128)(2,1)S(1)} collective-permute-done((bf16[2,256,256]{2,1,0:T(8,128)(2,1)S(1)}, bf16[2,256,256]{2,1,0:T(8,128)(2,1)S(1)}, u32[]{:S(2)}, u32[]{:S(2)}) %collective-permute-start.5) | collective-permute-done | bytes 262176 | tf_op jit(solution)/shard_map/ppermute | solution.py:27
  30.2 0.1 fusion.3
  30.3 2.7 %collective-permute-start.6 = (bf16[256,256]{1,0:T(8,128)(2,1)S(1)}, bf16[256,256]{1,0:T(8,128)(2,1)S(1)}, u32[]{:S(2)}, u32[]{:S(2)}) collective-permute-start(bf16[256,256]{1,0:T(8,128)(2,1)S(1)} %dynamic-slice_bitcast_fusion.2), channel_id=1, source_target_pairs={{0,16},{1,17},{2,18},{3,19},{4,20},{5,21},{6,22},{7,23},{8,24},{9,... | collective-permute-start | bytes 393224 | tf_op jit(solution)/shard_map/ppermute | solution.py:27
  33.0 4.8 %collective-permute-done.1 = bf16[2,256,256]{2,1,0:T(8,128)(2,1)S(1)} collective-permute-done((bf16[2,256,256]{2,1,0:T(8,128)(2,1)S(1)}, bf16[2,256,256]{2,1,0:T(8,128)(2,1)S(1)}, u32[]{:S(2)}, u32[]{:S(2)}) %collective-permute-start.1) | collective-permute-done | bytes 262176 | tf_op jit(solution)/shard_map/ppermute | solution.py:27
  37.8 0.1 fusion.4
  37.9 0.7 copy-done.11
  38.5 2.0 %collective-permute-start.3 = (bf16[256,256]{1,0:T(8,128)(2,1)S(1)}, bf16[256,256]{1,0:T(8,128)(2,1)}, u32[]{:S(2)}, u32[]{:S(2)}) collective-permute-start(bf16[256,256]{1,0:T(8,128)(2,1)S(1)} %dynamic-slice_bitcast_fusion.3), channel_id=1, source_target_pairs={{0,16},{1,17},{2,18},{3,19},{4,20},{5,21},{6,22},{7,23},{8,24},{9,... | collective-permute-start | bytes 393224 | tf_op jit(solution)/shard_map/ppermute | solution.py:27
  40.5 1.6 %collective-permute-start.9 = (bf16[128,2048]{1,0:T(8,128)(2,1)S(1)}, bf16[128,2048]{1,0:T(8,128)(2,1)S(1)}, u32[]{:S(2)}, u32[]{:S(2)}) collective-permute-start(bf16[128,2048]{1,0:T(8,128)(2,1)S(1)} %get-tuple-element.41), channel_id=1, source_target_pairs={{0,3},{1,2},{2,1},{3,0},{4,7},{5,6},{6,5},{7,4},{8,11},{9,10},{10,... | collective-permute-start | bytes 1572872 | tf_op jit(solution)/shard_map/ppermute | solution.py:27
  42.2 3.2 %collective-permute-done.3 = bf16[256,256]{1,0:T(8,128)(2,1)} collective-permute-done((bf16[256,256]{1,0:T(8,128)(2,1)S(1)}, bf16[256,256]{1,0:T(8,128)(2,1)}, u32[]{:S(2)}, u32[]{:S(2)}) %collective-permute-start.3) | collective-permute-done | bytes 131104 | tf_op jit(solution)/shard_map/ppermute | solution.py:27
  45.3 2.5 %subtract_convert_fusion.1 = (bf16[256,256]{1,0:T(8,128)(2,1)S(1)}, f32[256,256]{1,0:T(8,128)S(1)}, bf16[256,256]{1,0:T(8,128)(2,1)S(1)}, f32[256,256]{1,0:T(8,128)}) fusion(f32[256,512]{1,0:T(8,128)} %param.12, f32[256,512]{1,0:T(8,128)} %param.11, f32[256,512]{1,0:T(8,128)S(1)} %copy-done.4, bf16[256,256]{1,0:T(8,128)(2,1)} %collective-permute-done.3, ...), kind=kLoop, calls=%fused_computation.45 | loop fusion | flops 2490368 | bytes 2883588 | tf_op jit(solution)/shard_map/convert_element_type | solution.py:290
  47.8 1.2 %collective-permute-start.7 = (bf16[256,256]{1,0:T(8,128)(2,1)S(1)}, bf16[256,256]{1,0:T(8,128)(2,1)S(1)}, u32[]{:S(2)}, u32[]{:S(2)}) collective-permute-start(bf16[256,256]{1,0:T(8,128)(2,1)S(1)} %get-tuple-element.60), channel_id=1, source_target_pairs={{0,16},{1,17},{2,18},{3,19},{4,20},{5,21},{6,22},{7,23},{8,24},{9,... | collective-permute-start | bytes 393224 | tf_op jit(solution)/shard_map/ppermute | solution.py:27
  49.1 0.5 convert_bitcast_fusion
  49.6 1.7 %collective-permute-start.12 = (bf16[256,256]{1,0:T(8,128)(2,1)S(1)}, bf16[256,256]{1,0:T(8,128)(2,1)S(1)}, u32[]{:S(2)}, u32[]{:S(2)}) collective-permute-start(bf16[256,256]{1,0:T(8,128)(2,1)S(1)} %get-tuple-element.67), channel_id=1, source_target_pairs={{0,16},{1,17},{2,18},{3,19},{4,20},{5,21},{6,22},{7,23},{8,24},{9,... | collective-permute-start | bytes 393224 | tf_op jit(solution)/shard_map/ppermute | solution.py:27
  51.2 2.9 %collective-permute-done.9.refs_3_ = bf16[128,2048]{1,0:T(8,128)(2,1)S(1)} collective-permute-done((bf16[128,2048]{1,0:T(8,128)(2,1)S(1)}, bf16[128,2048]{1,0:T(8,128)(2,1)S(1)}, u32[]{:S(2)}, u32[]{:S(2)}) %collective-permute-start.9) | collective-permute-done | bytes 524320 | tf_op jit(solution)/shard_map/ppermute | solution.py:27
  54.1 3.6 %collective-permute-done.7 = bf16[256,256]{1,0:T(8,128)(2,1)S(1)} collective-permute-done((bf16[256,256]{1,0:T(8,128)(2,1)S(1)}, bf16[256,256]{1,0:T(8,128)(2,1)S(1)}, u32[]{:S(2)}, u32[]{:S(2)}) %collective-permute-start.7) | collective-permute-done | bytes 131104 | tf_op jit(solution)/shard_map/ppermute | solution.py:27
  57.7 0.1 collective-permute-start.10
  57.8 1.5 %collective-permute-done.12 = bf16[256,256]{1,0:T(8,128)(2,1)S(1)} collective-permute-done((bf16[256,256]{1,0:T(8,128)(2,1)S(1)}, bf16[256,256]{1,0:T(8,128)(2,1)S(1)}, u32[]{:S(2)}, u32[]{:S(2)}) %collective-permute-start.12) | collective-permute-done | bytes 131104 | tf_op jit(solution)/shard_map/ppermute | solution.py:27
  59.4 1.6 %collective-permute-start.13 = (bf16[512,256]{1,0:T(8,128)(2,1)S(1)}, bf16[512,256]{1,0:T(8,128)(2,1)S(1)}, u32[]{:S(2)}, u32[]{:S(2)}) collective-permute-start(bf16[512,256]{1,0:T(8,128)(2,1)S(1)} %pad_maximum_fusion.4), channel_id=1, source_target_pairs={{0,4},{1,5},{2,6},{3,7},{4,0},{5,1},{6,2},{7,3},{8,12},{9,13},{10,... | collective-permute-start | bytes 786440 | tf_op jit(solution)/shard_map/ppermute | solution.py:27
  60.9 0.9 pad_maximum_fusion.5.rest_3_
  61.9 0.5 collective-permute-start.14
  62.4 0.7 collective-permute-start.15
  63.1 2.2 %collective-permute-start.16 = (bf16[144,512]{1,0:T(8,128)(2,1)S(1)}, bf16[144,512]{1,0:T(8,128)(2,1)S(1)}, u32[]{:S(2)}, u32[]{:S(2)}) collective-permute-start(bf16[144,512]{1,0:T(8,128)(2,1)S(1)} %pad_maximum_fusion.5.rest_3_), channel_id=1, source_target_pairs={{0,4},{4,8},{8,12},{12,16},{16,20},{20,24},{24,28},{28,0},{1,5},{5... | collective-permute-start | bytes 442376 | tf_op jit(solution)/shard_map/ppermute | solution.py:32
  65.3 4.3 %collective-permute-done.10 = bf16[512,256]{1,0:T(8,128)(2,1)S(1)} collective-permute-done((bf16[512,256]{1,0:T(8,128)(2,1)S(1)}, bf16[512,256]{1,0:T(8,128)(2,1)S(1)}, u32[]{:S(2)}, u32[]{:S(2)}) %collective-permute-start.10) | collective-permute-done | bytes 262176 | tf_op jit(solution)/shard_map/ppermute | solution.py:27
  69.6 0.1 collective-permute-start.11
  69.7 6.9 %collective-permute-done.14.rest_0_ = bf16[144,512]{1,0:T(8,128)(2,1)S(1)} collective-permute-done((bf16[144,512]{1,0:T(8,128)(2,1)S(1)}, bf16[144,512]{1,0:T(8,128)(2,1)S(1)}, u32[]{:S(2)}, u32[]{:S(2)}) %collective-permute-start.14) | collective-permute-done | bytes 147488 | tf_op jit(solution)/shard_map/ppermute | solution.py:32
  76.7 0.6 copy-done.13
  77.3 0.0 copy-done.14
  78.0 1.4 %copy.18.seg_ref = f32[128,1]{1,0:T(8,128)} copy(f32[128,1]{0,1:T(1,128)} %get-tuple-element.74) | data formatting | bytes 1024 | tf_op jit(solution)/shard_map/reshape | solution.py:255
  79.3 0.6 pad_add_fusion.place_ref
  79.9 0.5 projected_first.2.refs_4_
  80.4 0.8 copy-done.2
  81.2 6.4 %attention_weights.1.w_ref = bf16[4,1024,512]{2,1,0:T(8,128)(2,1)} custom-call(s32[2]{0:T(128)} %pad_add_fusion.place_ref, bf16[1,128,4096]{2,1,0:T(8,128)(2,1)} %q_ref.1, f32[128,1]{1,0:T(8,128)} %copy.18.seg_ref, bf16[144,512]{1,0:T(8,128)(2,1)} %copy-done.13, bf16[144,512]{1,0:T(8,128)(2,1)} %copy-done.14, bf16[144,512]{1,0:T(8,128)(2,1)} %copy-done.15, ...), custom_call_target="tpu_custom_call" | custom-call | flops 536870912 | bytes 5242880 | tf_op jit(solution)/shard_map/attention_weights/pallas_call | solution.py:176
  87.6 1.0 copy-done.3
  88.6 1.5 %projected_last.2 = (f32[2,128,256]{2,1,0:T(8,128)S(1)}, bf16[2,128,256]{2,1,0:T(8,128)(2,1)S(1)}) custom-call(bf16[128,2048]{1,0:T(8,128)(2,1)S(1)} %get-tuple-element.48.refs_0_, bf16[128,2048]{1,0:T(8,128)(2,1)S(1)} %collective-permute-done.8.refs_1_, bf16[128,2048]{1,0:T(8,128)(2,1)S(1)} %collective-permute-done.2.refs_2_, ...), custom_call_target="tpu_custom_call" | custom-call | flops 268435456 | bytes 1048576 | tf_op jit(solution)/shard_map/projected_last/pallas_call | solution.py:128
  90.1 0.1 collective-permute-start.17
  90.2 0.4 projected_first.3.refs_4_
  90.6 1.5 %projected_last.3 = (f32[2,128,256]{2,1,0:T(8,128)S(1)}, bf16[2,128,256]{2,1,0:T(8,128)(2,1)S(1)}) custom-call(bf16[128,2048]{1,0:T(8,128)(2,1)S(1)} %get-tuple-element.48.refs_0_, bf16[128,2048]{1,0:T(8,128)(2,1)S(1)} %collective-permute-done.8.refs_1_, bf16[128,2048]{1,0:T(8,128)(2,1)S(1)} %collective-permute-done.2.refs_2_, ...), custom_call_target="tpu_custom_call" | custom-call | flops 268435456 | bytes 1048576 | tf_op jit(solution)/shard_map/projected_last/pallas_call | solution.py:128
  92.2 0.6 collective-permute-start.19
  92.8 1.0 collective-permute-done.19
  93.8 0.1 maximum_bitcast_fusion
  93.9 0.5 collective-permute-start.20
  94.4 5.3 %collective-permute-done.20 = bf16[1,128,512]{2,1,0:T(8,128)(2,1)S(1)} collective-permute-done((bf16[1,128,512]{2,1,0:T(8,128)(2,1)S(1)}, bf16[1,128,512]{2,1,0:T(8,128)(2,1)S(1)}, u32[]{:S(2)}, u32[]{:S(2)}) %collective-permute-start.20) | collective-permute-done | bytes 131104 | tf_op jit(solution)/shard_map/ppermute | solution.py:27
  99.7 0.8 collective-permute-start.21
  100.6 1.3 %collective-permute-start.22 = (bf16[128,512]{1,0:T(8,128)(2,1)S(1)}, bf16[128,512]{1,0:T(8,128)(2,1)S(1)}, u32[]{:S(2)}, u32[]{:S(2)}) collective-permute-start(bf16[128,512]{1,0:T(8,128)(2,1)S(1)} %fusion.19.rest_3_), channel_id=1, source_target_pairs={{0,8},{4,12},{8,16},{12,20},{16,24},{20,28},{24,0},{28,4},{1,9},{5... | collective-permute-start | bytes 393224 | tf_op jit(solution)/shard_map/ppermute | solution.py:32
  101.8 1.1 collective-permute-start.23
  102.9 1.4 %multiply_subtract_fusion = (f32[256,512]{1,0:T(8,128)}, f32[256,512]{1,0:T(8,128)}, f32[256,512]{1,0:T(8,128)}) fusion(f32[256,512]{1,0:T(8,128)S(1)} %copy-done.5, f32[256,256]{1,0:T(8,128)S(1)} %copy-done.9, f32[256,256]{1,0:T(8,128)S(1)} %get-tuple-element.61, f32[256,512]{1,0:T(8,128)S(1)} %copy-done.7, f32[256,512]{1,0:T(8,128)S(1)} %copy-done.6), kind=kLoop, calls=%fused_computation.18 | loop fusion | flops 2097152 | bytes 3670016 | tf_op jit(solution)/shard_map/sub | solution.py:41
  104.3 10.6 %collective-permute-done.21.rest_0_ = bf16[128,512]{1,0:T(8,128)(2,1)S(1)} collective-permute-done((bf16[128,512]{1,0:T(8,128)(2,1)S(1)}, bf16[128,512]{1,0:T(8,128)(2,1)S(1)}, u32[]{:S(2)}, u32[]{:S(2)}) %collective-permute-start.21) | collective-permute-done | bytes 131104 | tf_op jit(solution)/shard_map/ppermute | solution.py:32
  115.0 2.8 %weighted_values.1 = bf16[1,128,4096]{2,1,0:T(8,128)(2,1)} custom-call(bf16[4,1024,512]{2,1,0:T(8,128)(2,1)S(1)} %copy-done, bf16[128,512]{1,0:T(8,128)(2,1)S(1)} %collective-permute-done.21.rest_0_, bf16[128,512]{1,0:T(8,128)(2,1)S(1)} %collective-permute-done.22.rest_1_, bf16[128,512]{1,0:T(8,128)(2,1)S(1)} %collective-permute-done.23.rest_2_, ...), custom_call_target="tpu_custom_call" | custom-call | flops 536870912 | bytes 4194304 | tf_op jit(solution)/shard_map/weighted_values/pallas_call | solution.py:210
  (58 shorter events, 0.4 us)
Async XLA Ops:
  4.2 8.3 %copy-start.1 = (bf16[1,128,8192]{2,1,0:T(8,128)(2,1)S(1)}, bf16[1,128,8192]{2,1,0:T(8,128)(2,1)}, u32[]{:S(2)}) copy-start(bf16[1,128,8192]{2,1,0:T(8,128)(2,1)} %param.15) | copy-start | bytes 6291460
  5.1 15.3 %collective-permute-start.4 = (bf16[2,2,256,256]{3,2,0,1:T(8,128)(2,1)}, bf16[2,2,256,256]{3,2,0,1:T(8,128)(2,1)}, u32[]{:S(2)}, u32[]{:S(2)}) collective-permute-start(bf16[2,2,256,256]{3,2,0,1:T(8,128)(2,1)} %bitcast.61), channel_id=1, source_target_pairs={{0,8},{1,9},{2,10},{3,11},{4,12},{5,13},{6,14},{7,15},{8,0},{9,1},... | collective-permute-start | bytes 1572872 | tf_op jit(solution)/shard_map/ppermute | solution.py:27
  11.0 14.6 %collective-permute-start = (bf16[2,2,256,256]{3,2,0,1:T(8,128)(2,1)}, bf16[2,2,256,256]{3,2,0,1:T(8,128)(2,1)}, u32[]{:S(2)}, u32[]{:S(2)}) collective-permute-start(bf16[2,2,256,256]{3,2,0,1:T(8,128)(2,1)} %bitcast.62), channel_id=1, source_target_pairs={{0,4},{1,5},{2,6},{3,7},{4,0},{5,1},{6,2},{7,3},{8,12},{9,13},{10,... | collective-permute-start | bytes 1572872 | tf_op jit(solution)/shard_map/ppermute | solution.py:27
  12.6 14.7 %copy-start.8 = (bf16[2,2,1,256,256]{4,3,2,1,0:T(8,128)(2,1)S(1)}, bf16[2,2,1,256,256]{4,3,2,1,0:T(8,128)(2,1)}, u32[]{:S(2)}) copy-start(bf16[2,2,1,256,256]{4,3,2,1,0:T(8,128)(2,1)} %get-tuple-element.69) | copy-start | bytes 1572868
  21.7 8.5 %collective-permute-start.5 = (bf16[2,256,256]{2,1,0:T(8,128)(2,1)S(1)}, bf16[2,256,256]{2,1,0:T(8,128)(2,1)S(1)}, u32[]{:S(2)}, u32[]{:S(2)}) collective-permute-start(bf16[2,256,256]{2,1,0:T(8,128)(2,1)S(1)} %dynamic-slice_bitcast_fusion), channel_id=1, source_target_pairs={{0,4},{1,5},{2,6},{3,7},{4,0},{5,1},{6,2},{7,3},{8,12},{9,13},{10,... | collective-permute-start | bytes 786440 | tf_op jit(solution)/shard_map/ppermute | solution.py:27
  25.6 12.2 %collective-permute-start.2 = (bf16[128,2048]{1,0:T(8,128)(2,1)S(1)}, bf16[128,2048]{1,0:T(8,128)(2,1)S(1)}, u32[]{:S(2)}, u32[]{:S(2)}) collective-permute-start(bf16[128,2048]{1,0:T(8,128)(2,1)S(1)} %get-tuple-element.36), channel_id=1, source_target_pairs={{0,2},{1,3},{2,0},{3,1},{4,6},{5,7},{6,4},{7,5},{8,10},{9,11},{10,... | collective-permute-start | bytes 1572872 | tf_op jit(solution)/shard_map/ppermute | solution.py:27
  27.2 18.1 %copy-start.4 = (f32[256,512]{1,0:T(8,128)S(1)}, f32[256,512]{1,0:T(8,128)}, u32[]{:S(2)}) copy-start(f32[256,512]{1,0:T(8,128)} %param.10) | copy-start | bytes 1572868
  28.5 9.2 %collective-permute-start.1 = (bf16[2,256,256]{2,1,0:T(8,128)(2,1)S(1)}, bf16[2,256,256]{2,1,0:T(8,128)(2,1)S(1)}, u32[]{:S(2)}, u32[]{:S(2)}) collective-permute-start(bf16[2,256,256]{2,1,0:T(8,128)(2,1)S(1)} %dynamic-slice_bitcast_fusion.1), channel_id=1, source_target_pairs={{0,8},{1,9},{2,10},{3,11},{4,12},{5,13},{6,14},{7,15},{8,0},{9,1},... | collective-permute-start | bytes 786440 | tf_op jit(solution)/shard_map/ppermute | solution.py:27
  30.3 10.3 %copy-start.10 = (bf16[2,256,256]{2,1,0:T(8,128)(2,1)}, bf16[2,256,256]{2,1,0:T(8,128)(2,1)S(1)}, u32[]{:S(2)}) copy-start(bf16[2,256,256]{2,1,0:T(8,128)(2,1)S(1)} %fusion.3) | copy-start | bytes 786436
  30.3 18.8 %copy-start.16 = (s32[1,128]{1,0:T(1,128)S(1)}, s32[1,128]{1,0:T(1,128)}, u32[]{:S(2)}) copy-start(s32[1,128]{1,0:T(1,128)} %param.16) | copy-start | bytes 1540
  30.3 11.9 %collective-permute-start.6 = (bf16[256,256]{1,0:T(8,128)(2,1)S(1)}, bf16[256,256]{1,0:T(8,128)(2,1)S(1)}, u32[]{:S(2)}, u32[]{:S(2)}) collective-permute-start(bf16[256,256]{1,0:T(8,128)(2,1)S(1)} %dynamic-slice_bitcast_fusion.2), channel_id=1, source_target_pairs={{0,16},{1,17},{2,18},{3,19},{4,20},{5,21},{6,22},{7,23},{8,24},{9,... | collective-permute-start | bytes 393224 | tf_op jit(solution)/shard_map/ppermute | solution.py:27
  37.8 0.7 copy-start.11
  38.5 6.8 %collective-permute-start.3 = (bf16[256,256]{1,0:T(8,128)(2,1)S(1)}, bf16[256,256]{1,0:T(8,128)(2,1)}, u32[]{:S(2)}, u32[]{:S(2)}) collective-permute-start(bf16[256,256]{1,0:T(8,128)(2,1)S(1)} %dynamic-slice_bitcast_fusion.3), channel_id=1, source_target_pairs={{0,16},{1,17},{2,18},{3,19},{4,20},{5,21},{6,22},{7,23},{8,24},{9,... | collective-permute-start | bytes 393224 | tf_op jit(solution)/shard_map/ppermute | solution.py:27
  40.5 10.7 %collective-permute-start.8 = (bf16[128,2048]{1,0:T(8,128)(2,1)}, bf16[128,2048]{1,0:T(8,128)(2,1)S(1)}, u32[]{:S(2)}, u32[]{:S(2)}) collective-permute-start(bf16[128,2048]{1,0:T(8,128)(2,1)} %get-tuple-element.39), channel_id=1, source_target_pairs={{0,1},{1,0},{2,3},{3,2},{4,5},{5,4},{6,7},{7,6},{8,9},{9,8},{10,11... | collective-permute-start | bytes 1572872 | tf_op jit(solution)/shard_map/ppermute | solution.py:27
  40.5 13.6 %collective-permute-start.9 = (bf16[128,2048]{1,0:T(8,128)(2,1)S(1)}, bf16[128,2048]{1,0:T(8,128)(2,1)S(1)}, u32[]{:S(2)}, u32[]{:S(2)}) collective-permute-start(bf16[128,2048]{1,0:T(8,128)(2,1)S(1)} %get-tuple-element.41), channel_id=1, source_target_pairs={{0,3},{1,2},{2,1},{3,0},{4,7},{5,6},{6,5},{7,4},{8,11},{9,10},{10,... | collective-permute-start | bytes 1572872 | tf_op jit(solution)/shard_map/ppermute | solution.py:27
  47.8 9.9 %collective-permute-start.7 = (bf16[256,256]{1,0:T(8,128)(2,1)S(1)}, bf16[256,256]{1,0:T(8,128)(2,1)S(1)}, u32[]{:S(2)}, u32[]{:S(2)}) collective-permute-start(bf16[256,256]{1,0:T(8,128)(2,1)S(1)} %get-tuple-element.60), channel_id=1, source_target_pairs={{0,16},{1,17},{2,18},{3,19},{4,20},{5,21},{6,22},{7,23},{8,24},{9,... | collective-permute-start | bytes 393224 | tf_op jit(solution)/shard_map/ppermute | solution.py:27
  49.6 9.8 %collective-permute-start.12 = (bf16[256,256]{1,0:T(8,128)(2,1)S(1)}, bf16[256,256]{1,0:T(8,128)(2,1)S(1)}, u32[]{:S(2)}, u32[]{:S(2)}) collective-permute-start(bf16[256,256]{1,0:T(8,128)(2,1)S(1)} %get-tuple-element.67), channel_id=1, source_target_pairs={{0,16},{1,17},{2,18},{3,19},{4,20},{5,21},{6,22},{7,23},{8,24},{9,... | collective-permute-start | bytes 393224 | tf_op jit(solution)/shard_map/ppermute | solution.py:27
  57.7 11.8 %collective-permute-start.10 = (bf16[512,256]{1,0:T(8,128)(2,1)S(1)}, bf16[512,256]{1,0:T(8,128)(2,1)S(1)}, u32[]{:S(2)}, u32[]{:S(2)}) collective-permute-start(bf16[512,256]{1,0:T(8,128)(2,1)S(1)} %pad_maximum_fusion.3), channel_id=1, source_target_pairs={{0,8},{1,9},{2,10},{3,11},{4,12},{5,13},{6,14},{7,15},{8,0},{9,1},... | collective-permute-start | bytes 786440 | tf_op jit(solution)/shard_map/ppermute | solution.py:27
  59.4 17.2 %collective-permute-start.13 = (bf16[512,256]{1,0:T(8,128)(2,1)S(1)}, bf16[512,256]{1,0:T(8,128)(2,1)S(1)}, u32[]{:S(2)}, u32[]{:S(2)}) collective-permute-start(bf16[512,256]{1,0:T(8,128)(2,1)S(1)} %pad_maximum_fusion.4), channel_id=1, source_target_pairs={{0,4},{1,5},{2,6},{3,7},{4,0},{5,1},{6,2},{7,3},{8,12},{9,13},{10,... | collective-permute-start | bytes 786440 | tf_op jit(solution)/shard_map/ppermute | solution.py:27
  61.9 18.5 %copy-start.12 = (bf16[144,512]{1,0:T(8,128)(2,1)}, bf16[144,512]{1,0:T(8,128)(2,1)S(1)}, u32[]{:S(2)}) copy-start(bf16[144,512]{1,0:T(8,128)(2,1)S(1)} %pad_maximum_fusion.5.rest_3_) | copy-start | bytes 442372
  61.9 14.7 %collective-permute-start.14 = (bf16[144,512]{1,0:T(8,128)(2,1)S(1)}, bf16[144,512]{1,0:T(8,128)(2,1)S(1)}, u32[]{:S(2)}, u32[]{:S(2)}) collective-permute-start(bf16[144,512]{1,0:T(8,128)(2,1)S(1)} %pad_maximum_fusion.5.rest_3_), channel_id=1, source_target_pairs={{0,12},{4,16},{8,20},{12,24},{16,28},{20,0},{24,4},{28,8},{1,13},{... | collective-permute-start | bytes 442376 | tf_op jit(solution)/shard_map/ppermute | solution.py:32
  62.4 14.2 %collective-permute-start.15 = (bf16[144,512]{1,0:T(8,128)(2,1)S(1)}, bf16[144,512]{1,0:T(8,128)(2,1)S(1)}, u32[]{:S(2)}, u32[]{:S(2)}) collective-permute-start(bf16[144,512]{1,0:T(8,128)(2,1)S(1)} %pad_maximum_fusion.5.rest_3_), channel_id=1, source_target_pairs={{0,8},{4,12},{8,16},{12,20},{16,24},{20,28},{24,0},{28,4},{1,9},{5... | collective-permute-start | bytes 442376 | tf_op jit(solution)/shard_map/ppermute | solution.py:32
  63.1 13.5 %collective-permute-start.16 = (bf16[144,512]{1,0:T(8,128)(2,1)S(1)}, bf16[144,512]{1,0:T(8,128)(2,1)S(1)}, u32[]{:S(2)}, u32[]{:S(2)}) collective-permute-start(bf16[144,512]{1,0:T(8,128)(2,1)S(1)} %pad_maximum_fusion.5.rest_3_), channel_id=1, source_target_pairs={{0,4},{4,8},{8,12},{12,16},{16,20},{20,24},{24,28},{28,0},{1,5},{5... | collective-permute-start | bytes 442376 | tf_op jit(solution)/shard_map/ppermute | solution.py:32
  69.6 17.9 %collective-permute-start.11 = (bf16[1024,256]{1,0:T(8,128)(2,1)S(1)}, bf16[1024,256]{1,0:T(8,128)(2,1)}, u32[]{:S(2)}, u32[]{:S(2)}) collective-permute-start(bf16[1024,256]{1,0:T(8,128)(2,1)S(1)} %pad_maximum_fusion.1.refs_4_), channel_id=1, source_target_pairs={{0,4},{1,5},{2,6},{3,7},{4,0},{5,1},{6,2},{7,3},{8,12},{9,13},{10,... | collective-permute-start | bytes 1572872 | tf_op jit(solution)/shard_map/ppermute | solution.py:27
  76.6 0.7 copy-start.13
  76.6 0.7 copy-start.14
  76.6 1.4 %copy-start.15 = (bf16[144,512]{1,0:T(8,128)(2,1)}, bf16[144,512]{1,0:T(8,128)(2,1)S(1)}, u32[]{:S(2)}) copy-start(bf16[144,512]{1,0:T(8,128)(2,1)S(1)} %collective-permute-done.16.rest_2_) | copy-start | bytes 442372
  77.3 13.4 %collective-permute-start.18 = (bf16[1024,256]{1,0:T(8,128)(2,1)S(1)}, bf16[1024,256]{1,0:T(8,128)(2,1)}, u32[]{:S(2)}, u32[]{:S(2)}) collective-permute-start(bf16[1024,256]{1,0:T(8,128)(2,1)S(1)} %pad_maximum_fusion.2.refs_4_), channel_id=1, source_target_pairs={{0,8},{1,9},{2,10},{3,11},{4,12},{5,13},{6,14},{7,15},{8,0},{9,1},... | collective-permute-start | bytes 1572872 | tf_op jit(solution)/shard_map/ppermute | solution.py:27
  80.4 0.8 copy-start.2
  87.6 1.0 copy-start.3
  90.1 2.7 %collective-permute-start.17 = (bf16[2,128,256]{2,1,0:T(8,128)(2,1)S(1)}, bf16[2,128,256]{2,1,0:T(8,128)(2,1)S(1)}, u32[]{:S(2)}, u32[]{:S(2)}) collective-permute-start(bf16[2,128,256]{2,1,0:T(8,128)(2,1)S(1)} %get-tuple-element.54), channel_id=1, source_target_pairs={{0,1},{1,0},{2,3},{3,2},{4,5},{5,4},{6,7},{7,6},{8,9},{9,8},{10,11... | collective-permute-start | bytes 393224 | tf_op jit(solution)/shard_map/ppermute | solution.py:27
  92.2 10.8 %copy-start.5 = (f32[256,512]{1,0:T(8,128)S(1)}, f32[256,512]{1,0:T(8,128)}, u32[]{:S(2)}) copy-start(f32[256,512]{1,0:T(8,128)} %param.10) | copy-start | bytes 1572868
  92.2 10.8 %copy-start.6 = (f32[256,512]{1,0:T(8,128)S(1)}, f32[256,512]{1,0:T(8,128)}, u32[]{:S(2)}) copy-start(f32[256,512]{1,0:T(8,128)} %param.12) | copy-start | bytes 1572868
  92.2 10.8 %copy-start.7 = (f32[256,512]{1,0:T(8,128)S(1)}, f32[256,512]{1,0:T(8,128)}, u32[]{:S(2)}) copy-start(f32[256,512]{1,0:T(8,128)} %param.11) | copy-start | bytes 1572868
  92.2 10.7 %copy-start.9 = (f32[256,256]{1,0:T(8,128)S(1)}, f32[256,256]{1,0:T(8,128)}, u32[]{:S(2)}) copy-start(f32[256,256]{1,0:T(8,128)} %get-tuple-element.68) | copy-start | bytes 786436
  92.2 1.5 %collective-permute-start.19 = (bf16[2,128,256]{2,1,0:T(8,128)(2,1)S(1)}, bf16[2,128,256]{2,1,0:T(8,128)(2,1)S(1)}, u32[]{:S(2)}, u32[]{:S(2)}) collective-permute-start(bf16[2,128,256]{2,1,0:T(8,128)(2,1)S(1)} %get-tuple-element.57), channel_id=1, source_target_pairs={{0,1},{1,0},{2,3},{3,2},{4,5},{5,4},{6,7},{7,6},{8,9},{9,8},{10,11... | collective-permute-start | bytes 393224 | tf_op jit(solution)/shard_map/ppermute | solution.py:27
  93.9 21.1 %copy-start = (bf16[4,1024,512]{2,1,0:T(8,128)(2,1)S(1)}, bf16[4,1024,512]{2,1,0:T(8,128)(2,1)}, u32[]{:S(2)}) copy-start(bf16[4,1024,512]{2,1,0:T(8,128)(2,1)} %attention_weights.1.w_ref) | copy-start | bytes 12582916
  93.9 5.8 %collective-permute-start.20 = (bf16[1,128,512]{2,1,0:T(8,128)(2,1)S(1)}, bf16[1,128,512]{2,1,0:T(8,128)(2,1)S(1)}, u32[]{:S(2)}, u32[]{:S(2)}) collective-permute-start(bf16[1,128,512]{2,1,0:T(8,128)(2,1)S(1)} %fusion.20), channel_id=1, source_target_pairs={{0,2},{1,3},{2,0},{3,1},{4,6},{5,7},{6,4},{7,5},{8,10},{9,11},{10,... | collective-permute-start | bytes 393224 | tf_op jit(solution)/shard_map/ppermute | solution.py:27
  99.7 15.2 %collective-permute-start.21 = (bf16[128,512]{1,0:T(8,128)(2,1)S(1)}, bf16[128,512]{1,0:T(8,128)(2,1)S(1)}, u32[]{:S(2)}, u32[]{:S(2)}) collective-permute-start(bf16[128,512]{1,0:T(8,128)(2,1)S(1)} %fusion.19.rest_3_), channel_id=1, source_target_pairs={{0,12},{4,16},{8,20},{12,24},{16,28},{20,0},{24,4},{28,8},{1,13},{... | collective-permute-start | bytes 393224 | tf_op jit(solution)/shard_map/ppermute | solution.py:32
  100.6 14.4 %collective-permute-start.22 = (bf16[128,512]{1,0:T(8,128)(2,1)S(1)}, bf16[128,512]{1,0:T(8,128)(2,1)S(1)}, u32[]{:S(2)}, u32[]{:S(2)}) collective-permute-start(bf16[128,512]{1,0:T(8,128)(2,1)S(1)} %fusion.19.rest_3_), channel_id=1, source_target_pairs={{0,8},{4,12},{8,16},{12,20},{16,24},{20,28},{24,0},{28,4},{1,9},{5... | collective-permute-start | bytes 393224 | tf_op jit(solution)/shard_map/ppermute | solution.py:32
  101.8 13.1 %collective-permute-start.23 = (bf16[128,512]{1,0:T(8,128)(2,1)S(1)}, bf16[128,512]{1,0:T(8,128)(2,1)S(1)}, u32[]{:S(2)}, u32[]{:S(2)}) collective-permute-start(bf16[128,512]{1,0:T(8,128)(2,1)S(1)} %fusion.19.rest_3_), channel_id=1, source_target_pairs={{0,4},{4,8},{8,12},{12,16},{16,20},{20,24},{24,28},{28,0},{1,5},{5... | collective-permute-start | bytes 393224 | tf_op jit(solution)/shard_map/ppermute | solution.py:32

commit v3 on v2

v3 whole, which is shorter than its diff:
```python
import jax
import jax.numpy as jnp
from jax import lax
from jax.experimental import pallas as pl
from jax.experimental.pallas import tpu as pltpu
from jax.sharding import PartitionSpec as P

HD = 128
ALL = ("dp", "replica")
SMALL = 12 * 2**20

beta_one = 0.9
beta_two = 0.95
bias_one = 1.0 - 0.9**10
bias_two = 1.0 - 0.95**10
adam_eps = 1e-08
learn_rate = 0.002
weight_decay = 0.1


def bits_of(count):
    return [1 << j for j in range(count.bit_length() - 1)]


def swapped(block, mask):
    total = lax.axis_size("dp") * lax.axis_size("replica")
    return lax.ppermute(block, ALL, [(i, i ^ mask) for i in range(total)])


def passed_along(block, distance):
    n_dp = lax.axis_size("dp")
    return lax.ppermute(block, "dp", [(i, i + distance) for i in range(n_dp - distance)])


def adam_update(grad_sum, master, moment_first, moment_second):
    first_new = beta_one * moment_first + (1.0 - beta_one) * grad_sum
    second_new = beta_two * moment_second + (1.0 - beta_two) * grad_sum * grad_sum
    step_dir = (
        first_new / bias_one / (jnp.sqrt(second_new / bias_two) + adam_eps) + weight_decay * master
    )
    master_new = master - learn_rate * step_dir
    return (master_new, first_new, second_new)


def tied(*values):
    return lax.optimization_barrier(values)


def halving(bits):
    if not bits:
        return [0]
    rest = halving(bits[1:])
    return [offset | bits[0] for offset in rest] + rest


def blocks_taken(terms, flips):
    _, rows, columns = terms.shape
    parts, blocks = len(flips), len(flips[0])
    width = columns // parts

    def kernel(terms_ref, *refs):
        out_refs, sems = refs[:parts], refs[parts]
        here = lax.axis_index("dp")
        copies = []
        for part in range(parts):
            for i, flip in enumerate(flips[part]):
                copies.append(
                    pltpu.make_async_copy(
                        terms_ref.at[here ^ flip, :, pl.ds(part * width, width)],
                        out_refs[part].at[i],
                        sems.at[part, i],
                    )
                )
        for copy in copies:
            copy.start()
        for copy in copies:
            copy.wait()

    return pl.pallas_call(
        kernel,
        in_specs=[pl.BlockSpec(memory_space=pltpu.HBM)],
        out_specs=[pl.BlockSpec(memory_space=pltpu.VMEM)] * parts,
        out_shape=[jax.ShapeDtypeStruct((blocks, rows, width), terms.dtype)] * parts,
        scratch_shapes=[pltpu.SemaphoreType.DMA((parts, blocks))],
        compiler_params=pltpu.CompilerParams(vmem_limit_bytes=SMALL),
        cost_estimate=pl.CostEstimate(
            flops=0, bytes_accessed=4 * blocks * rows * columns, transcendentals=0
        ),
        name="blocks_taken",
    )(terms)


def first_half_sums(streams, left):
    count = len(streams)
    sizes = [len(terms) for terms in streams]
    _, rows, width = streams[0][0].shape

    def kernel(*refs):
        out_ref = refs[-1]
        at = 0
        for i, size in enumerate(sizes):
            for j in range(left // 2):
                total = None
                for ref in refs[at : at + size]:
                    term = ref[ref.shape[0] - left + j].astype(jnp.float32)
                    total = term if total is None else total + term
                out_ref[i, j] = total.astype(jnp.bfloat16)
            at += size

    out = jax.ShapeDtypeStruct((count, left // 2, rows, width), jnp.bfloat16)
    return pl.pallas_call(
        kernel,
        out_shape=out,
        compiler_params=pltpu.CompilerParams(vmem_limit_bytes=SMALL),
        cost_estimate=pl.CostEstimate(
            flops=2 * sizes[0] * out.size, bytes_accessed=8 * out.size, transcendentals=0
        ),
        name="first_half_sums",
    )(*[term for terms in streams for term in terms])


def fresh_rows(streams, state):
    parts = len(streams)
    sizes = [len(terms) for terms in streams]
    _, rows, width = streams[0][0].shape

    def kernel(*refs):
        master_ref, first_ref, second_ref, out_ref = refs[-4:]
        at = 0
        for part, size in enumerate(sizes):
            grad = None
            for ref in refs[at : at + size]:
                term = ref[ref.shape[0] - 1].astype(jnp.float32)
                grad = term if grad is None else grad + term
            at += size
            cut = slice(part * width, (part + 1) * width)
            updated = adam_update(grad, master_ref[:, cut], first_ref[:, cut], second_ref[:, cut])
            out_ref[part] = updated[0].astype(jnp.bfloat16)

    out = jax.ShapeDtypeStruct((parts, rows, width), jnp.bfloat16)
    return pl.pallas_call(
        kernel,
        out_shape=out,
        compiler_params=pltpu.CompilerParams(vmem_limit_bytes=SMALL),
        cost_estimate=pl.CostEstimate(
            flops=20 * out.size, bytes_accessed=20 * out.size, transcendentals=out.size
        ),
        name="fresh_rows",
    )(*[term for terms in streams for term in terms], *state)


def one_below(first, second, part=None):
    rows, width = first.shape[-2:]

    def kernel(first_ref, second_ref, out_ref):
        out_ref[:rows] = first_ref[...] if part is None else first_ref[part]
        out_ref[rows:] = second_ref[...] if part is None else second_ref[part]

    return pl.pallas_call(
        kernel,
        out_shape=jax.ShapeDtypeStruct((2 * rows, width), first.dtype),
        compiler_params=pltpu.CompilerParams(vmem_limit_bytes=SMALL),
        cost_estimate=pl.CostEstimate(
            flops=0, bytes_accessed=8 * rows * width, transcendentals=0
        ),
        name="one_below",
    )(first, second)


def staged(arrays):
    count = len(arrays)

    def kernel(*refs):
        for i in range(count):
            refs[count + i][...] = refs[i][...]

    rows, columns = arrays[0].shape
    return pl.pallas_call(
        kernel,
        grid=(2,),
        in_specs=[pl.BlockSpec((rows, columns // 2), lambda i: (0, i))] * count,
        out_specs=[pl.BlockSpec((rows, columns // 2), lambda i: (0, i))] * count,
        out_shape=[jax.ShapeDtypeStruct(x.shape, x.dtype) for x in arrays],
        compiler_params=pltpu.CompilerParams(vmem_limit_bytes=SMALL),
        cost_estimate=pl.CostEstimate(
            flops=0, bytes_accessed=8 * count * arrays[0].size, transcendentals=0
        ),
        name="staged",
    )(*arrays)


def packed_columns(hidden_rows, width, n_dp, n_replica):
    tokens = hidden_rows.shape[0]
    if width % HD:
        owner = lax.axis_index("dp") ^ jnp.arange(n_dp, dtype=jnp.int32)
        replica = lax.axis_index("replica") ^ jnp.arange(n_replica, dtype=jnp.int32)
        picks = owner[None, :] * n_replica + replica[:, None]
        cut = hidden_rows.reshape(tokens, -1, width)
        taken = jnp.take(cut, picks.reshape(-1), axis=1)
        taken = taken.reshape(tokens, n_replica, n_dp * width)
        return [taken[:, m] for m in range(n_replica)]

    def kernel(source_ref, *out_refs):
        dp, replica = lax.axis_index("dp"), lax.axis_index("replica")
        for m in range(n_replica):
            for o in range(n_dp):
                start = pl.multiple_of(((dp ^ o) * n_replica + (replica ^ m)) * width, width)
                out_refs[m][:, o * width : (o + 1) * width] = source_ref[:, pl.ds(start, width)]

    return pl.pallas_call(
        kernel,
        out_shape=[
            jax.ShapeDtypeStruct((tokens, n_dp * width), hidden_rows.dtype)
            for _ in range(n_replica)
        ],
        compiler_params=pltpu.CompilerParams(vmem_limit_bytes=16 * 2**20),
        cost_estimate=pl.CostEstimate(
            flops=0, bytes_accessed=4 * hidden_rows.size, transcendentals=0
        ),
        name="pack_hidden",
    )(hidden_rows)


def projected(token_blocks, pieces, width, before):
    count = len(token_blocks)
    parts = len(pieces)
    tokens = token_blocks[0].shape[0]
    depth, columns = pieces[0][0].shape

    def total_of(token_ref, weight_ref, places):
        total = None
        for i, place in enumerate(places):
            term = jnp.dot(
                token_ref[:, place * width : (place + 1) * width],
                weight_ref[i * width : (i + 1) * width, :],
                preferred_element_type=jnp.float32,
            )
            total = term if total is None else total + term
        return total

    def first_kernel(*refs):
        for m in range(count):
            for part in range(parts):
                total = total_of(refs[m], refs[count + part], pieces[part][1])
                refs[-1][m, :, part * columns : (part + 1) * columns] = total

    def last_kernel(*refs):
        kept_ref, away_ref = refs[-2], refs[-1]
        for m in range(count):
            for part in range(parts):
                cut = slice(part * columns, (part + 1) * columns)
                total = total_of(refs[m], refs[count + 1 + part], pieces[part][1])
                total = refs[count][m, :, cut] + total
                if m % 2:
                    away_ref[m // 2, :, cut] = total.astype(jnp.bfloat16)
                else:
                    kept_ref[m // 2, :, cut] = total

    cost = pl.CostEstimate(
        flops=2 * count * tokens * depth * columns * parts,
        bytes_accessed=2 * count * tokens * depth * parts,
        transcendentals=0,
    )
    params = pltpu.CompilerParams(vmem_limit_bytes=24 * 2**20)
    weights = [piece for piece, _ in pieces]
    if before is None:
        return pl.pallas_call(
            first_kernel,
            out_shape=jax.ShapeDtypeStruct((count, tokens, columns * parts), jnp.float32),
            compiler_params=params,
            cost_estimate=cost,
            name="projected_first",
        )(*token_blocks, *weights)
    return pl.pallas_call(
        last_kernel,
        out_shape=(
            jax.ShapeDtypeStruct((count // 2, tokens, columns * parts), jnp.float32),
            jax.ShapeDtypeStruct((count // 2, tokens, columns * parts), jnp.bfloat16),
        ),
        compiler_params=params,
        cost_estimate=cost,
        name="projected_last",
    )(*token_blocks, before, *weights)


def keys_and_numbers(keys_in, segment_ids):
    _, tokens, columns = keys_in.shape

    def kernel(key_ref, seg_ref, out_ref):
        out_ref[:tokens, :] = key_ref[0]
        numbers = seg_ref[...].astype(jnp.float32)
        numbers = jnp.concatenate([numbers] * (columns // tokens), axis=1)
        out_ref[tokens:, :] = jnp.broadcast_to(numbers, (16, columns)).astype(jnp.bfloat16)

    return pl.pallas_call(
        kernel,
        out_shape=jax.ShapeDtypeStruct((tokens + 16, columns), keys_in.dtype),
        compiler_params=pltpu.CompilerParams(vmem_limit_bytes=SMALL),
        name="keys_and_numbers",
    )(keys_in, segment_ids)


def attention_weights(packed_len, queries, key_blocks):
    tokens = queries.shape[1]
    heads_kv = key_blocks[0].shape[1] // HD
    groups = queries.shape[2] // (heads_kv * HD)
    spans = len(key_blocks)
    padded = key_blocks[0].shape[0]
    keys_all = spans * tokens

    def kernel(used_ref, q_ref, *rest):
        key_refs, out_ref = rest[:-1], rest[-1]
        here, used = lax.axis_index("dp"), used_ref[0]
        keys = jnp.concatenate([ref[0:tokens, :] for ref in key_refs], axis=0)
        seg_keys = jnp.concatenate(
            [ref[tokens : tokens + 16, :].astype(jnp.float32)[0:1, :] for ref in key_refs], axis=1
        )
        row = lax.broadcasted_iota(jnp.int32, (tokens, keys_all), 0)
        offset = lax.broadcasted_iota(jnp.int32, (tokens, keys_all), 1) - (spans - 1) * tokens
        seg_own = jnp.sum(jnp.where(offset == row, seg_keys, 0.0), axis=1, keepdims=True)
        allowed = (seg_own == seg_keys) & (offset <= row) & (offset + here * tokens >= 0)
        live = (here * tokens + lax.broadcasted_iota(jnp.int32, (tokens, 1), 0)) < used
        for j in range(groups):
            scores = lax.dot_general(
                q_ref[0, :, j * HD : (j + 1) * HD],
                keys,
                (((1,), (1,)), ((), ())),
                preferred_element_type=jnp.float32,
            ) * HD ** (-0.5)
            scores = jnp.where(allowed, scores, -1e30)
            weights = jnp.exp(scores - jnp.max(scores, axis=-1, keepdims=True))
            totals = jnp.sum(weights, axis=-1, keepdims=True)
            scale = jnp.where(live, 1.0 / totals, 0.0)
            out_ref[0, j * tokens : (j + 1) * tokens, :] = (weights * scale).astype(jnp.bfloat16)

    key_spec = pl.BlockSpec((padded, HD), lambda g: (0, g))
    return pl.pallas_call(
        kernel,
        grid=(heads_kv,),
        out_shape=jax.ShapeDtypeStruct((heads_kv, groups * tokens, keys_all), jnp.bfloat16),
        in_specs=[
            pl.BlockSpec(memory_space=pltpu.SMEM),
            pl.BlockSpec((1, tokens, groups * HD), lambda g: (0, 0, g)),
        ]
        + [key_spec] * spans,
        out_specs=pl.BlockSpec((1, groups * tokens, keys_all), lambda g: (g, 0, 0)),
        compiler_params=pltpu.CompilerParams(vmem_limit_bytes=16 * 2**20),
        cost_estimate=pl.CostEstimate(
            flops=2 * heads_kv * groups * tokens * keys_all * HD,
            bytes_accessed=2 * heads_kv * groups * tokens * (keys_all + HD),
            transcendentals=heads_kv * groups * tokens * keys_all,
        ),
        name="attention_weights",
    )(packed_len, queries, *key_blocks)


def weighted_values(weights, value_blocks):
    heads_kv, rows, keys_all = weights.shape
    tokens, columns = value_blocks[0].shape
    groups = rows // tokens

    def kernel(w_ref, *rest):
        value_refs, out_ref = rest[:-1], rest[-1]
        for g in range(heads_kv):
            cut = slice(g * HD, (g + 1) * HD)
            values = jnp.concatenate([ref[:, cut] for ref in value_refs], axis=0)
            mixed = jnp.dot(w_ref[g], values, preferred_element_type=jnp.float32)
            for j in range(groups):
                place = (g * groups + j) * HD
                out_ref[0, :, place : place + HD] = mixed[
                    j * tokens : (j + 1) * tokens, :
                ].astype(jnp.bfloat16)

    return pl.pallas_call(
        kernel,
        out_shape=jax.ShapeDtypeStruct((1, tokens, heads_kv * groups * HD), jnp.bfloat16),
        compiler_params=pltpu.CompilerParams(vmem_limit_bytes=24 * 2**20),
        cost_estimate=pl.CostEstimate(
            flops=2 * heads_kv * rows * keys_all * HD,
            bytes_accessed=2 * heads_kv * rows * keys_all,
            transcendentals=0,
        ),
        name="weighted_values",
    )(weights, *value_blocks)


def on_device(
    grad_parts,
    master_weight,
    moment_one,
    moment_two,
    queries,
    keys_in,
    hidden,
    segment_ids,
    packed_len,
):
    n_dp, n_replica = lax.axis_size("dp"), lax.axis_size("replica")
    tokens = queries.shape[1]
    rows, columns = master_weight.shape
    bits = bits_of(n_dp)
    orders = [bits, [bits[1], bits[0]] + bits[2:]]
    parts = len(orders)
    width = columns // parts
    state = (master_weight, moment_one, moment_two)

    flips = [halving(order) for order in orders]
    away = blocks_taken(grad_parts, [part[: n_dp // 2] for part in flips])
    came = [swapped(block, order[0] * n_replica) for block, order in zip(away, orders)]
    kept = list(blocks_taken(grad_parts, [part[n_dp // 2 :] for part in flips]))

    packed = packed_columns(hidden[0], rows, n_dp, n_replica)

    key_own = keys_and_numbers(keys_in, segment_ids)

    came[0], came[1], kept[0], kept[1], key_own, *packed = tied(
        came[0], came[1], kept[0], kept[1], key_own, *packed
    )
    streams = [[kept[part], came[part]] for part in range(parts)]
    token_blocks = [packed[0]] + [swapped(packed[m], m) for m in range(1, n_replica)]
    key_blocks = [passed_along(key_own, d) for d in (3, 2, 1)] + [key_own]
    state_here = staged(state)

    left = n_dp // 2
    for step in range(1, len(bits)):
        marks = [order[step] for order in orders]
        if marks[0] == marks[1]:
            both = swapped(first_half_sums(streams, left), marks[0] * n_replica)
            came = [both[part] for part in range(parts)]
        else:
            came = [
                swapped(first_half_sums([terms], left)[0], mark * n_replica)
                for terms, mark in zip(streams, marks)
            ]
        left = left // 2
        if step == 1:
            came[0], came[1], key_blocks[0], *state_here = tied(
                came[0], came[1], key_blocks[0], *state_here
            )
        if step == 2:
            came[0], came[1], token_blocks[2], key_blocks[1] = tied(
                came[0], came[1], token_blocks[2], key_blocks[1]
            )
        for part in range(parts):
            streams[part].append(came[part])

    fresh = fresh_rows(streams, state_here)
    grad_total = [
        sum(term[-1].astype(jnp.float32) for term in streams[part]) for part in range(parts)
    ]
    new_master, new_first, new_second = adam_update(
        jnp.concatenate(grad_total, axis=1), *state
    )
    labels = [[0] for _ in orders]
    for step in range(len(bits)):
        marks = [order[-1 - step] for order in orders]
        if marks[0] == marks[1]:
            came = swapped(fresh, marks[0] * n_replica)
            if step == 0:
                came, key_blocks[2], token_blocks[1] = tied(came, key_blocks[2], token_blocks[1])
                weights = attention_weights(packed_len, queries, key_blocks)
            joined = [one_below(fresh, came, part) for part in range(parts)]
            fresh = jnp.stack(joined) if step + 3 < len(bits) else None
        else:
            came = [swapped(joined[part], marks[part] * n_replica) for part in range(parts)]
            if step == len(bits) - 1:
                break
            came[0], came[1], *token_blocks = tied(came[0], came[1], *token_blocks)
            joined = [one_below(joined[part], came[part]) for part in range(parts)]
        labels = [own + [label ^ mark for label in own] for own, mark in zip(labels, marks)]
    last = [[label ^ mark for label in own] for own, mark in zip(labels, marks)]
    before = projected(token_blocks, list(zip(joined, labels)), rows, None)
    came[0], came[1], weights, before = tied(came[0], came[1], weights, before)
    partial, leaving = projected(token_blocks, list(zip(came, last)), rows, before)

    came = swapped(leaving, 1)
    partial = partial + came.astype(jnp.float32)
    for bit in bits_of(n_replica)[1:]:
        partial = partial.reshape(-1, 2, tokens, columns)
        came = swapped(partial[:, 1].astype(jnp.bfloat16), bit)
        partial = partial[:, 0] + came.astype(jnp.float32)
    value = partial[0].astype(jnp.bfloat16)
    value_blocks = [passed_along(value, d) for d in (3, 2, 1)] + [value]
    attended = weighted_values(weights, value_blocks)
    return (new_master, new_first, new_second, attended)


def solution(mesh):
    in_specs = (
        P("dp", "replica", None),
        P(("dp", "replica"), None),
        P(("dp", "replica"), None),
        P(("dp", "replica"), None),
        P("replica", "dp", None),
        P("replica", "dp", None),
        P("replica", "dp", None),
        P("replica", "dp"),
        P("replica"),
    )
    out_specs = (
        P(("dp", "replica"), None),
        P(("dp", "replica"), None),
        P(("dp", "replica"), None),
        P("replica", "dp", None),
    )
    return jax.shard_map(
        on_device, mesh=mesh, in_specs=in_specs, out_specs=out_specs, check_vma=False
    )
```

time: 118 us -> 112 us (0.949); the launches traced: 118 us -> 110 us
  starting transfers between devices: 26.6 us -> 51.7 us
  waiting for transfers between devices: 53.9 us -> 43.3 us
  local copies, waits for them, and re-layouts: 12 us -> 1.66 us
  other arithmetic: 8.86 us -> 1.62 us
  Pallas kernels: 14.8 us -> 9.72 us
    ppermute x6, starting transfers between devices: 6.61 us -> 26.2 us  [passed_along(): lax.ppermute(block, 'dp', [(i, i + distance) for i in range(n_dp - distan...]
    ppermute x6, waiting for transfers between devices: 17.5 us -> 10.7 us  [passed_along(): lax.ppermute(block, 'dp', [(i, i + distance) for i in range(n_dp - distan...]
    ppermute x18 -> x15, starting transfers between devices: 20 us -> 25.5 us  [swapped(): return lax.ppermute(block, ALL, [(i, i ^ mask) for i in range(total)])]
    convert_element_type x5 -> x0, other arithmetic: 5.15 us -> none  [the longest x4 2.7 us: on_device(): held[part] = held[part].astype(jnp.bfloat16)]
    dynamic_slice x4 -> x0, local copies, waits for them, and re-layouts: 4.6 us -> none  [the longest x2 2.92 us: on_device(): lax.dynamic_index_in_dim(held[part], mine, axis, keepdims=False)]
    ppermute x18 -> x15, waiting for transfers between devices: 36.4 us -> 32.6 us  [swapped(): return lax.ppermute(block, ALL, [(i, i ^ mask) for i in range(total)])]
    slice x1 -> x0, local copies, waits for them, and re-layouts: 2.68 us -> none  [on_device(): grad_parts[:, :, cut].reshape((2,) * len(names) + (rows, width))]
    pallas_call x2 -> x1, Pallas kernels: 2.99 us -> 0.72 us  [projected(): pl.pallas_call(last_kernel, out_shape=(jax.ShapeDtypeStruct((count // 2,...]
  transfers between devices with their start and end apart: 24 -> 21, of which waited for: 13 -> 13; matrix products, arithmetic and copies ran while one was open for 11% -> 1% of each run, Pallas kernels for 10% -> 6%
where the time goes in v3:
time: 112 us; the launch traced here: 110 us
  starting transfers between devices  51.7 us (46%)
  waiting for transfers between devices  43.3 us (39%)
  Pallas kernels  9.72 us (9%)
  local copies, waits for them, and re-layouts  1.66 us (1%)
  other arithmetic  1.62 us (1%)
  between operations  1.56 us (1%)
    ppermute x15, waiting for transfers between devices, swapped(): return lax.ppermute(block, ALL, [(i, i ^ mask) for i in range(total)])  32.6 us
    ppermute x6, starting transfers between devices, passed_along(): lax.ppermute(block, 'dp', [(i, i + distance) for i in range(n_dp - distan...  26.2 us
    ppermute x15, starting transfers between devices, swapped(): return lax.ppermute(block, ALL, [(i, i ^ mask) for i in range(total)])  25.5 us
    ppermute x6, waiting for transfers between devices, passed_along(): lax.ppermute(block, 'dp', [(i, i + distance) for i in range(n_dp - distan...  10.7 us
    pallas_call x1, Pallas kernels, attention_weights(): pl.pallas_call(kernel, grid=(heads_kv,), out_shape=jax.ShapeDtypeStruct((...  4.18 us
  transfers between devices with their start and end apart: 21, of which 13 were waited for; matrix products, arithmetic and copies ran while one was open for 1% of the time, Pallas kernels for 6%

profile of v3, /device:TPU:0, one launch (start us, length us, event | category | flops | bytes accessed | tf_op | source)
XLA Modules:
  0.0 109.5 jit_solution(13715707500867985758)
XLA Ops:
  0.6 0.0 copy-start
  0.6 1.6 %copy-done = bf16[8,256,512]{2,1,0:T(8,128)(2,1)S(1)} copy-done((bf16[8,256,512]{2,1,0:T(8,128)(2,1)S(1)}, bf16[8,256,512]{2,1,0:T(8,128)(2,1)}, u32[]{:S(2)}) %copy-start) | copy-done | bytes 2097176
  2.2 0.2 blocks_taken.2
  2.4 3.0 %collective-permute-start = (bf16[4,256,256]{2,1,0:T(8,128)(2,1)S(1)}, bf16[4,256,256]{2,1,0:T(8,128)(2,1)S(1)}, u32[]{:S(2)}, u32[]{:S(2)}) collective-permute-start(bf16[4,256,256]{2,1,0:T(8,128)(2,1)S(1)} %get-tuple-element.49), channel_id=1, source_target_pairs={{0,4},{1,5},{2,6},{3,7},{4,0},{5,1},{6,2},{7,3},{8,12},{9,13},{10,... | collective-permute-start | bytes 1572872 | tf_op jit(solution)/shard_map/ppermute | solution.py:27
  5.4 1.6 %collective-permute-start.1 = (bf16[4,256,256]{2,1,0:T(8,128)(2,1)S(1)}, bf16[4,256,256]{2,1,0:T(8,128)(2,1)S(1)}, u32[]{:S(2)}, u32[]{:S(2)}) collective-permute-start(bf16[4,256,256]{2,1,0:T(8,128)(2,1)S(1)} %get-tuple-element.50), channel_id=1, source_target_pairs={{0,8},{1,9},{2,10},{3,11},{4,12},{5,13},{6,14},{7,15},{8,0},{9,1},... | collective-permute-start | bytes 1572872 | tf_op jit(solution)/shard_map/ppermute | solution.py:27
  7.0 0.2 blocks_taken.3
  7.2 0.0 copy-start.1
  7.2 0.0 copy-start.2
  7.2 0.0 copy-start.3
  7.2 0.3 pack_hidden.1
  7.5 9.8 %collective-permute-done.refs_1_ = bf16[4,256,256]{2,1,0:T(8,128)(2,1)S(1)} collective-permute-done((bf16[4,256,256]{2,1,0:T(8,128)(2,1)S(1)}, bf16[4,256,256]{2,1,0:T(8,128)(2,1)S(1)}, u32[]{:S(2)}, u32[]{:S(2)}) %collective-permute-start) | collective-permute-done | bytes 524320 | tf_op jit(solution)/shard_map/ppermute | solution.py:27
  17.3 1.5 %collective-permute-done.1.refs_1_.refs_4_.refs_5_ = bf16[4,256,256]{2,1,0:T(8,128)(2,1)S(1)} collective-permute-done((bf16[4,256,256]{2,1,0:T(8,128)(2,1)S(1)}, bf16[4,256,256]{2,1,0:T(8,128)(2,1)S(1)}, u32[]{:S(2)}, u32[]{:S(2)}) %collective-permute-start.1) | collective-permute-done | bytes 524320 | tf_op jit(solution)/shard_map/ppermute | solution.py:27
  18.8 0.1 first_half_sums.4
  18.9 0.4 collective-permute-start.3
  19.3 0.1 first_half_sums.3
  19.4 1.8 %collective-permute-start.2 = (bf16[2,256,256]{2,1,0:T(8,128)(2,1)S(1)}, bf16[2,256,256]{2,1,0:T(8,128)(2,1)S(1)}, u32[]{:S(2)}, u32[]{:S(2)}) collective-permute-start(bf16[2,256,256]{2,1,0:T(8,128)(2,1)S(1)} %bitcast.27), channel_id=1, source_target_pairs={{0,8},{1,9},{2,10},{3,11},{4,12},{5,13},{6,14},{7,15},{8,0},{9,1},... | collective-permute-start | bytes 786440 | tf_op jit(solution)/shard_map/ppermute | solution.py:27
  21.2 3.3 %collective-permute-start.4 = (bf16[144,512]{1,0:T(8,128)(2,1)S(1)}, bf16[144,512]{1,0:T(8,128)(2,1)S(1)}, u32[]{:S(2)}, u32[]{:S(2)}) collective-permute-start(bf16[144,512]{1,0:T(8,128)(2,1)S(1)} %keys_and_numbers.1.rest_3_), channel_id=1, source_target_pairs={{0,12},{4,16},{8,20},{12,24},{16,28},{1,13},{5,17},{9,21},{13,25},... | collective-permute-start | bytes 442376 | tf_op jit(solution)/shard_map/ppermute | solution.py:32
  24.4 1.6 %collective-permute-start.6 = (bf16[128,2048]{1,0:T(8,128)(2,1)S(1)}, bf16[128,2048]{1,0:T(8,128)(2,1)S(1)}, u32[]{:S(2)}, u32[]{:S(2)}) collective-permute-start(bf16[128,2048]{1,0:T(8,128)(2,1)S(1)} %get-tuple-element.67), channel_id=1, source_target_pairs={{0,2},{1,3},{2,0},{3,1},{4,6},{5,7},{6,4},{7,5},{8,10},{9,11},{10,... | collective-permute-start | bytes 1572872 | tf_op jit(solution)/shard_map/ppermute | solution.py:27
  26.0 0.0 copy-done.3
  26.0 0.4 staged.1
  26.4 2.0 %collective-permute-done.4.rest_0_ = bf16[144,512]{1,0:T(8,128)(2,1)S(1)} collective-permute-done((bf16[144,512]{1,0:T(8,128)(2,1)S(1)}, bf16[144,512]{1,0:T(8,128)(2,1)S(1)}, u32[]{:S(2)}, u32[]{:S(2)}) %collective-permute-start.4) | collective-permute-done | bytes 147488 | tf_op jit(solution)/shard_map/ppermute | solution.py:32
  28.5 0.0 collective-permute-done.3.refs_5_.refs_6_
  28.5 0.0 collective-permute-done.2.refs_2_
  28.5 0.1 first_half_sums.5
  28.6 4.4 %collective-permute-start.5 = (bf16[2,1,256,256]{3,2,1,0:T(8,128)(2,1)S(1)}, bf16[2,1,256,256]{3,2,1,0:T(8,128)(2,1)S(1)}, u32[]{:S(2)}, u32[]{:S(2)}) collective-permute-start(bf16[2,1,256,256]{3,2,1,0:T(8,128)(2,1)S(1)} %first_half_sums.5), channel_id=1, source_target_pairs={{0,16},{1,17},{2,18},{3,19},{4,20},{5,21},{6,22},{7,23},{8,24},{9,... | collective-permute-start | bytes 786440 | tf_op jit(solution)/shard_map/ppermute | solution.py:27
  33.0 0.0 collective-permute-start.10
  33.0 7.6 %collective-permute-start.7 = (bf16[144,512]{1,0:T(8,128)(2,1)S(1)}, bf16[144,512]{1,0:T(8,128)(2,1)S(1)}, u32[]{:S(2)}, u32[]{:S(2)}) collective-permute-start(bf16[144,512]{1,0:T(8,128)(2,1)S(1)} %keys_and_numbers.1.rest_3_), channel_id=1, source_target_pairs={{0,8},{4,12},{8,16},{12,20},{16,24},{20,28},{1,9},{5,13},{9,17},{1... | collective-permute-start | bytes 442376 | tf_op jit(solution)/shard_map/ppermute | solution.py:32
  40.6 0.0 collective-permute-done.5
  40.6 3.7 %collective-permute-done.7.rest_1_ = bf16[144,512]{1,0:T(8,128)(2,1)S(1)} collective-permute-done((bf16[144,512]{1,0:T(8,128)(2,1)S(1)}, bf16[144,512]{1,0:T(8,128)(2,1)S(1)}, u32[]{:S(2)}, u32[]{:S(2)}) %collective-permute-start.7) | collective-permute-done | bytes 147488 | tf_op jit(solution)/shard_map/ppermute | solution.py:32
  44.3 0.0 collective-permute-done.6.refs_2_
  44.3 0.5 fresh_rows.1.first_ref
  44.9 0.0 copy-start.5
  44.9 3.4 %collective-permute-start.8 = (bf16[2,256,256]{2,1,0:T(8,128)(2,1)S(1)}, bf16[2,256,256]{2,1,0:T(8,128)(2,1)S(1)}, u32[]{:S(2)}, u32[]{:S(2)}) collective-permute-start(bf16[2,256,256]{2,1,0:T(8,128)(2,1)S(1)} %fresh_rows.1.first_ref), channel_id=1, source_target_pairs={{0,16},{1,17},{2,18},{3,19},{4,20},{5,21},{6,22},{7,23},{8,24},{9,... | collective-permute-start | bytes 786440 | tf_op jit(solution)/shard_map/ppermute | solution.py:27
  48.2 0.0 collective-permute-start.13
  48.2 3.3 %collective-permute-start.9 = (bf16[144,512]{1,0:T(8,128)(2,1)S(1)}, bf16[144,512]{1,0:T(8,128)(2,1)S(1)}, u32[]{:S(2)}, u32[]{:S(2)}) collective-permute-start(bf16[144,512]{1,0:T(8,128)(2,1)S(1)} %keys_and_numbers.1.rest_3_), channel_id=1, source_target_pairs={{0,4},{4,8},{8,12},{12,16},{16,20},{20,24},{24,28},{1,5},{5,9},{9,... | collective-permute-start | bytes 442376 | tf_op jit(solution)/shard_map/ppermute | solution.py:32
  51.6 3.8 %collective-permute-done.9.rest_2_ = bf16[144,512]{1,0:T(8,128)(2,1)S(1)} collective-permute-done((bf16[144,512]{1,0:T(8,128)(2,1)S(1)}, bf16[144,512]{1,0:T(8,128)(2,1)S(1)}, u32[]{:S(2)}, u32[]{:S(2)}) %collective-permute-start.9) | collective-permute-done | bytes 147488 | tf_op jit(solution)/shard_map/ppermute | solution.py:32
  55.4 0.0 collective-permute-done.10.refs_1_
  55.4 4.0 %collective-permute-done.8.second_ref = bf16[2,256,256]{2,1,0:T(8,128)(2,1)S(1)} collective-permute-done((bf16[2,256,256]{2,1,0:T(8,128)(2,1)S(1)}, bf16[2,256,256]{2,1,0:T(8,128)(2,1)S(1)}, u32[]{:S(2)}, u32[]{:S(2)}) %collective-permute-start.8) | collective-permute-done | bytes 262176 | tf_op jit(solution)/shard_map/ppermute | solution.py:27
  59.5 0.8 collective-permute-start.11
  60.2 4.7 %collective-permute-start.12 = (bf16[512,256]{1,0:T(8,128)(2,1)S(1)}, bf16[512,256]{1,0:T(8,128)(2,1)S(1)}, u32[]{:S(2)}, u32[]{:S(2)}) collective-permute-start(bf16[512,256]{1,0:T(8,128)(2,1)S(1)} %one_below.5.first_ref), channel_id=1, source_target_pairs={{0,4},{1,5},{2,6},{3,7},{4,0},{5,1},{6,2},{7,3},{8,12},{9,13},{10,... | collective-permute-start | bytes 786440 | tf_op jit(solution)/shard_map/ppermute | solution.py:27
  65.0 0.0 collective-permute-done.13.refs_3_
  65.0 1.8 %collective-permute-done.11.second_ref = bf16[512,256]{1,0:T(8,128)(2,1)S(1)} collective-permute-done((bf16[512,256]{1,0:T(8,128)(2,1)S(1)}, bf16[512,256]{1,0:T(8,128)(2,1)S(1)}, u32[]{:S(2)}, u32[]{:S(2)}) %collective-permute-start.11) | collective-permute-done | bytes 262176 | tf_op jit(solution)/shard_map/ppermute | solution.py:27
  66.7 4.4 %collective-permute-done.12.second_ref = bf16[512,256]{1,0:T(8,128)(2,1)S(1)} collective-permute-done((bf16[512,256]{1,0:T(8,128)(2,1)S(1)}, bf16[512,256]{1,0:T(8,128)(2,1)S(1)}, u32[]{:S(2)}, u32[]{:S(2)}) %collective-permute-start.12) | collective-permute-done | bytes 262176 | tf_op jit(solution)/shard_map/ppermute | solution.py:27
  71.3 0.4 collective-permute-start.15
  71.7 1.7 %collective-permute-start.14 = (bf16[1024,256]{1,0:T(8,128)(2,1)S(1)}, bf16[1024,256]{1,0:T(8,128)(2,1)S(1)}, u32[]{:S(2)}, u32[]{:S(2)}) collective-permute-start(bf16[1024,256]{1,0:T(8,128)(2,1)S(1)} %one_below.6.refs_4_), channel_id=1, source_target_pairs={{0,4},{1,5},{2,6},{3,7},{4,0},{5,1},{6,2},{7,3},{8,12},{9,13},{10,... | collective-permute-start | bytes 1572872 | tf_op jit(solution)/shard_map/ppermute | solution.py:27
  74.1 4.2 %attention_weights.1.w_ref = bf16[4,1024,512]{2,1,0:T(8,128)(2,1)S(1)} custom-call(s32[1]{0:T(128)S(6)} %copy.13.used_ref, bf16[1,128,4096]{2,1,0:T(8,128)(2,1)S(1)} %copy-done.5, bf16[144,512]{1,0:T(8,128)(2,1)S(1)} %collective-permute-done.4.rest_0_, bf16[144,512]{1,0:T(8,128)(2,1)S(1)} %collective-permute-done.7.rest_1_, ...), custom_call_target="tpu_custom_call" | custom-call | flops 536870912 | bytes 5242880 | tf_op jit(solution)/shard_map/attention_weights/pallas_call | solution.py:337
  78.3 0.7 projected_first.1.refs_4_
  79.0 5.3 %collective-permute-done.15.refs_6_ = bf16[1024,256]{1,0:T(8,128)(2,1)S(1)} collective-permute-done((bf16[1024,256]{1,0:T(8,128)(2,1)S(1)}, bf16[1024,256]{1,0:T(8,128)(2,1)S(1)}, u32[]{:S(2)}, u32[]{:S(2)}) %collective-permute-start.15) | collective-permute-done | bytes 524320 | tf_op jit(solution)/shard_map/ppermute | solution.py:27
  84.3 0.4 collective-permute-done.14.refs_5_
  84.7 0.7 projected_last.1
  85.5 0.1 collective-permute-start.16
  85.5 1.5 %collective-permute-done.16 = bf16[2,128,512]{2,1,0:T(8,128)(2,1)S(1)} collective-permute-done((bf16[2,128,512]{2,1,0:T(8,128)(2,1)S(1)}, bf16[2,128,512]{2,1,0:T(8,128)(2,1)S(1)}, u32[]{:S(2)}, u32[]{:S(2)}) %collective-permute-start.16) | collective-permute-done | bytes 262176 | tf_op jit(solution)/shard_map/ppermute | solution.py:27
  87.1 0.1 add_bitcast_fusion
  87.2 1.6 %collective-permute-start.17 = (bf16[1,128,512]{2,1,0:T(8,128)(2,1)S(1)}, bf16[1,128,512]{2,1,0:T(8,128)(2,1)S(1)}, u32[]{:S(2)}, u32[]{:S(2)}) collective-permute-start(bf16[1,128,512]{2,1,0:T(8,128)(2,1)S(1)} %fusion.4), channel_id=1, source_target_pairs={{0,2},{1,3},{2,0},{3,1},{4,6},{5,7},{6,4},{7,5},{8,10},{9,11},{10,... | collective-permute-start | bytes 393224 | tf_op jit(solution)/shard_map/ppermute | solution.py:27
  88.8 0.1 add_bitcast_fusion.1
  88.9 3.9 %collective-permute-done.17 = bf16[1,128,512]{2,1,0:T(8,128)(2,1)S(1)} collective-permute-done((bf16[1,128,512]{2,1,0:T(8,128)(2,1)S(1)}, bf16[1,128,512]{2,1,0:T(8,128)(2,1)S(1)}, u32[]{:S(2)}, u32[]{:S(2)}) %collective-permute-start.17) | collective-permute-done | bytes 131104 | tf_op jit(solution)/shard_map/ppermute | solution.py:27
  92.8 3.3 %collective-permute-start.20 = (bf16[128,512]{1,0:T(8,128)(2,1)S(1)}, bf16[128,512]{1,0:T(8,128)(2,1)S(1)}, u32[]{:S(2)}, u32[]{:S(2)}) collective-permute-start(bf16[128,512]{1,0:T(8,128)(2,1)S(1)} %fusion.3.rest_3_), channel_id=1, source_target_pairs={{0,4},{4,8},{8,12},{12,16},{16,20},{20,24},{24,28},{1,5},{5,9},{9,... | collective-permute-start | bytes 393224 | tf_op jit(solution)/shard_map/ppermute | solution.py:32
  96.2 3.3 %collective-permute-start.19 = (bf16[128,512]{1,0:T(8,128)(2,1)S(1)}, bf16[128,512]{1,0:T(8,128)(2,1)S(1)}, u32[]{:S(2)}, u32[]{:S(2)}) collective-permute-start(bf16[128,512]{1,0:T(8,128)(2,1)S(1)} %fusion.3.rest_3_), channel_id=1, source_target_pairs={{0,8},{4,12},{8,16},{12,20},{16,24},{20,28},{1,9},{5,13},{9,17},{1... | collective-permute-start | bytes 393224 | tf_op jit(solution)/shard_map/ppermute | solution.py:32
  99.4 5.4 %collective-permute-start.18 = (bf16[128,512]{1,0:T(8,128)(2,1)S(1)}, bf16[128,512]{1,0:T(8,128)(2,1)S(1)}, u32[]{:S(2)}, u32[]{:S(2)}) collective-permute-start(bf16[128,512]{1,0:T(8,128)(2,1)S(1)} %fusion.3.rest_3_), channel_id=1, source_target_pairs={{0,12},{4,16},{8,20},{12,24},{16,28},{1,13},{5,17},{9,21},{13,25},... | collective-permute-start | bytes 393224 | tf_op jit(solution)/shard_map/ppermute | solution.py:32
  104.8 1.4 %multiply_subtract_fusion = (f32[256,512]{1,0:T(8,128)}, f32[256,512]{1,0:T(8,128)}, f32[256,512]{1,0:T(8,128)}) fusion(f32[256,512]{1,0:T(8,128)S(1)} %copy-done.1, f32[256,256]{1,0:T(8,128)S(1)} %get-tuple-element.99, f32[256,256]{1,0:T(8,128)S(1)} %get-tuple-element.100, f32[256,512]{1,0:T(8,128)S(1)} %copy-done.2, f32[256,512]{1,0:T(8,128)S(1)} %copy-done.3), kind=kLoop, calls=%fused_computation.4 | loop fusion | flops 2097152 | bytes 3670016 | tf_op jit(solution)/shard_map/sub | solution.py:41
  106.2 0.0 collective-permute-done.20.rest_2_
  106.2 0.0 collective-permute-done.19.rest_1_
  106.2 1.1 collective-permute-done.18.rest_0_
  107.3 2.2 %weighted_values.1 = bf16[1,128,4096]{2,1,0:T(8,128)(2,1)} custom-call(bf16[4,1024,512]{2,1,0:T(8,128)(2,1)S(1)} %attention_weights.1.w_ref, bf16[128,512]{1,0:T(8,128)(2,1)S(1)} %collective-permute-done.18.rest_0_, bf16[128,512]{1,0:T(8,128)(2,1)S(1)} %collective-permute-done.19.rest_1_, bf16[128,512]{1,0:T(8,128)(2,1)S(1)} %collective-permute-done.20.rest_2_, ...), custom_call_target="tpu_custom_call" | custom-call | flops 536870912 | bytes 4194304 | tf_op jit(solution)/shard_map/weighted_values/pallas_call | solution.py:374
  (17 shorter events, 0.2 us)
Async XLA Ops:
  0.6 1.6 %copy-start = (bf16[8,256,512]{2,1,0:T(8,128)(2,1)S(1)}, bf16[8,256,512]{2,1,0:T(8,128)(2,1)}, u32[]{:S(2)}) copy-start(bf16[8,256,512]{2,1,0:T(8,128)(2,1)} %terms_ref.3) | copy-start | bytes 6291460
  2.2 4.9 %copy-start.4 = (bf16[1,128,8192]{2,1,0:T(8,128)(2,1)S(1)}, bf16[1,128,8192]{2,1,0:T(8,128)(2,1)}, u32[]{:S(2)}) copy-start(bf16[1,128,8192]{2,1,0:T(8,128)(2,1)} %param.15) | copy-start | bytes 6291460
  2.4 14.9 %collective-permute-start = (bf16[4,256,256]{2,1,0:T(8,128)(2,1)S(1)}, bf16[4,256,256]{2,1,0:T(8,128)(2,1)S(1)}, u32[]{:S(2)}, u32[]{:S(2)}) collective-permute-start(bf16[4,256,256]{2,1,0:T(8,128)(2,1)S(1)} %get-tuple-element.49), channel_id=1, source_target_pairs={{0,4},{1,5},{2,6},{3,7},{4,0},{5,1},{6,2},{7,3},{8,12},{9,13},{10,... | collective-permute-start | bytes 1572872 | tf_op jit(solution)/shard_map/ppermute | solution.py:27
  5.4 2.1 %copy-start.6 = (bf16[1,128,512]{2,1,0:T(8,128)(2,1)S(1)}, bf16[1,128,512]{2,1,0:T(8,128)(2,1)}, u32[]{:S(2)}) copy-start(bf16[1,128,512]{2,1,0:T(8,128)(2,1)} %key_ref.1) | copy-start | bytes 393220
  5.4 2.1 %copy-start.7 = (s32[1,128]{1,0:T(1,128)S(1)}, s32[1,128]{1,0:T(1,128)}, u32[]{:S(2)}) copy-start(s32[1,128]{1,0:T(1,128)} %seg_ref.1) | copy-start | bytes 1540
  5.4 13.4 %collective-permute-start.1 = (bf16[4,256,256]{2,1,0:T(8,128)(2,1)S(1)}, bf16[4,256,256]{2,1,0:T(8,128)(2,1)S(1)}, u32[]{:S(2)}, u32[]{:S(2)}) collective-permute-start(bf16[4,256,256]{2,1,0:T(8,128)(2,1)S(1)} %get-tuple-element.50), channel_id=1, source_target_pairs={{0,8},{1,9},{2,10},{3,11},{4,12},{5,13},{6,14},{7,15},{8,0},{9,1},... | collective-permute-start | bytes 1572872 | tf_op jit(solution)/shard_map/ppermute | solution.py:27
  7.2 18.9 %copy-start.1 = (f32[256,512]{1,0:T(8,128)S(1)}, f32[256,512]{1,0:T(8,128)}, u32[]{:S(2)}) copy-start(f32[256,512]{1,0:T(8,128)} %refs_0_.1) | copy-start | bytes 1572868
  7.2 18.9 %copy-start.2 = (f32[256,512]{1,0:T(8,128)S(1)}, f32[256,512]{1,0:T(8,128)}, u32[]{:S(2)}) copy-start(f32[256,512]{1,0:T(8,128)} %refs_1_.1) | copy-start | bytes 1572868
  7.2 18.9 %copy-start.3 = (f32[256,512]{1,0:T(8,128)S(1)}, f32[256,512]{1,0:T(8,128)}, u32[]{:S(2)}) copy-start(f32[256,512]{1,0:T(8,128)} %refs_2_.1) | copy-start | bytes 1572868
  18.9 9.6 %collective-permute-start.3 = (bf16[2,256,256]{2,1,0:T(8,128)(2,1)S(1)}, bf16[2,256,256]{2,1,0:T(8,128)(2,1)S(1)}, u32[]{:S(2)}, u32[]{:S(2)}) collective-permute-start(bf16[2,256,256]{2,1,0:T(8,128)(2,1)S(1)} %bitcast.26), channel_id=1, source_target_pairs={{0,4},{1,5},{2,6},{3,7},{4,0},{5,1},{6,2},{7,3},{8,12},{9,13},{10,... | collective-permute-start | bytes 786440 | tf_op jit(solution)/shard_map/ppermute | solution.py:27
  19.4 9.1 %collective-permute-start.2 = (bf16[2,256,256]{2,1,0:T(8,128)(2,1)S(1)}, bf16[2,256,256]{2,1,0:T(8,128)(2,1)S(1)}, u32[]{:S(2)}, u32[]{:S(2)}) collective-permute-start(bf16[2,256,256]{2,1,0:T(8,128)(2,1)S(1)} %bitcast.27), channel_id=1, source_target_pairs={{0,8},{1,9},{2,10},{3,11},{4,12},{5,13},{6,14},{7,15},{8,0},{9,1},... | collective-permute-start | bytes 786440 | tf_op jit(solution)/shard_map/ppermute | solution.py:27
  21.2 7.3 %collective-permute-start.4 = (bf16[144,512]{1,0:T(8,128)(2,1)S(1)}, bf16[144,512]{1,0:T(8,128)(2,1)S(1)}, u32[]{:S(2)}, u32[]{:S(2)}) collective-permute-start(bf16[144,512]{1,0:T(8,128)(2,1)S(1)} %keys_and_numbers.1.rest_3_), channel_id=1, source_target_pairs={{0,12},{4,16},{8,20},{12,24},{16,28},{1,13},{5,17},{9,21},{13,25},... | collective-permute-start | bytes 442376 | tf_op jit(solution)/shard_map/ppermute | solution.py:32
  24.4 19.9 %collective-permute-start.6 = (bf16[128,2048]{1,0:T(8,128)(2,1)S(1)}, bf16[128,2048]{1,0:T(8,128)(2,1)S(1)}, u32[]{:S(2)}, u32[]{:S(2)}) collective-permute-start(bf16[128,2048]{1,0:T(8,128)(2,1)S(1)} %get-tuple-element.67), channel_id=1, source_target_pairs={{0,2},{1,3},{2,0},{3,1},{4,6},{5,7},{6,4},{7,5},{8,10},{9,11},{10,... | collective-permute-start | bytes 1572872 | tf_op jit(solution)/shard_map/ppermute | solution.py:27
  28.6 12.0 %collective-permute-start.5 = (bf16[2,1,256,256]{3,2,1,0:T(8,128)(2,1)S(1)}, bf16[2,1,256,256]{3,2,1,0:T(8,128)(2,1)S(1)}, u32[]{:S(2)}, u32[]{:S(2)}) collective-permute-start(bf16[2,1,256,256]{3,2,1,0:T(8,128)(2,1)S(1)} %first_half_sums.5), channel_id=1, source_target_pairs={{0,16},{1,17},{2,18},{3,19},{4,20},{5,21},{6,22},{7,23},{8,24},{9,... | collective-permute-start | bytes 786440 | tf_op jit(solution)/shard_map/ppermute | solution.py:27
  33.0 22.4 %collective-permute-start.10 = (bf16[128,2048]{1,0:T(8,128)(2,1)S(1)}, bf16[128,2048]{1,0:T(8,128)(2,1)S(1)}, u32[]{:S(2)}, u32[]{:S(2)}) collective-permute-start(bf16[128,2048]{1,0:T(8,128)(2,1)S(1)} %get-tuple-element.73), channel_id=1, source_target_pairs={{0,1},{1,0},{2,3},{3,2},{4,5},{5,4},{6,7},{7,6},{8,9},{9,8},{10,11... | collective-permute-start | bytes 1572872 | tf_op jit(solution)/shard_map/ppermute | solution.py:27
  33.0 11.3 %collective-permute-start.7 = (bf16[144,512]{1,0:T(8,128)(2,1)S(1)}, bf16[144,512]{1,0:T(8,128)(2,1)S(1)}, u32[]{:S(2)}, u32[]{:S(2)}) collective-permute-start(bf16[144,512]{1,0:T(8,128)(2,1)S(1)} %keys_and_numbers.1.rest_3_), channel_id=1, source_target_pairs={{0,8},{4,12},{8,16},{12,20},{16,24},{20,28},{1,9},{5,13},{9,17},{1... | collective-permute-start | bytes 442376 | tf_op jit(solution)/shard_map/ppermute | solution.py:32
  44.9 29.2 %copy-start.5 = (bf16[1,128,4096]{2,1,0:T(8,128)(2,1)S(1)}, bf16[1,128,4096]{2,1,0:T(8,128)(2,1)}, u32[]{:S(2)}) copy-start(bf16[1,128,4096]{2,1,0:T(8,128)(2,1)} %q_ref.1) | copy-start | bytes 3145732
  44.9 14.5 %collective-permute-start.8 = (bf16[2,256,256]{2,1,0:T(8,128)(2,1)S(1)}, bf16[2,256,256]{2,1,0:T(8,128)(2,1)S(1)}, u32[]{:S(2)}, u32[]{:S(2)}) collective-permute-start(bf16[2,256,256]{2,1,0:T(8,128)(2,1)S(1)} %fresh_rows.1.first_ref), channel_id=1, source_target_pairs={{0,16},{1,17},{2,18},{3,19},{4,20},{5,21},{6,22},{7,23},{8,24},{9,... | collective-permute-start | bytes 786440 | tf_op jit(solution)/shard_map/ppermute | solution.py:27
  48.2 16.7 %collective-permute-start.13 = (bf16[128,2048]{1,0:T(8,128)(2,1)S(1)}, bf16[128,2048]{1,0:T(8,128)(2,1)S(1)}, u32[]{:S(2)}, u32[]{:S(2)}) collective-permute-start(bf16[128,2048]{1,0:T(8,128)(2,1)S(1)} %get-tuple-element.78), channel_id=1, source_target_pairs={{0,3},{1,2},{2,1},{3,0},{4,7},{5,6},{6,5},{7,4},{8,11},{9,10},{10,... | collective-permute-start | bytes 1572872 | tf_op jit(solution)/shard_map/ppermute | solution.py:27
  48.2 7.2 %collective-permute-start.9 = (bf16[144,512]{1,0:T(8,128)(2,1)S(1)}, bf16[144,512]{1,0:T(8,128)(2,1)S(1)}, u32[]{:S(2)}, u32[]{:S(2)}) collective-permute-start(bf16[144,512]{1,0:T(8,128)(2,1)S(1)} %keys_and_numbers.1.rest_3_), channel_id=1, source_target_pairs={{0,4},{4,8},{8,12},{12,16},{16,20},{20,24},{24,28},{1,5},{5,9},{9,... | collective-permute-start | bytes 442376 | tf_op jit(solution)/shard_map/ppermute | solution.py:32
  59.5 7.3 %collective-permute-start.11 = (bf16[512,256]{1,0:T(8,128)(2,1)S(1)}, bf16[512,256]{1,0:T(8,128)(2,1)S(1)}, u32[]{:S(2)}, u32[]{:S(2)}) collective-permute-start(bf16[512,256]{1,0:T(8,128)(2,1)S(1)} %one_below.4.first_ref), channel_id=1, source_target_pairs={{0,8},{1,9},{2,10},{3,11},{4,12},{5,13},{6,14},{7,15},{8,0},{9,1},... | collective-permute-start | bytes 786440 | tf_op jit(solution)/shard_map/ppermute | solution.py:27
  60.2 10.9 %collective-permute-start.12 = (bf16[512,256]{1,0:T(8,128)(2,1)S(1)}, bf16[512,256]{1,0:T(8,128)(2,1)S(1)}, u32[]{:S(2)}, u32[]{:S(2)}) collective-permute-start(bf16[512,256]{1,0:T(8,128)(2,1)S(1)} %one_below.5.first_ref), channel_id=1, source_target_pairs={{0,4},{1,5},{2,6},{3,7},{4,0},{5,1},{6,2},{7,3},{8,12},{9,13},{10,... | collective-permute-start | bytes 786440 | tf_op jit(solution)/shard_map/ppermute | solution.py:27
  71.3 13.1 %collective-permute-start.15 = (bf16[1024,256]{1,0:T(8,128)(2,1)S(1)}, bf16[1024,256]{1,0:T(8,128)(2,1)S(1)}, u32[]{:S(2)}, u32[]{:S(2)}) collective-permute-start(bf16[1024,256]{1,0:T(8,128)(2,1)S(1)} %one_below.7.refs_5_), channel_id=1, source_target_pairs={{0,8},{1,9},{2,10},{3,11},{4,12},{5,13},{6,14},{7,15},{8,0},{9,1},... | collective-permute-start | bytes 1572872 | tf_op jit(solution)/shard_map/ppermute | solution.py:27
  71.7 13.1 %collective-permute-start.14 = (bf16[1024,256]{1,0:T(8,128)(2,1)S(1)}, bf16[1024,256]{1,0:T(8,128)(2,1)S(1)}, u32[]{:S(2)}, u32[]{:S(2)}) collective-permute-start(bf16[1024,256]{1,0:T(8,128)(2,1)S(1)} %one_below.6.refs_4_), channel_id=1, source_target_pairs={{0,4},{1,5},{2,6},{3,7},{4,0},{5,1},{6,2},{7,3},{8,12},{9,13},{10,... | collective-permute-start | bytes 1572872 | tf_op jit(solution)/shard_map/ppermute | solution.py:27
  85.5 1.6 %collective-permute-start.16 = (bf16[2,128,512]{2,1,0:T(8,128)(2,1)S(1)}, bf16[2,128,512]{2,1,0:T(8,128)(2,1)S(1)}, u32[]{:S(2)}, u32[]{:S(2)}) collective-permute-start(bf16[2,128,512]{2,1,0:T(8,128)(2,1)S(1)} %get-tuple-element.93), channel_id=1, source_target_pairs={{0,1},{1,0},{2,3},{3,2},{4,5},{5,4},{6,7},{7,6},{8,9},{9,8},{10,11... | collective-permute-start | bytes 786440 | tf_op jit(solution)/shard_map/ppermute | solution.py:27
  87.2 5.6 %collective-permute-start.17 = (bf16[1,128,512]{2,1,0:T(8,128)(2,1)S(1)}, bf16[1,128,512]{2,1,0:T(8,128)(2,1)S(1)}, u32[]{:S(2)}, u32[]{:S(2)}) collective-permute-start(bf16[1,128,512]{2,1,0:T(8,128)(2,1)S(1)} %fusion.4), channel_id=1, source_target_pairs={{0,2},{1,3},{2,0},{3,1},{4,6},{5,7},{6,4},{7,5},{8,10},{9,11},{10,... | collective-permute-start | bytes 393224 | tf_op jit(solution)/shard_map/ppermute | solution.py:27
  92.8 13.4 %collective-permute-start.20 = (bf16[128,512]{1,0:T(8,128)(2,1)S(1)}, bf16[128,512]{1,0:T(8,128)(2,1)S(1)}, u32[]{:S(2)}, u32[]{:S(2)}) collective-permute-start(bf16[128,512]{1,0:T(8,128)(2,1)S(1)} %fusion.3.rest_3_), channel_id=1, source_target_pairs={{0,4},{4,8},{8,12},{12,16},{16,20},{20,24},{24,28},{1,5},{5,9},{9,... | collective-permute-start | bytes 393224 | tf_op jit(solution)/shard_map/ppermute | solution.py:32
  96.2 10.1 %collective-permute-start.19 = (bf16[128,512]{1,0:T(8,128)(2,1)S(1)}, bf16[128,512]{1,0:T(8,128)(2,1)S(1)}, u32[]{:S(2)}, u32[]{:S(2)}) collective-permute-start(bf16[128,512]{1,0:T(8,128)(2,1)S(1)} %fusion.3.rest_3_), channel_id=1, source_target_pairs={{0,8},{4,12},{8,16},{12,20},{16,24},{20,28},{1,9},{5,13},{9,17},{1... | collective-permute-start | bytes 393224 | tf_op jit(solution)/shard_map/ppermute | solution.py:32
  99.4 7.9 %collective-permute-start.18 = (bf16[128,512]{1,0:T(8,128)(2,1)S(1)}, bf16[128,512]{1,0:T(8,128)(2,1)S(1)}, u32[]{:S(2)}, u32[]{:S(2)}) collective-permute-start(bf16[128,512]{1,0:T(8,128)(2,1)S(1)} %fusion.3.rest_3_), channel_id=1, source_target_pairs={{0,12},{4,16},{8,20},{12,24},{16,28},{1,13},{5,17},{9,21},{13,25},... | collective-permute-start | bytes 393224 | tf_op jit(solution)/shard_map/ppermute | solution.py:32

commit v4 on v3

--- a/solution.py
+++ b/solution.py
@@ -27,9 +27,17 @@
     return lax.ppermute(block, ALL, [(i, i ^ mask) for i in range(total)])
 
 
-def passed_along(block, distance):
+def preceding(block):
     n_dp = lax.axis_size("dp")
-    return lax.ppermute(block, "dp", [(i, i + distance) for i in range(n_dp - distance)])
+    two_before = lax.ppermute(block, "dp", [(i, i + 2) for i in range(n_dp - 2)])
+    leaps = [(i, i + 1 + 2 * (i % 2)) for i in range(n_dp)]
+    leapt = lax.ppermute(block, "dp", [leap for leap in leaps if leap[1] < n_dp])
+    return [two_before, leapt, swapped(two_before, lax.axis_size("replica"))]
+
+
+def in_order(two_before, leapt, relayed, own):
+    odd = lax.axis_index("dp") % 2 == 1
+    return [jnp.where(odd, relayed, leapt), two_before, jnp.where(odd, leapt, relayed), own]
 
 
 def adam_update(grad_sum, master, moment_first, moment_second):
@@ -119,7 +127,7 @@
     )(*[term for terms in streams for term in terms])
 
 
-def fresh_rows(streams, state):
+def fresh_rows(streams, first_part, state):
     parts = len(streams)
     sizes = [len(terms) for terms in streams]
     _, rows, width = streams[0][0].shape
@@ -133,7 +141,7 @@
                 term = ref[ref.shape[0] - 1].astype(jnp.float32)
                 grad = term if grad is None else grad + term
             at += size
-            cut = slice(part * width, (part + 1) * width)
+            cut = slice((first_part + part) * width, (first_part + part + 1) * width)
             updated = adam_update(grad, master_ref[:, cut], first_ref[:, cut], second_ref[:, cut])
             out_ref[part] = updated[0].astype(jnp.bfloat16)
 
@@ -311,10 +319,9 @@
     def kernel(used_ref, q_ref, *rest):
         key_refs, out_ref = rest[:-1], rest[-1]
         here, used = lax.axis_index("dp"), used_ref[0]
-        keys = jnp.concatenate([ref[0:tokens, :] for ref in key_refs], axis=0)
-        seg_keys = jnp.concatenate(
-            [ref[tokens : tokens + 16, :].astype(jnp.float32)[0:1, :] for ref in key_refs], axis=1
-        )
+        keys = jnp.concatenate(in_order(*[ref[0:tokens, :] for ref in key_refs]), axis=0)
+        numbers = [ref[tokens : tokens + 16, :].astype(jnp.float32)[0:1, :] for ref in key_refs]
+        seg_keys = jnp.concatenate(in_order(*numbers), axis=1)
         row = lax.broadcasted_iota(jnp.int32, (tokens, keys_all), 0)
         offset = lax.broadcasted_iota(jnp.int32, (tokens, keys_all), 1) - (spans - 1) * tokens
         seg_own = jnp.sum(jnp.where(offset == row, seg_keys, 0.0), axis=1, keepdims=True)
@@ -363,7 +370,7 @@
         value_refs, out_ref = rest[:-1], rest[-1]
         for g in range(heads_kv):
             cut = slice(g * HD, (g + 1) * HD)
-            values = jnp.concatenate([ref[:, cut] for ref in value_refs], axis=0)
+            values = jnp.concatenate(in_order(*[ref[:, cut] for ref in value_refs]), axis=0)
             mixed = jnp.dot(w_ref[g], values, preferred_element_type=jnp.float32)
             for j in range(groups):
                 place = (g * groups + j) * HD
@@ -416,58 +423,43 @@
     came[0], came[1], kept[0], kept[1], key_own, *packed = tied(
         came[0], came[1], kept[0], kept[1], key_own, *packed
     )
+    key_blocks = preceding(key_own) + [key_own]
     streams = [[kept[part], came[part]] for part in range(parts)]
     token_blocks = [packed[0]] + [swapped(packed[m], m) for m in range(1, n_replica)]
-    key_blocks = [passed_along(key_own, d) for d in (3, 2, 1)] + [key_own]
     state_here = staged(state)
 
     left = n_dp // 2
     for step in range(1, len(bits)):
-        marks = [order[step] for order in orders]
-        if marks[0] == marks[1]:
-            both = swapped(first_half_sums(streams, left), marks[0] * n_replica)
-            came = [both[part] for part in range(parts)]
-        else:
-            came = [
-                swapped(first_half_sums([terms], left)[0], mark * n_replica)
-                for terms, mark in zip(streams, marks)
-            ]
+        for part in range(parts):
+            mark = orders[part][step] * n_replica
+            came[part] = swapped(first_half_sums([streams[part]], left)[0], mark)
         left = left // 2
         if step == 1:
-            came[0], came[1], key_blocks[0], *state_here = tied(
-                came[0], came[1], key_blocks[0], *state_here
-            )
+            came[0], *state_here = tied(came[0], *state_here)
         if step == 2:
-            came[0], came[1], token_blocks[2], key_blocks[1] = tied(
-                came[0], came[1], token_blocks[2], key_blocks[1]
-            )
+            came[0], token_blocks[2] = tied(came[0], token_blocks[2])
         for part in range(parts):
             streams[part].append(came[part])
 
-    fresh = fresh_rows(streams, state_here)
+    fresh = [fresh_rows([terms], part, state_here)[0] for part, terms in enumerate(streams)]
     grad_total = [
         sum(term[-1].astype(jnp.float32) for term in streams[part]) for part in range(parts)
     ]
-    new_master, new_first, new_second = adam_update(
-        jnp.concatenate(grad_total, axis=1), *state
-    )
+    new_master, new_first, new_second = adam_update(jnp.concatenate(grad_total, axis=1), *state)
     labels = [[0] for _ in orders]
     for step in range(len(bits)):
         marks = [order[-1 - step] for order in orders]
-        if marks[0] == marks[1]:
-            came = swapped(fresh, marks[0] * n_replica)
-            if step == 0:
-                came, key_blocks[2], token_blocks[1] = tied(came, key_blocks[2], token_blocks[1])
-                weights = attention_weights(packed_len, queries, key_blocks)
-            joined = [one_below(fresh, came, part) for part in range(parts)]
-            fresh = jnp.stack(joined) if step + 3 < len(bits) else None
-        else:
-            came = [swapped(joined[part], marks[part] * n_replica) for part in range(parts)]
-            if step == len(bits) - 1:
-                break
-            came[0], came[1], *token_blocks = tied(came[0], came[1], *token_blocks)
-            joined = [one_below(joined[part], came[part]) for part in range(parts)]
-        labels = [own + [label ^ mark for label in own] for own, mark in zip(labels, marks)]
+        came = [swapped(fresh[part], marks[part] * n_replica) for part in range(parts)]
+        if step == 0:
+            came[0], token_blocks[1] = tied(came[0], token_blocks[1])
+        if step == 1:
+            came[0], *token_blocks = tied(came[0], *token_blocks)
+            came[1], *key_blocks = tied(came[1], *key_blocks)
+        if step < len(bits) - 1:
+            fresh = [one_below(fresh[part], came[part]) for part in range(parts)]
+            labels = [own + [label ^ mark for label in own] for own, mark in zip(labels, marks)]
+    weights = attention_weights(packed_len, queries, key_blocks)
+    joined = fresh
     last = [[label ^ mark for label in own] for own, mark in zip(labels, marks)]
     before = projected(token_blocks, list(zip(joined, labels)), rows, None)
     came[0], came[1], weights, before = tied(came[0], came[1], weights, before)
@@ -477,10 +469,11 @@
     partial = partial + came.astype(jnp.float32)
     for bit in bits_of(n_replica)[1:]:
         partial = partial.reshape(-1, 2, tokens, columns)
-        came = swapped(partial[:, 1].astype(jnp.bfloat16), bit)
+        leaving = partial[:, 1].astype(jnp.bfloat16)
+        came = swapped(leaving, bit)
         partial = partial[:, 0] + came.astype(jnp.float32)
     value = partial[0].astype(jnp.bfloat16)
-    value_blocks = [passed_along(value, d) for d in (3, 2, 1)] + [value]
+    value_blocks = preceding(value) + [value]
     attended = weighted_values(weights, value_blocks)
     return (new_master, new_first, new_second, attended)
 

time: 112 us -> 97.9 us (0.87); the launches traced: 110 us -> 97.1 us
  starting transfers between devices: 51.7 us -> 42.5 us
  waiting for transfers between devices: 43.3 us -> 39.9 us
    ppermute x6 -> x4, waiting for transfers between devices: 10.7 us -> 0.61 us  [the longest x2 0.61 us: preceding(): lax.ppermute(block, 'dp', [leap for leap in leaps if leap[1] < n_dp])]
    ppermute x15 -> x19, waiting for transfers between devices: 32.6 us -> 39.3 us  [swapped(): return lax.ppermute(block, ALL, [(i, i ^ mask) for i in range(total)])]
    ppermute x6 -> x4, starting transfers between devices: 26.2 us -> 20.2 us  [the longest x2 13.5 us: preceding(): lax.ppermute(block, 'dp', [(i, i + 2) for i in range(n_dp - 2)])]
    ppermute x15 -> x19, starting transfers between devices: 25.5 us -> 22.3 us  [swapped(): return lax.ppermute(block, ALL, [(i, i ^ mask) for i in range(total)])]
  transfers between devices with their start and end apart: 21 -> 23, of which waited for: 13 -> 13; matrix products, arithmetic and copies ran while one was open for 1% -> 2% of each run, Pallas kernels for 6% -> 7%
where the time goes in v4:
time: 97.9 us; the launch traced here: 97.1 us
  starting transfers between devices  42.5 us (43%)
  waiting for transfers between devices  39.9 us (41%)
  Pallas kernels  9.82 us (10%)
  local copies, waits for them, and re-layouts  1.64 us (2%)
  other arithmetic  1.62 us (2%)
  between operations  1.61 us (2%)
    ppermute x19, waiting for transfers between devices, swapped(): return lax.ppermute(block, ALL, [(i, i ^ mask) for i in range(total)])  39.3 us
    ppermute x19, starting transfers between devices, swapped(): return lax.ppermute(block, ALL, [(i, i ^ mask) for i in range(total)])  22.3 us
    ppermute x2, starting transfers between devices, preceding(): lax.ppermute(block, 'dp', [(i, i + 2) for i in range(n_dp - 2)])  13.5 us
    ppermute x2, starting transfers between devices, preceding(): lax.ppermute(block, 'dp', [leap for leap in leaps if leap[1] < n_dp])  6.68 us
    pallas_call x1, Pallas kernels, attention_weights(): pl.pallas_call(kernel, grid=(heads_kv,), out_shape=jax.ShapeDtypeStruct((...  4.25 us
    pallas_call x1, Pallas kernels, weighted_values(): pl.pallas_call(kernel, out_shape=jax.ShapeDtypeStruct((1, tokens, heads_k...  2.23 us
  transfers between devices with their start and end apart: 23, of which 13 were waited for; matrix products, arithmetic and copies ran while one was open for 2% of the time, Pallas kernels for 7%

profile of v4, /device:TPU:0, one launch (start us, length us, event | category | flops | bytes accessed | tf_op | source)
XLA Modules:
  0.0 97.1 jit_solution(3640235894224807444)
XLA Ops:
  0.6 1.6 %copy-done = bf16[8,256,512]{2,1,0:T(8,128)(2,1)S(1)} copy-done((bf16[8,256,512]{2,1,0:T(8,128)(2,1)S(1)}, bf16[8,256,512]{2,1,0:T(8,128)(2,1)}, u32[]{:S(2)}) %copy-start) | copy-done | bytes 2097176
  2.2 0.2 blocks_taken.2
  2.4 3.0 %collective-permute-start = (bf16[4,256,256]{2,1,0:T(8,128)(2,1)S(1)}, bf16[4,256,256]{2,1,0:T(8,128)(2,1)S(1)}, u32[]{:S(2)}, u32[]{:S(2)}) collective-permute-start(bf16[4,256,256]{2,1,0:T(8,128)(2,1)S(1)} %get-tuple-element.48), channel_id=1, source_target_pairs={{0,4},{1,5},{2,6},{3,7},{4,0},{5,1},{6,2},{7,3},{8,12},{9,13},{10,... | collective-permute-start | bytes 1572872 | tf_op jit(solution)/shard_map/ppermute | solution.py:27
  5.4 1.6 %collective-permute-start.1 = (bf16[4,256,256]{2,1,0:T(8,128)(2,1)S(1)}, bf16[4,256,256]{2,1,0:T(8,128)(2,1)S(1)}, u32[]{:S(2)}, u32[]{:S(2)}) collective-permute-start(bf16[4,256,256]{2,1,0:T(8,128)(2,1)S(1)} %get-tuple-element.49), channel_id=1, source_target_pairs={{0,8},{1,9},{2,10},{3,11},{4,12},{5,13},{6,14},{7,15},{8,0},{9,1},... | collective-permute-start | bytes 1572872 | tf_op jit(solution)/shard_map/ppermute | solution.py:27
  7.0 0.2 blocks_taken.3
  7.2 0.0 copy-start.1
  7.2 0.0 copy-start.2
  7.2 0.0 copy-start.3
  7.2 0.3 pack_hidden.1
  7.5 9.8 %collective-permute-done.refs_1_ = bf16[4,256,256]{2,1,0:T(8,128)(2,1)S(1)} collective-permute-done((bf16[4,256,256]{2,1,0:T(8,128)(2,1)S(1)}, bf16[4,256,256]{2,1,0:T(8,128)(2,1)S(1)}, u32[]{:S(2)}, u32[]{:S(2)}) %collective-permute-start) | collective-permute-done | bytes 524320 | tf_op jit(solution)/shard_map/ppermute | solution.py:27
  17.3 1.5 %collective-permute-done.1.refs_1_ = bf16[4,256,256]{2,1,0:T(8,128)(2,1)S(1)} collective-permute-done((bf16[4,256,256]{2,1,0:T(8,128)(2,1)S(1)}, bf16[4,256,256]{2,1,0:T(8,128)(2,1)S(1)}, u32[]{:S(2)}, u32[]{:S(2)}) %collective-permute-start.1) | collective-permute-done | bytes 524320 | tf_op jit(solution)/shard_map/ppermute | solution.py:27
  18.8 1.5 %collective-permute-start.4 = (bf16[128,2048]{1,0:T(8,128)(2,1)S(1)}, bf16[128,2048]{1,0:T(8,128)(2,1)S(1)}, u32[]{:S(2)}, u32[]{:S(2)}) collective-permute-start(bf16[128,2048]{1,0:T(8,128)(2,1)S(1)} %get-tuple-element.62), channel_id=1, source_target_pairs={{0,2},{1,3},{2,0},{3,1},{4,6},{5,7},{6,4},{7,5},{8,10},{9,11},{10,... | collective-permute-start | bytes 1572872 | tf_op jit(solution)/shard_map/ppermute | solution.py:27
  20.3 0.1 first_half_sums.6
  20.4 0.6 collective-permute-start.5
  21.0 0.1 first_half_sums.4
  21.0 1.6 %collective-permute-start.2 = (bf16[2,256,256]{2,1,0:T(8,128)(2,1)S(1)}, bf16[2,256,256]{2,1,0:T(8,128)(2,1)S(1)}, u32[]{:S(2)}, u32[]{:S(2)}) collective-permute-start(bf16[2,256,256]{2,1,0:T(8,128)(2,1)S(1)} %bitcast.30), channel_id=1, source_target_pairs={{0,8},{1,9},{2,10},{3,11},{4,12},{5,13},{6,14},{7,15},{8,0},{9,1},... | collective-permute-start | bytes 786440 | tf_op jit(solution)/shard_map/ppermute | solution.py:27
  22.7 0.0 collective-permute-start.8
  22.7 0.4 staged.1
  23.1 3.9 %collective-permute-done.5.refs_2_ = bf16[2,256,256]{2,1,0:T(8,128)(2,1)S(1)} collective-permute-done((bf16[2,256,256]{2,1,0:T(8,128)(2,1)S(1)}, bf16[2,256,256]{2,1,0:T(8,128)(2,1)S(1)}, u32[]{:S(2)}, u32[]{:S(2)}) %collective-permute-start.5) | collective-permute-done | bytes 262176 | tf_op jit(solution)/shard_map/ppermute | solution.py:27
  27.0 0.1 first_half_sums.7
  27.1 2.7 %collective-permute-start.6 = (bf16[1,256,256]{2,1,0:T(8,128)(2,1)S(1)}, bf16[1,256,256]{2,1,0:T(8,128)(2,1)S(1)}, u32[]{:S(2)}, u32[]{:S(2)}) collective-permute-start(bf16[1,256,256]{2,1,0:T(8,128)(2,1)S(1)} %bitcast.32), channel_id=1, source_target_pairs={{0,16},{1,17},{2,18},{3,19},{4,20},{5,21},{6,22},{7,23},{8,24},{9,... | collective-permute-start | bytes 393224 | tf_op jit(solution)/shard_map/ppermute | solution.py:27
  29.7 0.0 collective-permute-done.2.refs_2_
  29.7 0.1 first_half_sums.5
  29.8 0.8 collective-permute-start.3
  30.5 0.0 collective-permute-start.10
  30.5 8.1 %collective-permute-done.6.refs_3_ = bf16[1,256,256]{2,1,0:T(8,128)(2,1)S(1)} collective-permute-done((bf16[1,256,256]{2,1,0:T(8,128)(2,1)S(1)}, bf16[1,256,256]{2,1,0:T(8,128)(2,1)S(1)}, u32[]{:S(2)}, u32[]{:S(2)}) %collective-permute-start.6) | collective-permute-done | bytes 131104 | tf_op jit(solution)/shard_map/ppermute | solution.py:27
  38.6 0.3 fresh_rows.3
  38.9 0.1 collective-permute-start.12
  39.0 1.8 %collective-permute-done.3.refs_3_ = bf16[1,256,256]{2,1,0:T(8,128)(2,1)S(1)} collective-permute-done((bf16[1,256,256]{2,1,0:T(8,128)(2,1)S(1)}, bf16[1,256,256]{2,1,0:T(8,128)(2,1)S(1)}, u32[]{:S(2)}, u32[]{:S(2)}) %collective-permute-start.3) | collective-permute-done | bytes 131104 | tf_op jit(solution)/shard_map/ppermute | solution.py:27
  40.7 0.0 collective-permute-done.4.refs_2_
  40.7 0.3 fresh_rows.2
  41.0 0.0 copy-start.5
  41.0 1.2 %collective-permute-start.7 = (bf16[256,256]{1,0:T(8,128)(2,1)S(1)}, bf16[256,256]{1,0:T(8,128)(2,1)S(1)}, u32[]{:S(2)}, u32[]{:S(2)}) collective-permute-start(bf16[256,256]{1,0:T(8,128)(2,1)S(1)} %bitcast.26), channel_id=1, source_target_pairs={{0,16},{1,17},{2,18},{3,19},{4,20},{5,21},{6,22},{7,23},{8,24},{9,... | collective-permute-start | bytes 393224 | tf_op jit(solution)/shard_map/ppermute | solution.py:27
  42.2 9.9 %collective-permute-start.14 = (bf16[144,512]{1,0:T(8,128)(2,1)S(1)}, bf16[144,512]{1,0:T(8,128)(2,1)S(1)}, u32[]{:S(2)}, u32[]{:S(2)}) collective-permute-start(bf16[144,512]{1,0:T(8,128)(2,1)S(1)} %keys_and_numbers.1.rest_3_), channel_id=1, source_target_pairs={{0,8},{4,12},{8,16},{12,20},{16,24},{20,28},{1,9},{5,13},{9,17},{1... | collective-permute-start | bytes 442376 | tf_op jit(solution)/shard_map/ppermute | solution.py:32
  52.1 0.0 collective-permute-done.12.second_ref
  52.2 0.1 collective-permute-start.13
  52.2 0.0 collective-permute-done.7.second_ref
  52.3 1.0 collective-permute-start.9
  53.2 3.0 %collective-permute-start.15 = (bf16[144,512]{1,0:T(8,128)(2,1)S(1)}, bf16[144,512]{1,0:T(8,128)(2,1)S(1)}, u32[]{:S(2)}, u32[]{:S(2)}) collective-permute-start(bf16[144,512]{1,0:T(8,128)(2,1)S(1)} %keys_and_numbers.1.rest_3_), channel_id=1, source_target_pairs={{0,4},{4,16},{8,12},{12,24},{16,20},{24,28},{1,5},{5,17},{9,13},{1... | collective-permute-start | bytes 442376 | tf_op jit(solution)/shard_map/ppermute | solution.py:34
  56.3 3.5 %collective-permute-start.16 = (bf16[144,512]{1,0:T(8,128)(2,1)S(1)}, bf16[144,512]{1,0:T(8,128)(2,1)S(1)}, u32[]{:S(2)}, u32[]{:S(2)}) collective-permute-start(bf16[144,512]{1,0:T(8,128)(2,1)S(1)} %collective-permute-done.14.rest_0_), channel_id=1, source_target_pairs={{0,4},{1,5},{2,6},{3,7},{4,0},{5,1},{6,2},{7,3},{8,12},{9,13},{10,... | collective-permute-start | bytes 442376 | tf_op jit(solution)/shard_map/ppermute | solution.py:27
  59.7 0.3 collective-permute-done.15.rest_1_
  60.1 2.8 %collective-permute-done.16.rest_2_ = bf16[144,512]{1,0:T(8,128)(2,1)S(1)} collective-permute-done((bf16[144,512]{1,0:T(8,128)(2,1)S(1)}, bf16[144,512]{1,0:T(8,128)(2,1)S(1)}, u32[]{:S(2)}, u32[]{:S(2)}) %collective-permute-start.16) | collective-permute-done | bytes 147488 | tf_op jit(solution)/shard_map/ppermute | solution.py:27
  62.9 0.0 collective-permute-done.13.second_ref
  62.9 0.7 collective-permute-start.17
  63.6 1.5 %collective-permute-start.11 = (bf16[1024,256]{1,0:T(8,128)(2,1)S(1)}, bf16[1024,256]{1,0:T(8,128)(2,1)S(1)}, u32[]{:S(2)}, u32[]{:S(2)}) collective-permute-start(bf16[1024,256]{1,0:T(8,128)(2,1)S(1)} %one_below.5.refs_4_), channel_id=1, source_target_pairs={{0,4},{1,5},{2,6},{3,7},{4,0},{5,1},{6,2},{7,3},{8,12},{9,13},{10,... | collective-permute-start | bytes 1572872 | tf_op jit(solution)/shard_map/ppermute | solution.py:27
  65.9 4.2 %attention_weights.1.w_ref = bf16[4,1024,512]{2,1,0:T(8,128)(2,1)S(1)} custom-call(s32[1]{0:T(128)S(6)} %copy.13.used_ref, bf16[1,128,4096]{2,1,0:T(8,128)(2,1)S(1)} %copy-done.5, bf16[144,512]{1,0:T(8,128)(2,1)S(1)} %collective-permute-done.14.rest_0_, bf16[144,512]{1,0:T(8,128)(2,1)S(1)} %collective-permute-done.15.rest_1_, ...), custom_call_target="tpu_custom_call" | custom-call | flops 536870912 | bytes 5242880 | tf_op jit(solution)/shard_map/attention_weights/pallas_call | solution.py:344
  70.1 0.7 projected_first.1.refs_4_
  70.8 3.3 %collective-permute-done.17.refs_6_ = bf16[1024,256]{1,0:T(8,128)(2,1)S(1)} collective-permute-done((bf16[1024,256]{1,0:T(8,128)(2,1)S(1)}, bf16[1024,256]{1,0:T(8,128)(2,1)S(1)}, u32[]{:S(2)}, u32[]{:S(2)}) %collective-permute-start.17) | collective-permute-done | bytes 524320 | tf_op jit(solution)/shard_map/ppermute | solution.py:27
  74.2 0.2 collective-permute-done.11.refs_5_
  74.4 0.7 projected_last.1
  75.1 0.1 collective-permute-start.18
  75.2 1.5 %collective-permute-done.18 = bf16[2,128,512]{2,1,0:T(8,128)(2,1)S(1)} collective-permute-done((bf16[2,128,512]{2,1,0:T(8,128)(2,1)S(1)}, bf16[2,128,512]{2,1,0:T(8,128)(2,1)S(1)}, u32[]{:S(2)}, u32[]{:S(2)}) %collective-permute-start.18) | collective-permute-done | bytes 262176 | tf_op jit(solution)/shard_map/ppermute | solution.py:27
  76.7 0.1 add_bitcast_fusion
  76.8 0.6 collective-permute-start.19
  77.4 0.1 add_bitcast_fusion.1
  77.4 5.0 %collective-permute-done.19 = bf16[1,128,512]{2,1,0:T(8,128)(2,1)S(1)} collective-permute-done((bf16[1,128,512]{2,1,0:T(8,128)(2,1)S(1)}, bf16[1,128,512]{2,1,0:T(8,128)(2,1)S(1)}, u32[]{:S(2)}, u32[]{:S(2)}) %collective-permute-start.19) | collective-permute-done | bytes 131104 | tf_op jit(solution)/shard_map/ppermute | solution.py:27
  82.4 3.6 %collective-permute-start.20 = (bf16[128,512]{1,0:T(8,128)(2,1)S(1)}, bf16[128,512]{1,0:T(8,128)(2,1)S(1)}, u32[]{:S(2)}, u32[]{:S(2)}) collective-permute-start(bf16[128,512]{1,0:T(8,128)(2,1)S(1)} %fusion.3.rest_3_), channel_id=1, source_target_pairs={{0,8},{4,12},{8,16},{12,20},{16,24},{20,28},{1,9},{5,13},{9,17},{1... | collective-permute-start | bytes 393224 | tf_op jit(solution)/shard_map/ppermute | solution.py:32
  86.1 0.1 add_bitcast_fusion.2
  86.1 3.7 %collective-permute-start.21 = (bf16[128,512]{1,0:T(8,128)(2,1)S(1)}, bf16[128,512]{1,0:T(8,128)(2,1)S(1)}, u32[]{:S(2)}, u32[]{:S(2)}) collective-permute-start(bf16[128,512]{1,0:T(8,128)(2,1)S(1)} %fusion.3.rest_3_), channel_id=1, source_target_pairs={{0,4},{4,16},{8,12},{12,24},{16,20},{24,28},{1,5},{5,17},{9,13},{1... | collective-permute-start | bytes 393224 | tf_op jit(solution)/shard_map/ppermute | solution.py:34
  89.8 1.9 %collective-permute-start.22 = (bf16[128,512]{1,0:T(8,128)(2,1)S(1)}, bf16[128,512]{1,0:T(8,128)(2,1)S(1)}, u32[]{:S(2)}, u32[]{:S(2)}) collective-permute-start(bf16[128,512]{1,0:T(8,128)(2,1)S(1)} %collective-permute-done.20.rest_0_), channel_id=1, source_target_pairs={{0,4},{1,5},{2,6},{3,7},{4,0},{5,1},{6,2},{7,3},{8,12},{9,13},{10,... | collective-permute-start | bytes 393224 | tf_op jit(solution)/shard_map/ppermute | solution.py:27
  91.7 1.4 %multiply_subtract_fusion = (f32[256,512]{1,0:T(8,128)}, f32[256,512]{1,0:T(8,128)}, f32[256,512]{1,0:T(8,128)}) fusion(f32[256,512]{1,0:T(8,128)S(1)} %copy-done.1, f32[256,256]{1,0:T(8,128)S(1)} %add_bitcast_fusion.1, f32[256,256]{1,0:T(8,128)S(1)} %add_bitcast_fusion.2, f32[256,512]{1,0:T(8,128)S(1)} %copy-done.2, f32[256,512]{1,0:T(8,128)S(1)} %copy-done.3), kind=kLoop, calls=%fused_computation.4 | loop fusion | flops 2097152 | bytes 3670016 | tf_op jit(solution)/shard_map/sub | solution.py:49
  93.1 0.3 collective-permute-done.21.rest_1_
  93.3 1.5 %collective-permute-done.22.rest_2_ = bf16[128,512]{1,0:T(8,128)(2,1)S(1)} collective-permute-done((bf16[128,512]{1,0:T(8,128)(2,1)S(1)}, bf16[128,512]{1,0:T(8,128)(2,1)S(1)}, u32[]{:S(2)}, u32[]{:S(2)}) %collective-permute-start.22) | collective-permute-done | bytes 131104 | tf_op jit(solution)/shard_map/ppermute | solution.py:27
  94.8 2.2 %weighted_values.1 = bf16[1,128,4096]{2,1,0:T(8,128)(2,1)} custom-call(bf16[4,1024,512]{2,1,0:T(8,128)(2,1)S(1)} %attention_weights.1.w_ref, bf16[128,512]{1,0:T(8,128)(2,1)S(1)} %collective-permute-done.20.rest_0_, bf16[128,512]{1,0:T(8,128)(2,1)S(1)} %collective-permute-done.21.rest_1_, bf16[128,512]{1,0:T(8,128)(2,1)S(1)} %collective-permute-done.22.rest_2_, ...), custom_call_target="tpu_custom_call" | custom-call | flops 536870912 | bytes 4194304 | tf_op jit(solution)/shard_map/weighted_values/pallas_call | solution.py:381
  (23 shorter events, 0.2 us)
Async XLA Ops:
  0.6 1.6 %copy-start = (bf16[8,256,512]{2,1,0:T(8,128)(2,1)S(1)}, bf16[8,256,512]{2,1,0:T(8,128)(2,1)}, u32[]{:S(2)}) copy-start(bf16[8,256,512]{2,1,0:T(8,128)(2,1)} %terms_ref.3) | copy-start | bytes 6291460
  2.2 4.9 %copy-start.4 = (bf16[1,128,8192]{2,1,0:T(8,128)(2,1)S(1)}, bf16[1,128,8192]{2,1,0:T(8,128)(2,1)}, u32[]{:S(2)}) copy-start(bf16[1,128,8192]{2,1,0:T(8,128)(2,1)} %param.15) | copy-start | bytes 6291460
  2.4 14.9 %collective-permute-start = (bf16[4,256,256]{2,1,0:T(8,128)(2,1)S(1)}, bf16[4,256,256]{2,1,0:T(8,128)(2,1)S(1)}, u32[]{:S(2)}, u32[]{:S(2)}) collective-permute-start(bf16[4,256,256]{2,1,0:T(8,128)(2,1)S(1)} %get-tuple-element.48), channel_id=1, source_target_pairs={{0,4},{1,5},{2,6},{3,7},{4,0},{5,1},{6,2},{7,3},{8,12},{9,13},{10,... | collective-permute-start | bytes 1572872 | tf_op jit(solution)/shard_map/ppermute | solution.py:27
  5.4 2.1 %copy-start.6 = (bf16[1,128,512]{2,1,0:T(8,128)(2,1)S(1)}, bf16[1,128,512]{2,1,0:T(8,128)(2,1)}, u32[]{:S(2)}) copy-start(bf16[1,128,512]{2,1,0:T(8,128)(2,1)} %key_ref.1) | copy-start | bytes 393220
  5.4 2.1 %copy-start.7 = (s32[1,128]{1,0:T(1,128)S(1)}, s32[1,128]{1,0:T(1,128)}, u32[]{:S(2)}) copy-start(s32[1,128]{1,0:T(1,128)} %seg_ref.1) | copy-start | bytes 1540
  5.4 13.4 %collective-permute-start.1 = (bf16[4,256,256]{2,1,0:T(8,128)(2,1)S(1)}, bf16[4,256,256]{2,1,0:T(8,128)(2,1)S(1)}, u32[]{:S(2)}, u32[]{:S(2)}) collective-permute-start(bf16[4,256,256]{2,1,0:T(8,128)(2,1)S(1)} %get-tuple-element.49), channel_id=1, source_target_pairs={{0,8},{1,9},{2,10},{3,11},{4,12},{5,13},{6,14},{7,15},{8,0},{9,1},... | collective-permute-start | bytes 1572872 | tf_op jit(solution)/shard_map/ppermute | solution.py:27
  7.2 15.5 %copy-start.1 = (f32[256,512]{1,0:T(8,128)S(1)}, f32[256,512]{1,0:T(8,128)}, u32[]{:S(2)}) copy-start(f32[256,512]{1,0:T(8,128)} %refs_0_.1) | copy-start | bytes 1572868
  7.2 15.5 %copy-start.2 = (f32[256,512]{1,0:T(8,128)S(1)}, f32[256,512]{1,0:T(8,128)}, u32[]{:S(2)}) copy-start(f32[256,512]{1,0:T(8,128)} %refs_1_.1) | copy-start | bytes 1572868
  7.2 15.5 %copy-start.3 = (f32[256,512]{1,0:T(8,128)S(1)}, f32[256,512]{1,0:T(8,128)}, u32[]{:S(2)}) copy-start(f32[256,512]{1,0:T(8,128)} %refs_2_.1) | copy-start | bytes 1572868
  18.8 22.0 %collective-permute-start.4 = (bf16[128,2048]{1,0:T(8,128)(2,1)S(1)}, bf16[128,2048]{1,0:T(8,128)(2,1)S(1)}, u32[]{:S(2)}, u32[]{:S(2)}) collective-permute-start(bf16[128,2048]{1,0:T(8,128)(2,1)S(1)} %get-tuple-element.62), channel_id=1, source_target_pairs={{0,2},{1,3},{2,0},{3,1},{4,6},{5,7},{6,4},{7,5},{8,10},{9,11},{10,... | collective-permute-start | bytes 1572872 | tf_op jit(solution)/shard_map/ppermute | solution.py:27
  20.4 6.6 %collective-permute-start.5 = (bf16[2,256,256]{2,1,0:T(8,128)(2,1)S(1)}, bf16[2,256,256]{2,1,0:T(8,128)(2,1)S(1)}, u32[]{:S(2)}, u32[]{:S(2)}) collective-permute-start(bf16[2,256,256]{2,1,0:T(8,128)(2,1)S(1)} %bitcast.31), channel_id=1, source_target_pairs={{0,4},{1,5},{2,6},{3,7},{4,0},{5,1},{6,2},{7,3},{8,12},{9,13},{10,... | collective-permute-start | bytes 786440 | tf_op jit(solution)/shard_map/ppermute | solution.py:27
  21.0 8.7 %collective-permute-start.2 = (bf16[2,256,256]{2,1,0:T(8,128)(2,1)S(1)}, bf16[2,256,256]{2,1,0:T(8,128)(2,1)S(1)}, u32[]{:S(2)}, u32[]{:S(2)}) collective-permute-start(bf16[2,256,256]{2,1,0:T(8,128)(2,1)S(1)} %bitcast.30), channel_id=1, source_target_pairs={{0,8},{1,9},{2,10},{3,11},{4,12},{5,13},{6,14},{7,15},{8,0},{9,1},... | collective-permute-start | bytes 786440 | tf_op jit(solution)/shard_map/ppermute | solution.py:27
  22.7 29.6 %collective-permute-start.8 = (bf16[128,2048]{1,0:T(8,128)(2,1)S(1)}, bf16[128,2048]{1,0:T(8,128)(2,1)S(1)}, u32[]{:S(2)}, u32[]{:S(2)}) collective-permute-start(bf16[128,2048]{1,0:T(8,128)(2,1)S(1)} %get-tuple-element.69), channel_id=1, source_target_pairs={{0,1},{1,0},{2,3},{3,2},{4,5},{5,4},{6,7},{7,6},{8,9},{9,8},{10,11... | collective-permute-start | bytes 1572872 | tf_op jit(solution)/shard_map/ppermute | solution.py:27
  27.1 11.5 %collective-permute-start.6 = (bf16[1,256,256]{2,1,0:T(8,128)(2,1)S(1)}, bf16[1,256,256]{2,1,0:T(8,128)(2,1)S(1)}, u32[]{:S(2)}, u32[]{:S(2)}) collective-permute-start(bf16[1,256,256]{2,1,0:T(8,128)(2,1)S(1)} %bitcast.32), channel_id=1, source_target_pairs={{0,16},{1,17},{2,18},{3,19},{4,20},{5,21},{6,22},{7,23},{8,24},{9,... | collective-permute-start | bytes 393224 | tf_op jit(solution)/shard_map/ppermute | solution.py:27
  29.8 11.0 %collective-permute-start.3 = (bf16[1,256,256]{2,1,0:T(8,128)(2,1)S(1)}, bf16[1,256,256]{2,1,0:T(8,128)(2,1)S(1)}, u32[]{:S(2)}, u32[]{:S(2)}) collective-permute-start(bf16[1,256,256]{2,1,0:T(8,128)(2,1)S(1)} %bitcast.33), channel_id=1, source_target_pairs={{0,16},{1,17},{2,18},{3,19},{4,20},{5,21},{6,22},{7,23},{8,24},{9,... | collective-permute-start | bytes 393224 | tf_op jit(solution)/shard_map/ppermute | solution.py:27
  30.5 33.1 %collective-permute-start.10 = (bf16[128,2048]{1,0:T(8,128)(2,1)S(1)}, bf16[128,2048]{1,0:T(8,128)(2,1)S(1)}, u32[]{:S(2)}, u32[]{:S(2)}) collective-permute-start(bf16[128,2048]{1,0:T(8,128)(2,1)S(1)} %get-tuple-element.74), channel_id=1, source_target_pairs={{0,3},{1,2},{2,1},{3,0},{4,7},{5,6},{6,5},{7,4},{8,11},{9,10},{10,... | collective-permute-start | bytes 1572872 | tf_op jit(solution)/shard_map/ppermute | solution.py:27
  38.9 13.2 %collective-permute-start.12 = (bf16[256,256]{1,0:T(8,128)(2,1)S(1)}, bf16[256,256]{1,0:T(8,128)(2,1)S(1)}, u32[]{:S(2)}, u32[]{:S(2)}) collective-permute-start(bf16[256,256]{1,0:T(8,128)(2,1)S(1)} %bitcast.28), channel_id=1, source_target_pairs={{0,16},{1,17},{2,18},{3,19},{4,20},{5,21},{6,22},{7,23},{8,24},{9,... | collective-permute-start | bytes 393224 | tf_op jit(solution)/shard_map/ppermute | solution.py:27
  41.0 24.8 %copy-start.5 = (bf16[1,128,4096]{2,1,0:T(8,128)(2,1)S(1)}, bf16[1,128,4096]{2,1,0:T(8,128)(2,1)}, u32[]{:S(2)}) copy-start(bf16[1,128,4096]{2,1,0:T(8,128)(2,1)} %q_ref.1) | copy-start | bytes 3145732
  41.0 11.2 %collective-permute-start.7 = (bf16[256,256]{1,0:T(8,128)(2,1)S(1)}, bf16[256,256]{1,0:T(8,128)(2,1)S(1)}, u32[]{:S(2)}, u32[]{:S(2)}) collective-permute-start(bf16[256,256]{1,0:T(8,128)(2,1)S(1)} %bitcast.26), channel_id=1, source_target_pairs={{0,16},{1,17},{2,18},{3,19},{4,20},{5,21},{6,22},{7,23},{8,24},{9,... | collective-permute-start | bytes 393224 | tf_op jit(solution)/shard_map/ppermute | solution.py:27
  42.2 14.0 %collective-permute-start.14 = (bf16[144,512]{1,0:T(8,128)(2,1)S(1)}, bf16[144,512]{1,0:T(8,128)(2,1)S(1)}, u32[]{:S(2)}, u32[]{:S(2)}) collective-permute-start(bf16[144,512]{1,0:T(8,128)(2,1)S(1)} %keys_and_numbers.1.rest_3_), channel_id=1, source_target_pairs={{0,8},{4,12},{8,16},{12,20},{16,24},{20,28},{1,9},{5,13},{9,17},{1... | collective-permute-start | bytes 442376 | tf_op jit(solution)/shard_map/ppermute | solution.py:32
  52.2 10.7 %collective-permute-start.13 = (bf16[512,256]{1,0:T(8,128)(2,1)S(1)}, bf16[512,256]{1,0:T(8,128)(2,1)S(1)}, u32[]{:S(2)}, u32[]{:S(2)}) collective-permute-start(bf16[512,256]{1,0:T(8,128)(2,1)S(1)} %one_below.6.first_ref), channel_id=1, source_target_pairs={{0,4},{1,5},{2,6},{3,7},{4,0},{5,1},{6,2},{7,3},{8,12},{9,13},{10,... | collective-permute-start | bytes 786440 | tf_op jit(solution)/shard_map/ppermute | solution.py:27
  52.3 11.3 %collective-permute-start.9 = (bf16[512,256]{1,0:T(8,128)(2,1)S(1)}, bf16[512,256]{1,0:T(8,128)(2,1)S(1)}, u32[]{:S(2)}, u32[]{:S(2)}) collective-permute-start(bf16[512,256]{1,0:T(8,128)(2,1)S(1)} %one_below.4.first_ref), channel_id=1, source_target_pairs={{0,8},{1,9},{2,10},{3,11},{4,12},{5,13},{6,14},{7,15},{8,0},{9,1},... | collective-permute-start | bytes 786440 | tf_op jit(solution)/shard_map/ppermute | solution.py:27
  53.2 6.8 %collective-permute-start.15 = (bf16[144,512]{1,0:T(8,128)(2,1)S(1)}, bf16[144,512]{1,0:T(8,128)(2,1)S(1)}, u32[]{:S(2)}, u32[]{:S(2)}) collective-permute-start(bf16[144,512]{1,0:T(8,128)(2,1)S(1)} %keys_and_numbers.1.rest_3_), channel_id=1, source_target_pairs={{0,4},{4,16},{8,12},{12,24},{16,20},{24,28},{1,5},{5,17},{9,13},{1... | collective-permute-start | bytes 442376 | tf_op jit(solution)/shard_map/ppermute | solution.py:34
  56.3 6.6 %collective-permute-start.16 = (bf16[144,512]{1,0:T(8,128)(2,1)S(1)}, bf16[144,512]{1,0:T(8,128)(2,1)S(1)}, u32[]{:S(2)}, u32[]{:S(2)}) collective-permute-start(bf16[144,512]{1,0:T(8,128)(2,1)S(1)} %collective-permute-done.14.rest_0_), channel_id=1, source_target_pairs={{0,4},{1,5},{2,6},{3,7},{4,0},{5,1},{6,2},{7,3},{8,12},{9,13},{10,... | collective-permute-start | bytes 442376 | tf_op jit(solution)/shard_map/ppermute | solution.py:27
  62.9 11.3 %collective-permute-start.17 = (bf16[1024,256]{1,0:T(8,128)(2,1)S(1)}, bf16[1024,256]{1,0:T(8,128)(2,1)S(1)}, u32[]{:S(2)}, u32[]{:S(2)}) collective-permute-start(bf16[1024,256]{1,0:T(8,128)(2,1)S(1)} %one_below.7.refs_5_), channel_id=1, source_target_pairs={{0,8},{1,9},{2,10},{3,11},{4,12},{5,13},{6,14},{7,15},{8,0},{9,1},... | collective-permute-start | bytes 1572872 | tf_op jit(solution)/shard_map/ppermute | solution.py:27
  63.6 10.7 %collective-permute-start.11 = (bf16[1024,256]{1,0:T(8,128)(2,1)S(1)}, bf16[1024,256]{1,0:T(8,128)(2,1)S(1)}, u32[]{:S(2)}, u32[]{:S(2)}) collective-permute-start(bf16[1024,256]{1,0:T(8,128)(2,1)S(1)} %one_below.5.refs_4_), channel_id=1, source_target_pairs={{0,4},{1,5},{2,6},{3,7},{4,0},{5,1},{6,2},{7,3},{8,12},{9,13},{10,... | collective-permute-start | bytes 1572872 | tf_op jit(solution)/shard_map/ppermute | solution.py:27
  75.1 1.6 %collective-permute-start.18 = (bf16[2,128,512]{2,1,0:T(8,128)(2,1)S(1)}, bf16[2,128,512]{2,1,0:T(8,128)(2,1)S(1)}, u32[]{:S(2)}, u32[]{:S(2)}) collective-permute-start(bf16[2,128,512]{2,1,0:T(8,128)(2,1)S(1)} %get-tuple-element.91), channel_id=1, source_target_pairs={{0,1},{1,0},{2,3},{3,2},{4,5},{5,4},{6,7},{7,6},{8,9},{9,8},{10,11... | collective-permute-start | bytes 786440 | tf_op jit(solution)/shard_map/ppermute | solution.py:27
  76.8 5.6 %collective-permute-start.19 = (bf16[1,128,512]{2,1,0:T(8,128)(2,1)S(1)}, bf16[1,128,512]{2,1,0:T(8,128)(2,1)S(1)}, u32[]{:S(2)}, u32[]{:S(2)}) collective-permute-start(bf16[1,128,512]{2,1,0:T(8,128)(2,1)S(1)} %fusion.4), channel_id=1, source_target_pairs={{0,2},{1,3},{2,0},{3,1},{4,6},{5,7},{6,4},{7,5},{8,10},{9,11},{10,... | collective-permute-start | bytes 393224 | tf_op jit(solution)/shard_map/ppermute | solution.py:27
  82.4 7.4 %collective-permute-start.20 = (bf16[128,512]{1,0:T(8,128)(2,1)S(1)}, bf16[128,512]{1,0:T(8,128)(2,1)S(1)}, u32[]{:S(2)}, u32[]{:S(2)}) collective-permute-start(bf16[128,512]{1,0:T(8,128)(2,1)S(1)} %fusion.3.rest_3_), channel_id=1, source_target_pairs={{0,8},{4,12},{8,16},{12,20},{16,24},{20,28},{1,9},{5,13},{9,17},{1... | collective-permute-start | bytes 393224 | tf_op jit(solution)/shard_map/ppermute | solution.py:32
  86.1 7.2 %collective-permute-start.21 = (bf16[128,512]{1,0:T(8,128)(2,1)S(1)}, bf16[128,512]{1,0:T(8,128)(2,1)S(1)}, u32[]{:S(2)}, u32[]{:S(2)}) collective-permute-start(bf16[128,512]{1,0:T(8,128)(2,1)S(1)} %fusion.3.rest_3_), channel_id=1, source_target_pairs={{0,4},{4,16},{8,12},{12,24},{16,20},{24,28},{1,5},{5,17},{9,13},{1... | collective-permute-start | bytes 393224 | tf_op jit(solution)/shard_map/ppermute | solution.py:34
  89.8 5.0 %collective-permute-start.22 = (bf16[128,512]{1,0:T(8,128)(2,1)S(1)}, bf16[128,512]{1,0:T(8,128)(2,1)S(1)}, u32[]{:S(2)}, u32[]{:S(2)}) collective-permute-start(bf16[128,512]{1,0:T(8,128)(2,1)S(1)} %collective-permute-done.20.rest_0_), channel_id=1, source_target_pairs={{0,4},{1,5},{2,6},{3,7},{4,0},{5,1},{6,2},{7,3},{8,12},{9,13},{10,... | collective-permute-start | bytes 393224 | tf_op jit(solution)/shard_map/ppermute | solution.py:27

commit v5 on v4

--- a/solution.py
+++ b/solution.py
@@ -29,7 +29,7 @@
 
 def preceding(block):
     n_dp = lax.axis_size("dp")
-    two_before = lax.ppermute(block, "dp", [(i, i + 2) for i in range(n_dp - 2)])
+    two_before = lax.ppermute(block, "dp", [(i, (i + 2) % n_dp) for i in range(n_dp)])
     leaps = [(i, i + 1 + 2 * (i % 2)) for i in range(n_dp)]
     leapt = lax.ppermute(block, "dp", [leap for leap in leaps if leap[1] < n_dp])
     return [two_before, leapt, swapped(two_before, lax.axis_size("replica"))]
@@ -361,34 +361,77 @@
     )(packed_len, queries, *key_blocks)
 
 
-def weighted_values(weights, value_blocks):
-    heads_kv, rows, keys_all = weights.shape
-    tokens, columns = value_blocks[0].shape
-    groups = rows // tokens
-
-    def kernel(w_ref, *rest):
-        value_refs, out_ref = rest[:-1], rest[-1]
+def weighted_values_early(weights, two_before, own):
+    heads_kv, rows, _ = weights.shape
+    tokens = own.shape[0]
+
+    def kernel(w_ref, before_ref, own_ref, out_ref):
         for g in range(heads_kv):
             cut = slice(g * HD, (g + 1) * HD)
-            values = jnp.concatenate(in_order(*[ref[:, cut] for ref in value_refs]), axis=0)
-            mixed = jnp.dot(w_ref[g], values, preferred_element_type=jnp.float32)
+            picked = jnp.concatenate(
+                [w_ref[g, :, tokens : 2 * tokens], w_ref[g, :, 3 * tokens : 4 * tokens]], axis=1
+            )
+            values = jnp.concatenate([before_ref[:, cut], own_ref[:, cut]], axis=0)
+            out_ref[g] = jnp.dot(picked, values, preferred_element_type=jnp.float32)
+
+    return pl.pallas_call(
+        kernel,
+        out_shape=jax.ShapeDtypeStruct((heads_kv, rows, HD), jnp.float32),
+        compiler_params=pltpu.CompilerParams(vmem_limit_bytes=16 * 2**20),
+        cost_estimate=pl.CostEstimate(
+            flops=4 * heads_kv * rows * tokens * HD,
+            bytes_accessed=4 * heads_kv * rows * tokens,
+            transcendentals=0,
+        ),
+        name="weighted_values_early",
+    )(weights, two_before, own)
+
+
+def weighted_values(weights, early, leapt, relayed):
+    heads_kv, rows, _ = weights.shape
+    tokens = leapt.shape[0]
+    groups = rows // tokens
+    span = groups * HD
+
+    def kernel(w_ref, early_ref, leapt_ref, relayed_ref, out_ref, mixed_ref, sems):
+        copies = []
+        for g in range(heads_kv):
+            cut = slice(g * HD, (g + 1) * HD)
+            picked = jnp.concatenate(
+                [w_ref[g, :, 0:tokens], w_ref[g, :, 2 * tokens : 3 * tokens]], axis=1
+            )
+            oldest, _, last, _ = in_order(None, leapt_ref[:, cut], relayed_ref[:, cut], None)
+            values = jnp.concatenate([oldest, last], axis=0)
+            mixed = early_ref[g] + jnp.dot(picked, values, preferred_element_type=jnp.float32)
             for j in range(groups):
-                place = (g * groups + j) * HD
-                out_ref[0, :, place : place + HD] = mixed[
+                mixed_ref[:, g * span + j * HD : g * span + (j + 1) * HD] = mixed[
                     j * tokens : (j + 1) * tokens, :
                 ].astype(jnp.bfloat16)
-
-    return pl.pallas_call(
-        kernel,
-        out_shape=jax.ShapeDtypeStruct((1, tokens, heads_kv * groups * HD), jnp.bfloat16),
+            here = pl.ds(g * span, span)
+            copies.append(
+                pltpu.make_async_copy(mixed_ref.at[:, here], out_ref.at[0, :, here], sems.at[g])
+            )
+            copies[-1].start()
+        for copy in copies:
+            copy.wait()
+
+    return pl.pallas_call(
+        kernel,
+        out_shape=jax.ShapeDtypeStruct((1, tokens, heads_kv * span), jnp.bfloat16),
+        in_specs=[pl.BlockSpec(memory_space=pltpu.VMEM)] * 4,
+        out_specs=pl.BlockSpec(memory_space=pltpu.HBM),
+        scratch_shapes=[
+            pltpu.VMEM((tokens, heads_kv * span), jnp.bfloat16),
+            pltpu.SemaphoreType.DMA((heads_kv,)),
+        ],
         compiler_params=pltpu.CompilerParams(vmem_limit_bytes=24 * 2**20),
         cost_estimate=pl.CostEstimate(
-            flops=2 * heads_kv * rows * keys_all * HD,
-            bytes_accessed=2 * heads_kv * rows * keys_all,
+            flops=4 * heads_kv * rows * tokens * HD,
+            bytes_accessed=4 * heads_kv * rows * tokens,
             transcendentals=0,
         ),
         name="weighted_values",
-    )(weights, *value_blocks)
+    )(weights, early, leapt, relayed)
 
 
 def on_device(
@@ -454,7 +497,7 @@
             came[0], token_blocks[1] = tied(came[0], token_blocks[1])
         if step == 1:
             came[0], *token_blocks = tied(came[0], *token_blocks)
-            came[1], *key_blocks = tied(came[1], *key_blocks)
+            came[0], *key_blocks = tied(came[0], *key_blocks)
         if step < len(bits) - 1:
             fresh = [one_below(fresh[part], came[part]) for part in range(parts)]
             labels = [own + [label ^ mark for label in own] for own, mark in zip(labels, marks)]
@@ -473,8 +516,9 @@
         came = swapped(leaving, bit)
         partial = partial[:, 0] + came.astype(jnp.float32)
     value = partial[0].astype(jnp.bfloat16)
-    value_blocks = preceding(value) + [value]
-    attended = weighted_values(weights, value_blocks)
+    two_before, leapt, relayed = preceding(value)
+    early = weighted_values_early(weights, two_before, value)
+    attended = weighted_values(weights, early, leapt, relayed)
     return (new_master, new_first, new_second, attended)
 
 

time: 97.9 us -> 95.9 us (0.980)
  starting transfers between devices: 42.5 us -> 40.2 us
    ppermute x2, starting transfers between devices: 13.5 us -> 10.2 us  [preceding(): lax.ppermute(block, 'dp', [(i, (i + 2) % n_dp) for i in range(n_dp)])]
    ppermute x2, starting transfers between devices: 6.68 us -> 8.13 us  [preceding(): lax.ppermute(block, 'dp', [leap for leap in leaps if leap[1] < n_dp])]
  transfers between devices with their start and end apart: 23 -> 23, of which waited for: 13 -> 13; matrix products, arithmetic and copies ran while one was open for 2% -> 2% of each run, Pallas kernels for 7% -> 8%
where the time goes in v5:
time: 95.9 us; the launch traced here: 95.6 us
  starting transfers between devices  40.2 us (42%)
  waiting for transfers between devices  40.2 us (42%)
  Pallas kernels  9.89 us (10%)
  local copies, waits for them, and re-layouts  2.13 us (2%)
  other arithmetic  1.62 us (2%)
  between operations  1.57 us (2%)
    ppermute x19, waiting for transfers between devices, swapped(): return lax.ppermute(block, ALL, [(i, i ^ mask) for i in range(total)])  39.5 us
    ppermute x19, starting transfers between devices, swapped(): return lax.ppermute(block, ALL, [(i, i ^ mask) for i in range(total)])  21.9 us
    ppermute x2, starting transfers between devices, preceding(): lax.ppermute(block, 'dp', [(i, (i + 2) % n_dp) for i in range(n_dp)])  10.2 us
    ppermute x2, starting transfers between devices, preceding(): lax.ppermute(block, 'dp', [leap for leap in leaps if leap[1] < n_dp])  8.13 us
    pallas_call x1, Pallas kernels, attention_weights(): pl.pallas_call(kernel, grid=(heads_kv,), out_shape=jax.ShapeDtypeStruct((...  4.23 us
    unnamed x16, local copies, waits for them, and re-layouts  2.11 us
  transfers between devices with their start and end apart: 23, of which 13 were waited for; matrix products, arithmetic and copies ran while one was open for 2% of the time, Pallas kernels for 8%

profile of v5, /device:TPU:0, one launch (start us, length us, event | category | flops | bytes accessed | tf_op | source)
XLA Modules:
  0.0 95.6 jit_solution(8606798396257889752)
XLA Ops:
  0.6 1.6 %copy-done = bf16[8,256,512]{2,1,0:T(8,128)(2,1)S(1)} copy-done((bf16[8,256,512]{2,1,0:T(8,128)(2,1)S(1)}, bf16[8,256,512]{2,1,0:T(8,128)(2,1)}, u32[]{:S(2)}) %copy-start) | copy-done | bytes 2097176
  2.2 0.2 blocks_taken.2
  2.4 3.0 %collective-permute-start = (bf16[4,256,256]{2,1,0:T(8,128)(2,1)S(1)}, bf16[4,256,256]{2,1,0:T(8,128)(2,1)S(1)}, u32[]{:S(2)}, u32[]{:S(2)}) collective-permute-start(bf16[4,256,256]{2,1,0:T(8,128)(2,1)S(1)} %get-tuple-element.48), channel_id=1, source_target_pairs={{0,4},{1,5},{2,6},{3,7},{4,0},{5,1},{6,2},{7,3},{8,12},{9,13},{10,... | collective-permute-start | bytes 1572872 | tf_op jit(solution)/shard_map/ppermute | solution.py:27
  5.4 1.6 %collective-permute-start.1 = (bf16[4,256,256]{2,1,0:T(8,128)(2,1)S(1)}, bf16[4,256,256]{2,1,0:T(8,128)(2,1)S(1)}, u32[]{:S(2)}, u32[]{:S(2)}) collective-permute-start(bf16[4,256,256]{2,1,0:T(8,128)(2,1)S(1)} %get-tuple-element.49), channel_id=1, source_target_pairs={{0,8},{1,9},{2,10},{3,11},{4,12},{5,13},{6,14},{7,15},{8,0},{9,1},... | collective-permute-start | bytes 1572872 | tf_op jit(solution)/shard_map/ppermute | solution.py:27
  7.0 0.2 blocks_taken.3
  7.2 0.0 copy-start.1
  7.2 0.0 copy-start.2
  7.2 0.0 copy-start.3
  7.2 0.3 pack_hidden.1
  7.5 9.8 %collective-permute-done.refs_1_ = bf16[4,256,256]{2,1,0:T(8,128)(2,1)S(1)} collective-permute-done((bf16[4,256,256]{2,1,0:T(8,128)(2,1)S(1)}, bf16[4,256,256]{2,1,0:T(8,128)(2,1)S(1)}, u32[]{:S(2)}, u32[]{:S(2)}) %collective-permute-start) | collective-permute-done | bytes 524320 | tf_op jit(solution)/shard_map/ppermute | solution.py:27
  17.3 1.5 %collective-permute-done.1.refs_1_ = bf16[4,256,256]{2,1,0:T(8,128)(2,1)S(1)} collective-permute-done((bf16[4,256,256]{2,1,0:T(8,128)(2,1)S(1)}, bf16[4,256,256]{2,1,0:T(8,128)(2,1)S(1)}, u32[]{:S(2)}, u32[]{:S(2)}) %collective-permute-start.1) | collective-permute-done | bytes 524320 | tf_op jit(solution)/shard_map/ppermute | solution.py:27
  18.8 1.5 %collective-permute-start.4 = (bf16[128,2048]{1,0:T(8,128)(2,1)S(1)}, bf16[128,2048]{1,0:T(8,128)(2,1)S(1)}, u32[]{:S(2)}, u32[]{:S(2)}) collective-permute-start(bf16[128,2048]{1,0:T(8,128)(2,1)S(1)} %get-tuple-element.62), channel_id=1, source_target_pairs={{0,2},{1,3},{2,0},{3,1},{4,6},{5,7},{6,4},{7,5},{8,10},{9,11},{10,... | collective-permute-start | bytes 1572872 | tf_op jit(solution)/shard_map/ppermute | solution.py:27
  20.3 0.1 first_half_sums.6
  20.4 0.6 collective-permute-start.5
  21.0 0.1 first_half_sums.4
  21.0 1.6 %collective-permute-start.2 = (bf16[2,256,256]{2,1,0:T(8,128)(2,1)S(1)}, bf16[2,256,256]{2,1,0:T(8,128)(2,1)S(1)}, u32[]{:S(2)}, u32[]{:S(2)}) collective-permute-start(bf16[2,256,256]{2,1,0:T(8,128)(2,1)S(1)} %bitcast.30), channel_id=1, source_target_pairs={{0,8},{1,9},{2,10},{3,11},{4,12},{5,13},{6,14},{7,15},{8,0},{9,1},... | collective-permute-start | bytes 786440 | tf_op jit(solution)/shard_map/ppermute | solution.py:27
  22.7 0.0 collective-permute-start.8
  22.7 0.4 staged.1
  23.1 3.9 %collective-permute-done.5.refs_2_ = bf16[2,256,256]{2,1,0:T(8,128)(2,1)S(1)} collective-permute-done((bf16[2,256,256]{2,1,0:T(8,128)(2,1)S(1)}, bf16[2,256,256]{2,1,0:T(8,128)(2,1)S(1)}, u32[]{:S(2)}, u32[]{:S(2)}) %collective-permute-start.5) | collective-permute-done | bytes 262176 | tf_op jit(solution)/shard_map/ppermute | solution.py:27
  27.0 0.1 first_half_sums.7
  27.1 2.7 %collective-permute-start.6 = (bf16[1,256,256]{2,1,0:T(8,128)(2,1)S(1)}, bf16[1,256,256]{2,1,0:T(8,128)(2,1)S(1)}, u32[]{:S(2)}, u32[]{:S(2)}) collective-permute-start(bf16[1,256,256]{2,1,0:T(8,128)(2,1)S(1)} %bitcast.32), channel_id=1, source_target_pairs={{0,16},{1,17},{2,18},{3,19},{4,20},{5,21},{6,22},{7,23},{8,24},{9,... | collective-permute-start | bytes 393224 | tf_op jit(solution)/shard_map/ppermute | solution.py:27
  29.7 0.0 collective-permute-done.2.refs_2_
  29.7 0.1 first_half_sums.5
  29.8 0.8 collective-permute-start.3
  30.5 8.1 %collective-permute-done.6.refs_3_ = bf16[1,256,256]{2,1,0:T(8,128)(2,1)S(1)} collective-permute-done((bf16[1,256,256]{2,1,0:T(8,128)(2,1)S(1)}, bf16[1,256,256]{2,1,0:T(8,128)(2,1)S(1)}, u32[]{:S(2)}, u32[]{:S(2)}) %collective-permute-start.6) | collective-permute-done | bytes 131104 | tf_op jit(solution)/shard_map/ppermute | solution.py:27
  38.6 0.3 fresh_rows.3
  38.9 0.1 collective-permute-start.15
  39.0 1.8 %collective-permute-done.3.refs_3_ = bf16[1,256,256]{2,1,0:T(8,128)(2,1)S(1)} collective-permute-done((bf16[1,256,256]{2,1,0:T(8,128)(2,1)S(1)}, bf16[1,256,256]{2,1,0:T(8,128)(2,1)S(1)}, u32[]{:S(2)}, u32[]{:S(2)}) %collective-permute-start.3) | collective-permute-done | bytes 131104 | tf_op jit(solution)/shard_map/ppermute | solution.py:27
  40.7 0.3 fresh_rows.2
  41.0 1.2 %collective-permute-start.7 = (bf16[256,256]{1,0:T(8,128)(2,1)S(1)}, bf16[256,256]{1,0:T(8,128)(2,1)S(1)}, u32[]{:S(2)}, u32[]{:S(2)}) collective-permute-start(bf16[256,256]{1,0:T(8,128)(2,1)S(1)} %bitcast.26), channel_id=1, source_target_pairs={{0,16},{1,17},{2,18},{3,19},{4,20},{5,21},{6,22},{7,23},{8,24},{9,... | collective-permute-start | bytes 393224 | tf_op jit(solution)/shard_map/ppermute | solution.py:27
  42.2 8.0 %collective-permute-start.11 = (bf16[144,512]{1,0:T(8,128)(2,1)S(1)}, bf16[144,512]{1,0:T(8,128)(2,1)S(1)}, u32[]{:S(2)}, u32[]{:S(2)}) collective-permute-start(bf16[144,512]{1,0:T(8,128)(2,1)S(1)} %keys_and_numbers.1.rest_3_), channel_id=1, source_target_pairs={{0,8},{4,12},{8,16},{12,20},{16,24},{20,28},{24,0},{28,4},{1,9},{5... | collective-permute-start | bytes 442376 | tf_op jit(solution)/shard_map/ppermute | solution.py:32
  50.2 0.0 collective-permute-done.15.second_ref
  50.2 0.1 collective-permute-start.16
  50.3 0.0 collective-permute-done.8.refs_1_
  50.3 0.9 collective-permute-done.7.second_ref
  51.2 2.0 %collective-permute-start.9 = (bf16[512,256]{1,0:T(8,128)(2,1)S(1)}, bf16[512,256]{1,0:T(8,128)(2,1)S(1)}, u32[]{:S(2)}, u32[]{:S(2)}) collective-permute-start(bf16[512,256]{1,0:T(8,128)(2,1)S(1)} %one_below.4.first_ref), channel_id=1, source_target_pairs={{0,8},{1,9},{2,10},{3,11},{4,12},{5,13},{6,14},{7,15},{8,0},{9,1},... | collective-permute-start | bytes 786440 | tf_op jit(solution)/shard_map/ppermute | solution.py:27
  53.2 4.2 %collective-permute-start.12 = (bf16[144,512]{1,0:T(8,128)(2,1)S(1)}, bf16[144,512]{1,0:T(8,128)(2,1)S(1)}, u32[]{:S(2)}, u32[]{:S(2)}) collective-permute-start(bf16[144,512]{1,0:T(8,128)(2,1)S(1)} %keys_and_numbers.1.rest_3_), channel_id=1, source_target_pairs={{0,4},{4,16},{8,12},{12,24},{16,20},{24,28},{1,5},{5,17},{9,13},{1... | collective-permute-start | bytes 442376 | tf_op jit(solution)/shard_map/ppermute | solution.py:34
  57.5 2.4 %collective-permute-start.13 = (bf16[144,512]{1,0:T(8,128)(2,1)S(1)}, bf16[144,512]{1,0:T(8,128)(2,1)S(1)}, u32[]{:S(2)}, u32[]{:S(2)}) collective-permute-start(bf16[144,512]{1,0:T(8,128)(2,1)S(1)} %collective-permute-done.11.rest_0_), channel_id=1, source_target_pairs={{0,4},{1,5},{2,6},{3,7},{4,0},{5,1},{6,2},{7,3},{8,12},{9,13},{10,... | collective-permute-start | bytes 442376 | tf_op jit(solution)/shard_map/ppermute | solution.py:27
  59.9 0.0 collective-permute-done.16.second_ref
  59.9 0.1 collective-permute-start.17
  60.0 0.1 collective-permute-done.12.rest_1_
  60.1 4.4 %collective-permute-done.13.rest_2_ = bf16[144,512]{1,0:T(8,128)(2,1)S(1)} collective-permute-done((bf16[144,512]{1,0:T(8,128)(2,1)S(1)}, bf16[144,512]{1,0:T(8,128)(2,1)S(1)}, u32[]{:S(2)}, u32[]{:S(2)}) %collective-permute-start.13) | collective-permute-done | bytes 147488 | tf_op jit(solution)/shard_map/ppermute | solution.py:27
  64.6 2.1 %collective-permute-start.14 = (bf16[1024,256]{1,0:T(8,128)(2,1)S(1)}, bf16[1024,256]{1,0:T(8,128)(2,1)S(1)}, u32[]{:S(2)}, u32[]{:S(2)}) collective-permute-start(bf16[1024,256]{1,0:T(8,128)(2,1)S(1)} %one_below.5.refs_4_), channel_id=1, source_target_pairs={{0,4},{1,5},{2,6},{3,7},{4,0},{5,1},{6,2},{7,3},{8,12},{9,13},{10,... | collective-permute-start | bytes 1572872 | tf_op jit(solution)/shard_map/ppermute | solution.py:27
  67.3 0.0 copy-start.5
  67.3 0.7 projected_first.1.refs_4_
  68.1 0.5 copy-done.5
  68.6 4.2 %attention_weights.1.w_ref = bf16[4,1024,512]{2,1,0:T(8,128)(2,1)S(1)} custom-call(s32[1]{0:T(128)S(6)} %copy.13.used_ref, bf16[1,128,4096]{2,1,0:T(8,128)(2,1)S(1)} %copy-done.5, bf16[144,512]{1,0:T(8,128)(2,1)S(1)} %collective-permute-done.11.rest_0_, bf16[144,512]{1,0:T(8,128)(2,1)S(1)} %collective-permute-done.12.rest_1_, ...), custom_call_target="tpu_custom_call" | custom-call | flops 536870912 | bytes 5242880 | tf_op jit(solution)/shard_map/attention_weights/pallas_call | solution.py:344
  72.8 1.3 %collective-permute-done.14.refs_5_ = bf16[1024,256]{1,0:T(8,128)(2,1)S(1)} collective-permute-done((bf16[1024,256]{1,0:T(8,128)(2,1)S(1)}, bf16[1024,256]{1,0:T(8,128)(2,1)S(1)}, u32[]{:S(2)}, u32[]{:S(2)}) %collective-permute-start.14) | collective-permute-done | bytes 524320 | tf_op jit(solution)/shard_map/ppermute | solution.py:27
  74.1 0.7 projected_last.1
  74.9 0.1 collective-permute-start.18
  74.9 1.5 %collective-permute-done.18 = bf16[2,128,512]{2,1,0:T(8,128)(2,1)S(1)} collective-permute-done((bf16[2,128,512]{2,1,0:T(8,128)(2,1)S(1)}, bf16[2,128,512]{2,1,0:T(8,128)(2,1)S(1)}, u32[]{:S(2)}, u32[]{:S(2)}) %collective-permute-start.18) | collective-permute-done | bytes 262176 | tf_op jit(solution)/shard_map/ppermute | solution.py:27
  76.5 0.1 add_bitcast_fusion
  76.6 0.4 collective-permute-start.19
  77.0 0.1 add_bitcast_fusion.1
  77.1 5.1 %collective-permute-done.19 = bf16[1,128,512]{2,1,0:T(8,128)(2,1)S(1)} collective-permute-done((bf16[1,128,512]{2,1,0:T(8,128)(2,1)S(1)}, bf16[1,128,512]{2,1,0:T(8,128)(2,1)S(1)}, u32[]{:S(2)}, u32[]{:S(2)}) %collective-permute-start.19) | collective-permute-done | bytes 131104 | tf_op jit(solution)/shard_map/ppermute | solution.py:27
  82.2 2.2 %collective-permute-start.20 = (bf16[128,512]{1,0:T(8,128)(2,1)S(1)}, bf16[128,512]{1,0:T(8,128)(2,1)S(1)}, u32[]{:S(2)}, u32[]{:S(2)}) collective-permute-start(bf16[128,512]{1,0:T(8,128)(2,1)S(1)} %fusion.3.own_ref), channel_id=1, source_target_pairs={{0,8},{4,12},{8,16},{12,20},{16,24},{20,28},{24,0},{28,4},{1,9},{5... | collective-permute-start | bytes 393224 | tf_op jit(solution)/shard_map/ppermute | solution.py:32
  84.4 0.1 add_bitcast_fusion.2
  84.5 3.9 %collective-permute-start.21 = (bf16[128,512]{1,0:T(8,128)(2,1)S(1)}, bf16[128,512]{1,0:T(8,128)(2,1)S(1)}, u32[]{:S(2)}, u32[]{:S(2)}) collective-permute-start(bf16[128,512]{1,0:T(8,128)(2,1)S(1)} %fusion.3.own_ref), channel_id=1, source_target_pairs={{0,4},{4,16},{8,12},{12,24},{16,20},{24,28},{1,5},{5,17},{9,13},{1... | collective-permute-start | bytes 393224 | tf_op jit(solution)/shard_map/ppermute | solution.py:34
  88.4 0.6 collective-permute-done.20.before_ref
  89.0 1.7 %collective-permute-start.22 = (bf16[128,512]{1,0:T(8,128)(2,1)S(1)}, bf16[128,512]{1,0:T(8,128)(2,1)S(1)}, u32[]{:S(2)}, u32[]{:S(2)}) collective-permute-start(bf16[128,512]{1,0:T(8,128)(2,1)S(1)} %collective-permute-done.20.before_ref), channel_id=1, source_target_pairs={{0,4},{1,5},{2,6},{3,7},{4,0},{5,1},{6,2},{7,3},{8,12},{9,13},{10,... | collective-permute-start | bytes 393224 | tf_op jit(solution)/shard_map/ppermute | solution.py:27
  90.8 1.4 %multiply_subtract_fusion = (f32[256,512]{1,0:T(8,128)}, f32[256,512]{1,0:T(8,128)}, f32[256,512]{1,0:T(8,128)}) fusion(f32[256,512]{1,0:T(8,128)S(1)} %copy-done.1, f32[256,256]{1,0:T(8,128)S(1)} %add_bitcast_fusion.1, f32[256,256]{1,0:T(8,128)S(1)} %add_bitcast_fusion.2, f32[256,512]{1,0:T(8,128)S(1)} %copy-done.2, f32[256,512]{1,0:T(8,128)S(1)} %copy-done.3), kind=kLoop, calls=%fused_computation.4 | loop fusion | flops 2097152 | bytes 3670016 | tf_op jit(solution)/shard_map/sub | solution.py:49
  92.2 0.7 weighted_values_early.1.early_ref
  92.9 1.1 %collective-permute-done.22.relayed_ref = bf16[128,512]{1,0:T(8,128)(2,1)S(1)} collective-permute-done((bf16[128,512]{1,0:T(8,128)(2,1)S(1)}, bf16[128,512]{1,0:T(8,128)(2,1)S(1)}, u32[]{:S(2)}, u32[]{:S(2)}) %collective-permute-start.22) | collective-permute-done | bytes 131104 | tf_op jit(solution)/shard_map/ppermute | solution.py:27
  94.0 1.6 %weighted_values.1 = bf16[1,128,4096]{2,1,0:T(8,128)(2,1)} custom-call(bf16[4,1024,512]{2,1,0:T(8,128)(2,1)S(1)} %attention_weights.1.w_ref, f32[4,1024,128]{2,1,0:T(8,128)S(1)} %weighted_values_early.1.early_ref, bf16[128,512]{1,0:T(8,128)(2,1)S(1)} %collective-permute-done.21.leapt_ref, bf16[128,512]{1,0:T(8,128)(2,1)S(1)} %collective-permute-done.22.relayed_ref), custom_call_target="tpu_custom_call" | custom-call | flops 268435456 | bytes 2097152 | tf_op jit(solution)/shard_map/weighted_values/pallas_call | solution.py:418
  (24 shorter events, 0.2 us)
Async XLA Ops:
  0.6 1.6 %copy-start = (bf16[8,256,512]{2,1,0:T(8,128)(2,1)S(1)}, bf16[8,256,512]{2,1,0:T(8,128)(2,1)}, u32[]{:S(2)}) copy-start(bf16[8,256,512]{2,1,0:T(8,128)(2,1)} %terms_ref.3) | copy-start | bytes 6291460
  2.2 4.9 %copy-start.4 = (bf16[1,128,8192]{2,1,0:T(8,128)(2,1)S(1)}, bf16[1,128,8192]{2,1,0:T(8,128)(2,1)}, u32[]{:S(2)}) copy-start(bf16[1,128,8192]{2,1,0:T(8,128)(2,1)} %param.15) | copy-start | bytes 6291460
  2.4 14.9 %collective-permute-start = (bf16[4,256,256]{2,1,0:T(8,128)(2,1)S(1)}, bf16[4,256,256]{2,1,0:T(8,128)(2,1)S(1)}, u32[]{:S(2)}, u32[]{:S(2)}) collective-permute-start(bf16[4,256,256]{2,1,0:T(8,128)(2,1)S(1)} %get-tuple-element.48), channel_id=1, source_target_pairs={{0,4},{1,5},{2,6},{3,7},{4,0},{5,1},{6,2},{7,3},{8,12},{9,13},{10,... | collective-permute-start | bytes 1572872 | tf_op jit(solution)/shard_map/ppermute | solution.py:27
  5.4 2.1 %copy-start.6 = (bf16[1,128,512]{2,1,0:T(8,128)(2,1)S(1)}, bf16[1,128,512]{2,1,0:T(8,128)(2,1)}, u32[]{:S(2)}) copy-start(bf16[1,128,512]{2,1,0:T(8,128)(2,1)} %key_ref.1) | copy-start | bytes 393220
  5.4 2.1 %copy-start.7 = (s32[1,128]{1,0:T(1,128)S(1)}, s32[1,128]{1,0:T(1,128)}, u32[]{:S(2)}) copy-start(s32[1,128]{1,0:T(1,128)} %seg_ref.1) | copy-start | bytes 1540
  5.4 13.4 %collective-permute-start.1 = (bf16[4,256,256]{2,1,0:T(8,128)(2,1)S(1)}, bf16[4,256,256]{2,1,0:T(8,128)(2,1)S(1)}, u32[]{:S(2)}, u32[]{:S(2)}) collective-permute-start(bf16[4,256,256]{2,1,0:T(8,128)(2,1)S(1)} %get-tuple-element.49), channel_id=1, source_target_pairs={{0,8},{1,9},{2,10},{3,11},{4,12},{5,13},{6,14},{7,15},{8,0},{9,1},... | collective-permute-start | bytes 1572872 | tf_op jit(solution)/shard_map/ppermute | solution.py:27
  7.2 15.5 %copy-start.1 = (f32[256,512]{1,0:T(8,128)S(1)}, f32[256,512]{1,0:T(8,128)}, u32[]{:S(2)}) copy-start(f32[256,512]{1,0:T(8,128)} %refs_0_.1) | copy-start | bytes 1572868
  7.2 15.5 %copy-start.2 = (f32[256,512]{1,0:T(8,128)S(1)}, f32[256,512]{1,0:T(8,128)}, u32[]{:S(2)}) copy-start(f32[256,512]{1,0:T(8,128)} %refs_1_.1) | copy-start | bytes 1572868
  7.2 15.5 %copy-start.3 = (f32[256,512]{1,0:T(8,128)S(1)}, f32[256,512]{1,0:T(8,128)}, u32[]{:S(2)}) copy-start(f32[256,512]{1,0:T(8,128)} %refs_2_.1) | copy-start | bytes 1572868
  18.8 22.0 %collective-permute-start.4 = (bf16[128,2048]{1,0:T(8,128)(2,1)S(1)}, bf16[128,2048]{1,0:T(8,128)(2,1)S(1)}, u32[]{:S(2)}, u32[]{:S(2)}) collective-permute-start(bf16[128,2048]{1,0:T(8,128)(2,1)S(1)} %get-tuple-element.62), channel_id=1, source_target_pairs={{0,2},{1,3},{2,0},{3,1},{4,6},{5,7},{6,4},{7,5},{8,10},{9,11},{10,... | collective-permute-start | bytes 1572872 | tf_op jit(solution)/shard_map/ppermute | solution.py:27
  20.4 6.6 %collective-permute-start.5 = (bf16[2,256,256]{2,1,0:T(8,128)(2,1)S(1)}, bf16[2,256,256]{2,1,0:T(8,128)(2,1)S(1)}, u32[]{:S(2)}, u32[]{:S(2)}) collective-permute-start(bf16[2,256,256]{2,1,0:T(8,128)(2,1)S(1)} %bitcast.31), channel_id=1, source_target_pairs={{0,4},{1,5},{2,6},{3,7},{4,0},{5,1},{6,2},{7,3},{8,12},{9,13},{10,... | collective-permute-start | bytes 786440 | tf_op jit(solution)/shard_map/ppermute | solution.py:27
  21.0 8.7 %collective-permute-start.2 = (bf16[2,256,256]{2,1,0:T(8,128)(2,1)S(1)}, bf16[2,256,256]{2,1,0:T(8,128)(2,1)S(1)}, u32[]{:S(2)}, u32[]{:S(2)}) collective-permute-start(bf16[2,256,256]{2,1,0:T(8,128)(2,1)S(1)} %bitcast.30), channel_id=1, source_target_pairs={{0,8},{1,9},{2,10},{3,11},{4,12},{5,13},{6,14},{7,15},{8,0},{9,1},... | collective-permute-start | bytes 786440 | tf_op jit(solution)/shard_map/ppermute | solution.py:27
  22.7 27.6 %collective-permute-start.8 = (bf16[128,2048]{1,0:T(8,128)(2,1)S(1)}, bf16[128,2048]{1,0:T(8,128)(2,1)S(1)}, u32[]{:S(2)}, u32[]{:S(2)}) collective-permute-start(bf16[128,2048]{1,0:T(8,128)(2,1)S(1)} %get-tuple-element.69), channel_id=1, source_target_pairs={{0,1},{1,0},{2,3},{3,2},{4,5},{5,4},{6,7},{7,6},{8,9},{9,8},{10,11... | collective-permute-start | bytes 1572872 | tf_op jit(solution)/shard_map/ppermute | solution.py:27
  27.1 11.5 %collective-permute-start.6 = (bf16[1,256,256]{2,1,0:T(8,128)(2,1)S(1)}, bf16[1,256,256]{2,1,0:T(8,128)(2,1)S(1)}, u32[]{:S(2)}, u32[]{:S(2)}) collective-permute-start(bf16[1,256,256]{2,1,0:T(8,128)(2,1)S(1)} %bitcast.32), channel_id=1, source_target_pairs={{0,16},{1,17},{2,18},{3,19},{4,20},{5,21},{6,22},{7,23},{8,24},{9,... | collective-permute-start | bytes 393224 | tf_op jit(solution)/shard_map/ppermute | solution.py:27
  29.8 11.0 %collective-permute-start.3 = (bf16[1,256,256]{2,1,0:T(8,128)(2,1)S(1)}, bf16[1,256,256]{2,1,0:T(8,128)(2,1)S(1)}, u32[]{:S(2)}, u32[]{:S(2)}) collective-permute-start(bf16[1,256,256]{2,1,0:T(8,128)(2,1)S(1)} %bitcast.33), channel_id=1, source_target_pairs={{0,16},{1,17},{2,18},{3,19},{4,20},{5,21},{6,22},{7,23},{8,24},{9,... | collective-permute-start | bytes 393224 | tf_op jit(solution)/shard_map/ppermute | solution.py:27
  30.5 29.5 %collective-permute-start.10 = (bf16[128,2048]{1,0:T(8,128)(2,1)S(1)}, bf16[128,2048]{1,0:T(8,128)(2,1)S(1)}, u32[]{:S(2)}, u32[]{:S(2)}) collective-permute-start(bf16[128,2048]{1,0:T(8,128)(2,1)S(1)} %get-tuple-element.74), channel_id=1, source_target_pairs={{0,3},{1,2},{2,1},{3,0},{4,7},{5,6},{6,5},{7,4},{8,11},{9,10},{10,... | collective-permute-start | bytes 1572872 | tf_op jit(solution)/shard_map/ppermute | solution.py:27
  38.9 11.3 %collective-permute-start.15 = (bf16[256,256]{1,0:T(8,128)(2,1)S(1)}, bf16[256,256]{1,0:T(8,128)(2,1)S(1)}, u32[]{:S(2)}, u32[]{:S(2)}) collective-permute-start(bf16[256,256]{1,0:T(8,128)(2,1)S(1)} %bitcast.28), channel_id=1, source_target_pairs={{0,16},{1,17},{2,18},{3,19},{4,20},{5,21},{6,22},{7,23},{8,24},{9,... | collective-permute-start | bytes 393224 | tf_op jit(solution)/shard_map/ppermute | solution.py:27
  41.0 10.2 %collective-permute-start.7 = (bf16[256,256]{1,0:T(8,128)(2,1)S(1)}, bf16[256,256]{1,0:T(8,128)(2,1)S(1)}, u32[]{:S(2)}, u32[]{:S(2)}) collective-permute-start(bf16[256,256]{1,0:T(8,128)(2,1)S(1)} %bitcast.26), channel_id=1, source_target_pairs={{0,16},{1,17},{2,18},{3,19},{4,20},{5,21},{6,22},{7,23},{8,24},{9,... | collective-permute-start | bytes 393224 | tf_op jit(solution)/shard_map/ppermute | solution.py:27
  42.2 15.2 %collective-permute-start.11 = (bf16[144,512]{1,0:T(8,128)(2,1)S(1)}, bf16[144,512]{1,0:T(8,128)(2,1)S(1)}, u32[]{:S(2)}, u32[]{:S(2)}) collective-permute-start(bf16[144,512]{1,0:T(8,128)(2,1)S(1)} %keys_and_numbers.1.rest_3_), channel_id=1, source_target_pairs={{0,8},{4,12},{8,16},{12,20},{16,24},{20,28},{24,0},{28,4},{1,9},{5... | collective-permute-start | bytes 442376 | tf_op jit(solution)/shard_map/ppermute | solution.py:32
  50.2 9.6 %collective-permute-start.16 = (bf16[512,256]{1,0:T(8,128)(2,1)S(1)}, bf16[512,256]{1,0:T(8,128)(2,1)S(1)}, u32[]{:S(2)}, u32[]{:S(2)}) collective-permute-start(bf16[512,256]{1,0:T(8,128)(2,1)S(1)} %one_below.6.first_ref), channel_id=1, source_target_pairs={{0,4},{1,5},{2,6},{3,7},{4,0},{5,1},{6,2},{7,3},{8,12},{9,13},{10,... | collective-permute-start | bytes 786440 | tf_op jit(solution)/shard_map/ppermute | solution.py:27
  51.2 8.7 %collective-permute-start.9 = (bf16[512,256]{1,0:T(8,128)(2,1)S(1)}, bf16[512,256]{1,0:T(8,128)(2,1)S(1)}, u32[]{:S(2)}, u32[]{:S(2)}) collective-permute-start(bf16[512,256]{1,0:T(8,128)(2,1)S(1)} %one_below.4.first_ref), channel_id=1, source_target_pairs={{0,8},{1,9},{2,10},{3,11},{4,12},{5,13},{6,14},{7,15},{8,0},{9,1},... | collective-permute-start | bytes 786440 | tf_op jit(solution)/shard_map/ppermute | solution.py:27
  53.2 6.9 %collective-permute-start.12 = (bf16[144,512]{1,0:T(8,128)(2,1)S(1)}, bf16[144,512]{1,0:T(8,128)(2,1)S(1)}, u32[]{:S(2)}, u32[]{:S(2)}) collective-permute-start(bf16[144,512]{1,0:T(8,128)(2,1)S(1)} %keys_and_numbers.1.rest_3_), channel_id=1, source_target_pairs={{0,4},{4,16},{8,12},{12,24},{16,20},{24,28},{1,5},{5,17},{9,13},{1... | collective-permute-start | bytes 442376 | tf_op jit(solution)/shard_map/ppermute | solution.py:34
  57.5 7.1 %collective-permute-start.13 = (bf16[144,512]{1,0:T(8,128)(2,1)S(1)}, bf16[144,512]{1,0:T(8,128)(2,1)S(1)}, u32[]{:S(2)}, u32[]{:S(2)}) collective-permute-start(bf16[144,512]{1,0:T(8,128)(2,1)S(1)} %collective-permute-done.11.rest_0_), channel_id=1, source_target_pairs={{0,4},{1,5},{2,6},{3,7},{4,0},{5,1},{6,2},{7,3},{8,12},{9,13},{10,... | collective-permute-start | bytes 442376 | tf_op jit(solution)/shard_map/ppermute | solution.py:27
  59.9 12.9 %collective-permute-start.17 = (bf16[1024,256]{1,0:T(8,128)(2,1)S(1)}, bf16[1024,256]{1,0:T(8,128)(2,1)S(1)}, u32[]{:S(2)}, u32[]{:S(2)}) collective-permute-start(bf16[1024,256]{1,0:T(8,128)(2,1)S(1)} %one_below.7.refs_5_), channel_id=1, source_target_pairs={{0,8},{1,9},{2,10},{3,11},{4,12},{5,13},{6,14},{7,15},{8,0},{9,1},... | collective-permute-start | bytes 1572872 | tf_op jit(solution)/shard_map/ppermute | solution.py:27
  64.6 9.6 %collective-permute-start.14 = (bf16[1024,256]{1,0:T(8,128)(2,1)S(1)}, bf16[1024,256]{1,0:T(8,128)(2,1)S(1)}, u32[]{:S(2)}, u32[]{:S(2)}) collective-permute-start(bf16[1024,256]{1,0:T(8,128)(2,1)S(1)} %one_below.5.refs_4_), channel_id=1, source_target_pairs={{0,4},{1,5},{2,6},{3,7},{4,0},{5,1},{6,2},{7,3},{8,12},{9,13},{10,... | collective-permute-start | bytes 1572872 | tf_op jit(solution)/shard_map/ppermute | solution.py:27
  67.3 1.2 %copy-start.5 = (bf16[1,128,4096]{2,1,0:T(8,128)(2,1)S(1)}, bf16[1,128,4096]{2,1,0:T(8,128)(2,1)}, u32[]{:S(2)}) copy-start(bf16[1,128,4096]{2,1,0:T(8,128)(2,1)} %q_ref.1) | copy-start | bytes 3145732
  74.9 1.6 %collective-permute-start.18 = (bf16[2,128,512]{2,1,0:T(8,128)(2,1)S(1)}, bf16[2,128,512]{2,1,0:T(8,128)(2,1)S(1)}, u32[]{:S(2)}, u32[]{:S(2)}) collective-permute-start(bf16[2,128,512]{2,1,0:T(8,128)(2,1)S(1)} %get-tuple-element.91), channel_id=1, source_target_pairs={{0,1},{1,0},{2,3},{3,2},{4,5},{5,4},{6,7},{7,6},{8,9},{9,8},{10,11... | collective-permute-start | bytes 786440 | tf_op jit(solution)/shard_map/ppermute | solution.py:27
  76.6 5.6 %collective-permute-start.19 = (bf16[1,128,512]{2,1,0:T(8,128)(2,1)S(1)}, bf16[1,128,512]{2,1,0:T(8,128)(2,1)S(1)}, u32[]{:S(2)}, u32[]{:S(2)}) collective-permute-start(bf16[1,128,512]{2,1,0:T(8,128)(2,1)S(1)} %fusion.4), channel_id=1, source_target_pairs={{0,2},{1,3},{2,0},{3,1},{4,6},{5,7},{6,4},{7,5},{8,10},{9,11},{10,... | collective-permute-start | bytes 393224 | tf_op jit(solution)/shard_map/ppermute | solution.py:27
  82.2 6.8 %collective-permute-start.20 = (bf16[128,512]{1,0:T(8,128)(2,1)S(1)}, bf16[128,512]{1,0:T(8,128)(2,1)S(1)}, u32[]{:S(2)}, u32[]{:S(2)}) collective-permute-start(bf16[128,512]{1,0:T(8,128)(2,1)S(1)} %fusion.3.own_ref), channel_id=1, source_target_pairs={{0,8},{4,12},{8,16},{12,20},{16,24},{20,28},{24,0},{28,4},{1,9},{5... | collective-permute-start | bytes 393224 | tf_op jit(solution)/shard_map/ppermute | solution.py:32
  84.5 8.4 %collective-permute-start.21 = (bf16[128,512]{1,0:T(8,128)(2,1)S(1)}, bf16[128,512]{1,0:T(8,128)(2,1)S(1)}, u32[]{:S(2)}, u32[]{:S(2)}) collective-permute-start(bf16[128,512]{1,0:T(8,128)(2,1)S(1)} %fusion.3.own_ref), channel_id=1, source_target_pairs={{0,4},{4,16},{8,12},{12,24},{16,20},{24,28},{1,5},{5,17},{9,13},{1... | collective-permute-start | bytes 393224 | tf_op jit(solution)/shard_map/ppermute | solution.py:34
  89.0 5.0 %collective-permute-start.22 = (bf16[128,512]{1,0:T(8,128)(2,1)S(1)}, bf16[128,512]{1,0:T(8,128)(2,1)S(1)}, u32[]{:S(2)}, u32[]{:S(2)}) collective-permute-start(bf16[128,512]{1,0:T(8,128)(2,1)S(1)} %collective-permute-done.20.before_ref), channel_id=1, source_target_pairs={{0,4},{1,5},{2,6},{3,7},{4,0},{5,1},{6,2},{7,3},{8,12},{9,13},{10,... | collective-permute-start | bytes 393224 | tf_op jit(solution)/shard_map/ppermute | solution.py:27

commit v6 on v5

--- a/solution.py
+++ b/solution.py
@@ -27,9 +27,10 @@
     return lax.ppermute(block, ALL, [(i, i ^ mask) for i in range(total)])
 
 
-def preceding(block):
+def preceding(block, wraps):
     n_dp = lax.axis_size("dp")
-    two_before = lax.ppermute(block, "dp", [(i, (i + 2) % n_dp) for i in range(n_dp)])
+    reach = n_dp if wraps else n_dp - 2
+    two_before = lax.ppermute(block, "dp", [(i, (i + 2) % n_dp) for i in range(reach)])
     leaps = [(i, i + 1 + 2 * (i % 2)) for i in range(n_dp)]
     leapt = lax.ppermute(block, "dp", [leap for leap in leaps if leap[1] < n_dp])
     return [two_before, leapt, swapped(two_before, lax.axis_size("replica"))]
@@ -61,10 +62,9 @@
     return [offset | bits[0] for offset in rest] + rest
 
 
-def blocks_taken(terms, flips):
+def blocks_taken(terms, flips, cuts):
     _, rows, columns = terms.shape
     parts, blocks = len(flips), len(flips[0])
-    width = columns // parts
 
     def kernel(terms_ref, *refs):
         out_refs, sems = refs[:parts], refs[parts]
@@ -74,7 +74,7 @@
             for i, flip in enumerate(flips[part]):
                 copies.append(
                     pltpu.make_async_copy(
-                        terms_ref.at[here ^ flip, :, pl.ds(part * width, width)],
+                        terms_ref.at[here ^ flip, :, pl.ds(*cuts[part])],
                         out_refs[part].at[i],
                         sems.at[part, i],
                     )
@@ -88,7 +88,9 @@
         kernel,
         in_specs=[pl.BlockSpec(memory_space=pltpu.HBM)],
         out_specs=[pl.BlockSpec(memory_space=pltpu.VMEM)] * parts,
-        out_shape=[jax.ShapeDtypeStruct((blocks, rows, width), terms.dtype)] * parts,
+        out_shape=[
+            jax.ShapeDtypeStruct((blocks, rows, width), terms.dtype) for _, width in cuts
+        ],
         scratch_shapes=[pltpu.SemaphoreType.DMA((parts, blocks))],
         compiler_params=pltpu.CompilerParams(vmem_limit_bytes=SMALL),
         cost_estimate=pl.CostEstimate(
@@ -127,25 +129,20 @@
     )(*[term for terms in streams for term in terms])
 
 
-def fresh_rows(streams, first_part, state):
-    parts = len(streams)
-    sizes = [len(terms) for terms in streams]
-    _, rows, width = streams[0][0].shape
+def fresh_rows(terms, start, state):
+    _, rows, width = terms[0].shape
 
     def kernel(*refs):
         master_ref, first_ref, second_ref, out_ref = refs[-4:]
-        at = 0
-        for part, size in enumerate(sizes):
-            grad = None
-            for ref in refs[at : at + size]:
-                term = ref[ref.shape[0] - 1].astype(jnp.float32)
-                grad = term if grad is None else grad + term
-            at += size
-            cut = slice((first_part + part) * width, (first_part + part + 1) * width)
-            updated = adam_update(grad, master_ref[:, cut], first_ref[:, cut], second_ref[:, cut])
-            out_ref[part] = updated[0].astype(jnp.bfloat16)
-
-    out = jax.ShapeDtypeStruct((parts, rows, width), jnp.bfloat16)
+        grad = None
+        for ref in refs[:-4]:
+            term = ref[ref.shape[0] - 1].astype(jnp.float32)
+            grad = term if grad is None else grad + term
+        cut = slice(start, start + width)
+        updated = adam_update(grad, master_ref[:, cut], first_ref[:, cut], second_ref[:, cut])
+        out_ref[...] = updated[0].astype(jnp.bfloat16)
+
+    out = jax.ShapeDtypeStruct((rows, width), jnp.bfloat16)
     return pl.pallas_call(
         kernel,
         out_shape=out,
@@ -154,7 +151,7 @@
             flops=20 * out.size, bytes_accessed=20 * out.size, transcendentals=out.size
         ),
         name="fresh_rows",
-    )(*[term for terms in streams for term in terms], *state)
+    )(*terms, *state)
 
 
 def one_below(first, second, part=None):
@@ -233,7 +230,9 @@
     count = len(token_blocks)
     parts = len(pieces)
     tokens = token_blocks[0].shape[0]
-    depth, columns = pieces[0][0].shape
+    widths = [piece.shape[1] for piece, _ in pieces]
+    cuts = [slice(sum(widths[:i]), sum(widths[: i + 1])) for i in range(parts)]
+    depth, columns = pieces[0][0].shape[0], sum(widths)
 
     def total_of(token_ref, weight_ref, places):
         total = None
@@ -250,13 +249,13 @@
         for m in range(count):
             for part in range(parts):
                 total = total_of(refs[m], refs[count + part], pieces[part][1])
-                refs[-1][m, :, part * columns : (part + 1) * columns] = total
+                refs[-1][m, :, cuts[part]] = total
 
     def last_kernel(*refs):
         kept_ref, away_ref = refs[-2], refs[-1]
         for m in range(count):
             for part in range(parts):
-                cut = slice(part * columns, (part + 1) * columns)
+                cut = cuts[part]
                 total = total_of(refs[m], refs[count + 1 + part], pieces[part][1])
                 total = refs[count][m, :, cut] + total
                 if m % 2:
@@ -265,7 +264,7 @@
                     kept_ref[m // 2, :, cut] = total
 
     cost = pl.CostEstimate(
-        flops=2 * count * tokens * depth * columns * parts,
+        flops=2 * count * tokens * depth * columns,
         bytes_accessed=2 * count * tokens * depth * parts,
         transcendentals=0,
     )
@@ -274,7 +273,7 @@
     if before is None:
         return pl.pallas_call(
             first_kernel,
-            out_shape=jax.ShapeDtypeStruct((count, tokens, columns * parts), jnp.float32),
+            out_shape=jax.ShapeDtypeStruct((count, tokens, columns), jnp.float32),
             compiler_params=params,
             cost_estimate=cost,
             name="projected_first",
@@ -282,8 +281,8 @@
     return pl.pallas_call(
         last_kernel,
         out_shape=(
-            jax.ShapeDtypeStruct((count // 2, tokens, columns * parts), jnp.float32),
-            jax.ShapeDtypeStruct((count // 2, tokens, columns * parts), jnp.bfloat16),
+            jax.ShapeDtypeStruct((count // 2, tokens, columns), jnp.float32),
+            jax.ShapeDtypeStruct((count // 2, tokens, columns), jnp.bfloat16),
         ),
         compiler_params=params,
         cost_estimate=cost,
@@ -450,23 +449,21 @@
     rows, columns = master_weight.shape
     bits = bits_of(n_dp)
     orders = [bits, [bits[1], bits[0]] + bits[2:]]
+    cuts = [(0, columns // 2), (columns // 2, columns // 2)]
     parts = len(orders)
-    width = columns // parts
     state = (master_weight, moment_one, moment_two)
 
     flips = [halving(order) for order in orders]
-    away = blocks_taken(grad_parts, [part[: n_dp // 2] for part in flips])
+    away = blocks_taken(grad_parts, [part[: n_dp // 2] for part in flips], cuts)
     came = [swapped(block, order[0] * n_replica) for block, order in zip(away, orders)]
-    kept = list(blocks_taken(grad_parts, [part[n_dp // 2 :] for part in flips]))
+    kept = list(blocks_taken(grad_parts, [part[n_dp // 2 :] for part in flips], cuts))
 
     packed = packed_columns(hidden[0], rows, n_dp, n_replica)
 
     key_own = keys_and_numbers(keys_in, segment_ids)
 
-    came[0], came[1], kept[0], kept[1], key_own, *packed = tied(
-        came[0], came[1], kept[0], kept[1], key_own, *packed
-    )
-    key_blocks = preceding(key_own) + [key_own]
+    came[0], came[1], key_own = tied(came[0], came[1], key_own)
+    key_blocks = preceding(key_own, False) + [key_own]
     streams = [[kept[part], came[part]] for part in range(parts)]
     token_blocks = [packed[0]] + [swapped(packed[m], m) for m in range(1, n_replica)]
     state_here = staged(state)
@@ -477,14 +474,12 @@
             mark = orders[part][step] * n_replica
             came[part] = swapped(first_half_sums([streams[part]], left)[0], mark)
         left = left // 2
-        if step == 1:
-            came[0], *state_here = tied(came[0], *state_here)
         if step == 2:
             came[0], token_blocks[2] = tied(came[0], token_blocks[2])
         for part in range(parts):
             streams[part].append(came[part])
 
-    fresh = [fresh_rows([terms], part, state_here)[0] for part, terms in enumerate(streams)]
+    fresh = [fresh_rows(terms, cut[0], state_here) for cut, terms in zip(cuts, streams)]
     grad_total = [
         sum(term[-1].astype(jnp.float32) for term in streams[part]) for part in range(parts)
     ]
@@ -496,8 +491,10 @@
         if step == 0:
             came[0], token_blocks[1] = tied(came[0], token_blocks[1])
         if step == 1:
-            came[0], *token_blocks = tied(came[0], *token_blocks)
-            came[0], *key_blocks = tied(came[0], *key_blocks)
+            came[0], token_blocks[3], key_blocks[1], key_blocks[2] = tied(
+                came[0], token_blocks[3], key_blocks[1], key_blocks[2]
+            )
+            came[1], key_blocks[0] = tied(came[1], key_blocks[0])
         if step < len(bits) - 1:
             fresh = [one_below(fresh[part], came[part]) for part in range(parts)]
             labels = [own + [label ^ mark for label in own] for own, mark in zip(labels, marks)]
@@ -505,7 +502,7 @@
     joined = fresh
     last = [[label ^ mark for label in own] for own, mark in zip(labels, marks)]
     before = projected(token_blocks, list(zip(joined, labels)), rows, None)
-    came[0], came[1], weights, before = tied(came[0], came[1], weights, before)
+    *came, weights, before = tied(*came, weights, before)
     partial, leaving = projected(token_blocks, list(zip(came, last)), rows, before)
 
     came = swapped(leaving, 1)
@@ -516,7 +513,7 @@
         came = swapped(leaving, bit)
         partial = partial[:, 0] + came.astype(jnp.float32)
     value = partial[0].astype(jnp.bfloat16)
-    two_before, leapt, relayed = preceding(value)
+    two_before, leapt, relayed = preceding(value, True)
     early = weighted_values_early(weights, two_before, value)
     attended = weighted_values(weights, early, leapt, relayed)
     return (new_master, new_first, new_second, attended)

time: 95.9 us -> 95 us (level)
  waiting for transfers between devices: 40.2 us -> 37.7 us
  local copies, waits for them, and re-layouts: 2.13 us -> 3.71 us
    ppermute x19, waiting for transfers between devices: 39.5 us -> 34.5 us  [swapped(): return lax.ppermute(block, ALL, [(i, i ^ mask) for i in range(total)])]
    ppermute x2, waiting for transfers between devices: 0.63 us -> 2.8 us  [preceding(): lax.ppermute(block, 'dp', [(i, (i + 2) % n_dp) for i in range(reach)])]
    ppermute x19, starting transfers between devices: 21.9 us -> 23.6 us  [swapped(): return lax.ppermute(block, ALL, [(i, i ^ mask) for i in range(total)])]
    unnamed x16 -> x18, local copies, waits for them, and re-layouts: 2.11 us -> 3.69 us
    ppermute x2, starting transfers between devices: 8.13 us -> 6.77 us  [preceding(): lax.ppermute(block, 'dp', [leap for leap in leaps if leap[1] < n_dp])]
  transfers between devices with their start and end apart: 23 -> 23, of which waited for: 13 -> 12; matrix products, arithmetic and copies ran while one was open for 2% -> 2% of each run, Pallas kernels for 8% -> 8%
where the time goes in v6:
time: 95 us; the launch traced here: 94.7 us
  starting transfers between devices  40.2 us (42%)
  waiting for transfers between devices  37.7 us (40%)
  Pallas kernels  9.91 us (10%)
  local copies, waits for them, and re-layouts  3.71 us (4%)
  other arithmetic  1.62 us (2%)
  between operations  1.58 us (2%)
    ppermute x19, waiting for transfers between devices, swapped(): return lax.ppermute(block, ALL, [(i, i ^ mask) for i in range(total)])  34.5 us
    ppermute x19, starting transfers between devices, swapped(): return lax.ppermute(block, ALL, [(i, i ^ mask) for i in range(total)])  23.6 us
    ppermute x2, starting transfers between devices, preceding(): lax.ppermute(block, 'dp', [(i, (i + 2) % n_dp) for i in range(reach)])  9.88 us
    ppermute x2, starting transfers between devices, preceding(): lax.ppermute(block, 'dp', [leap for leap in leaps if leap[1] < n_dp])  6.77 us
    pallas_call x1, Pallas kernels, attention_weights(): pl.pallas_call(kernel, grid=(heads_kv,), out_shape=jax.ShapeDtypeStruct((...  4.25 us
    unnamed x18, local copies, waits for them, and re-layouts  3.69 us
    ppermute x2, waiting for transfers between devices, preceding(): lax.ppermute(block, 'dp', [(i, (i + 2) % n_dp) for i in range(reach)])  2.8 us
  transfers between devices with their start and end apart: 23, of which 12 were waited for; matrix products, arithmetic and copies ran while one was open for 2% of the time, Pallas kernels for 8%

profile of v6, /device:TPU:0, one launch (start us, length us, event | category | flops | bytes accessed | tf_op | source)
XLA Modules:
  0.0 94.7 jit_solution(10863006302803444218)
XLA Ops:
  0.6 1.6 %copy-done = bf16[8,256,512]{2,1,0:T(8,128)(2,1)S(1)} copy-done((bf16[8,256,512]{2,1,0:T(8,128)(2,1)S(1)}, bf16[8,256,512]{2,1,0:T(8,128)(2,1)}, u32[]{:S(2)}) %copy-start) | copy-done | bytes 2097176
  2.2 0.2 blocks_taken.3
  2.4 3.0 %collective-permute-start = (bf16[4,256,256]{2,1,0:T(8,128)(2,1)S(1)}, bf16[4,256,256]{2,1,0:T(8,128)(2,1)S(1)}, u32[]{:S(2)}, u32[]{:S(2)}) collective-permute-start(bf16[4,256,256]{2,1,0:T(8,128)(2,1)S(1)} %get-tuple-element.35), channel_id=1, source_target_pairs={{0,4},{1,5},{2,6},{3,7},{4,0},{5,1},{6,2},{7,3},{8,12},{9,13},{10,... | collective-permute-start | bytes 1572872 | tf_op jit(solution)/shard_map/ppermute | solution.py:27
  5.4 1.6 %collective-permute-start.1 = (bf16[4,256,256]{2,1,0:T(8,128)(2,1)S(1)}, bf16[4,256,256]{2,1,0:T(8,128)(2,1)S(1)}, u32[]{:S(2)}, u32[]{:S(2)}) collective-permute-start(bf16[4,256,256]{2,1,0:T(8,128)(2,1)S(1)} %get-tuple-element.36), channel_id=1, source_target_pairs={{0,8},{1,9},{2,10},{3,11},{4,12},{5,13},{6,14},{7,15},{8,0},{9,1},... | collective-permute-start | bytes 1572872 | tf_op jit(solution)/shard_map/ppermute | solution.py:27
  7.0 1.6 %copy-done.5 = bf16[1,128,8192]{2,1,0:T(8,128)(2,1)S(1)} copy-done((bf16[1,128,8192]{2,1,0:T(8,128)(2,1)S(1)}, bf16[1,128,8192]{2,1,0:T(8,128)(2,1)}, u32[]{:S(2)}) %copy-start.5) | copy-done | bytes 2097176
  8.6 0.3 pack_hidden.1
  8.9 1.6 %collective-permute-start.4 = (bf16[128,2048]{1,0:T(8,128)(2,1)S(1)}, bf16[128,2048]{1,0:T(8,128)(2,1)S(1)}, u32[]{:S(2)}, u32[]{:S(2)}) collective-permute-start(bf16[128,2048]{1,0:T(8,128)(2,1)S(1)} %get-tuple-element.38), channel_id=1, source_target_pairs={{0,2},{1,3},{2,0},{3,1},{4,6},{5,7},{6,4},{7,5},{8,10},{9,11},{10,... | collective-permute-start | bytes 1572872 | tf_op jit(solution)/shard_map/ppermute | solution.py:27
  10.5 0.2 blocks_taken.2
  10.7 6.7 %collective-permute-done.refs_1_ = bf16[4,256,256]{2,1,0:T(8,128)(2,1)S(1)} collective-permute-done((bf16[4,256,256]{2,1,0:T(8,128)(2,1)S(1)}, bf16[4,256,256]{2,1,0:T(8,128)(2,1)S(1)}, u32[]{:S(2)}, u32[]{:S(2)}) %collective-permute-start) | collective-permute-done | bytes 524320 | tf_op jit(solution)/shard_map/ppermute | solution.py:27
  17.3 1.5 %collective-permute-done.1.refs_1_ = bf16[4,256,256]{2,1,0:T(8,128)(2,1)S(1)} collective-permute-done((bf16[4,256,256]{2,1,0:T(8,128)(2,1)S(1)}, bf16[4,256,256]{2,1,0:T(8,128)(2,1)S(1)}, u32[]{:S(2)}, u32[]{:S(2)}) %collective-permute-start.1) | collective-permute-done | bytes 524320 | tf_op jit(solution)/shard_map/ppermute | solution.py:27
  18.8 0.1 first_half_sums.6
  18.8 0.4 collective-permute-start.5
  19.3 0.1 first_half_sums.4
  19.4 1.8 %collective-permute-start.2 = (bf16[2,256,256]{2,1,0:T(8,128)(2,1)S(1)}, bf16[2,256,256]{2,1,0:T(8,128)(2,1)S(1)}, u32[]{:S(2)}, u32[]{:S(2)}) collective-permute-start(bf16[2,256,256]{2,1,0:T(8,128)(2,1)S(1)} %bitcast.24), channel_id=1, source_target_pairs={{0,8},{1,9},{2,10},{3,11},{4,12},{5,13},{6,14},{7,15},{8,0},{9,1},... | collective-permute-start | bytes 786440 | tf_op jit(solution)/shard_map/ppermute | solution.py:27
  21.2 0.0 collective-permute-start.8
  21.2 4.6 %collective-permute-done.5.refs_2_ = bf16[2,256,256]{2,1,0:T(8,128)(2,1)S(1)} collective-permute-done((bf16[2,256,256]{2,1,0:T(8,128)(2,1)S(1)}, bf16[2,256,256]{2,1,0:T(8,128)(2,1)S(1)}, u32[]{:S(2)}, u32[]{:S(2)}) %collective-permute-start.5) | collective-permute-done | bytes 262176 | tf_op jit(solution)/shard_map/ppermute | solution.py:27
  25.8 0.1 first_half_sums.7
  25.8 2.7 %collective-permute-start.6 = (bf16[1,256,256]{2,1,0:T(8,128)(2,1)S(1)}, bf16[1,256,256]{2,1,0:T(8,128)(2,1)S(1)}, u32[]{:S(2)}, u32[]{:S(2)}) collective-permute-start(bf16[1,256,256]{2,1,0:T(8,128)(2,1)S(1)} %bitcast.27), channel_id=1, source_target_pairs={{0,16},{1,17},{2,18},{3,19},{4,20},{5,21},{6,22},{7,23},{8,24},{9,... | collective-permute-start | bytes 393224 | tf_op jit(solution)/shard_map/ppermute | solution.py:27
  28.5 0.0 collective-permute-done.2.refs_2_
  28.5 0.1 first_half_sums.5
  28.5 0.5 collective-permute-start.3
  29.0 0.0 collective-permute-start.10
  29.0 0.4 staged.1
  29.4 8.0 %collective-permute-done.6.refs_3_ = bf16[1,256,256]{2,1,0:T(8,128)(2,1)S(1)} collective-permute-done((bf16[1,256,256]{2,1,0:T(8,128)(2,1)S(1)}, bf16[1,256,256]{2,1,0:T(8,128)(2,1)S(1)}, u32[]{:S(2)}, u32[]{:S(2)}) %collective-permute-start.6) | collective-permute-done | bytes 131104 | tf_op jit(solution)/shard_map/ppermute | solution.py:27
  37.4 0.3 fresh_rows.3.first_ref
  37.7 0.1 collective-permute-start.15
  37.8 1.9 %collective-permute-done.3.refs_3_ = bf16[1,256,256]{2,1,0:T(8,128)(2,1)S(1)} collective-permute-done((bf16[1,256,256]{2,1,0:T(8,128)(2,1)S(1)}, bf16[1,256,256]{2,1,0:T(8,128)(2,1)S(1)}, u32[]{:S(2)}, u32[]{:S(2)}) %collective-permute-start.3) | collective-permute-done | bytes 131104 | tf_op jit(solution)/shard_map/ppermute | solution.py:27
  39.7 0.3 fresh_rows.2.first_ref
  40.0 1.0 %collective-permute-start.7 = (bf16[256,256]{1,0:T(8,128)(2,1)S(1)}, bf16[256,256]{1,0:T(8,128)(2,1)S(1)}, u32[]{:S(2)}, u32[]{:S(2)}) collective-permute-start(bf16[256,256]{1,0:T(8,128)(2,1)S(1)} %fresh_rows.2.first_ref), channel_id=1, source_target_pairs={{0,16},{1,17},{2,18},{3,19},{4,20},{5,21},{6,22},{7,23},{8,24},{9,... | collective-permute-start | bytes 393224 | tf_op jit(solution)/shard_map/ppermute | solution.py:27
  41.0 9.7 %collective-permute-start.12 = (bf16[144,512]{1,0:T(8,128)(2,1)S(1)}, bf16[144,512]{1,0:T(8,128)(2,1)S(1)}, u32[]{:S(2)}, u32[]{:S(2)}) collective-permute-start(bf16[144,512]{1,0:T(8,128)(2,1)S(1)} %keys_and_numbers.1.rest_3_), channel_id=1, source_target_pairs={{0,8},{4,12},{8,16},{12,20},{16,24},{20,28},{1,9},{5,13},{9,17},{1... | collective-permute-start | bytes 442376 | tf_op jit(solution)/shard_map/ppermute | solution.py:33
  50.8 0.0 collective-permute-done.15.second_ref
  50.8 0.1 collective-permute-start.16
  50.9 0.0 collective-permute-done.8.refs_1_
  50.9 1.0 %collective-permute-start.9 = (bf16[512,256]{1,0:T(8,128)(2,1)S(1)}, bf16[512,256]{1,0:T(8,128)(2,1)S(1)}, u32[]{:S(2)}, u32[]{:S(2)}) collective-permute-start(bf16[512,256]{1,0:T(8,128)(2,1)S(1)} %one_below.4.first_ref), channel_id=1, source_target_pairs={{0,8},{1,9},{2,10},{3,11},{4,12},{5,13},{6,14},{7,15},{8,0},{9,1},... | collective-permute-start | bytes 786440 | tf_op jit(solution)/shard_map/ppermute | solution.py:27
  51.9 3.0 %collective-permute-start.11 = (bf16[144,512]{1,0:T(8,128)(2,1)S(1)}, bf16[144,512]{1,0:T(8,128)(2,1)S(1)}, u32[]{:S(2)}, u32[]{:S(2)}) collective-permute-start(bf16[144,512]{1,0:T(8,128)(2,1)S(1)} %keys_and_numbers.1.rest_3_), channel_id=1, source_target_pairs={{0,4},{4,16},{8,12},{12,24},{16,20},{24,28},{1,5},{5,17},{9,13},{1... | collective-permute-start | bytes 442376 | tf_op jit(solution)/shard_map/ppermute | solution.py:35
  54.9 0.0 collective-permute-done.12.rest_0_
  54.9 3.9 %collective-permute-start.13 = (bf16[144,512]{1,0:T(8,128)(2,1)S(1)}, bf16[144,512]{1,0:T(8,128)(2,1)S(1)}, u32[]{:S(2)}, u32[]{:S(2)}) collective-permute-start(bf16[144,512]{1,0:T(8,128)(2,1)S(1)} %collective-permute-done.12.rest_0_), channel_id=1, source_target_pairs={{0,4},{1,5},{2,6},{3,7},{4,0},{5,1},{6,2},{7,3},{8,12},{9,13},{10,... | collective-permute-start | bytes 442376 | tf_op jit(solution)/shard_map/ppermute | solution.py:27
  58.9 0.1 collective-permute-start.17
  59.0 0.4 collective-permute-done.11.rest_1_
  59.4 2.5 %collective-permute-done.13.rest_2_ = bf16[144,512]{1,0:T(8,128)(2,1)S(1)} collective-permute-done((bf16[144,512]{1,0:T(8,128)(2,1)S(1)}, bf16[144,512]{1,0:T(8,128)(2,1)S(1)}, u32[]{:S(2)}, u32[]{:S(2)}) %collective-permute-start.13) | collective-permute-done | bytes 147488 | tf_op jit(solution)/shard_map/ppermute | solution.py:27
  62.0 2.3 %collective-permute-start.14 = (bf16[1024,256]{1,0:T(8,128)(2,1)S(1)}, bf16[1024,256]{1,0:T(8,128)(2,1)S(1)}, u32[]{:S(2)}, u32[]{:S(2)}) collective-permute-start(bf16[1024,256]{1,0:T(8,128)(2,1)S(1)} %one_below.5.refs_4_), channel_id=1, source_target_pairs={{0,4},{1,5},{2,6},{3,7},{4,0},{5,1},{6,2},{7,3},{8,12},{9,13},{10,... | collective-permute-start | bytes 1572872 | tf_op jit(solution)/shard_map/ppermute | solution.py:27
  64.9 0.0 copy-start.6
  64.9 0.7 projected_first.1.refs_4_
  65.6 0.5 copy-done.6
  66.1 4.2 %attention_weights.1.w_ref = bf16[4,1024,512]{2,1,0:T(8,128)(2,1)S(1)} custom-call(s32[1]{0:T(128)S(6)} %copy.13.used_ref, bf16[1,128,4096]{2,1,0:T(8,128)(2,1)S(1)} %copy-done.6, bf16[144,512]{1,0:T(8,128)(2,1)S(1)} %collective-permute-done.12.rest_0_, bf16[144,512]{1,0:T(8,128)(2,1)S(1)} %collective-permute-done.11.rest_1_, ...), custom_call_target="tpu_custom_call" | custom-call | flops 536870912 | bytes 5242880 | tf_op jit(solution)/shard_map/attention_weights/pallas_call | solution.py:343
  70.4 0.0 collective-permute-done.17.refs_6_
  70.4 2.8 %collective-permute-done.14.refs_5_ = bf16[1024,256]{1,0:T(8,128)(2,1)S(1)} collective-permute-done((bf16[1024,256]{1,0:T(8,128)(2,1)S(1)}, bf16[1024,256]{1,0:T(8,128)(2,1)S(1)}, u32[]{:S(2)}, u32[]{:S(2)}) %collective-permute-start.14) | collective-permute-done | bytes 524320 | tf_op jit(solution)/shard_map/ppermute | solution.py:27
  73.2 0.7 projected_last.1
  74.0 0.1 collective-permute-start.18
  74.1 1.5 %collective-permute-done.18 = bf16[2,128,512]{2,1,0:T(8,128)(2,1)S(1)} collective-permute-done((bf16[2,128,512]{2,1,0:T(8,128)(2,1)S(1)}, bf16[2,128,512]{2,1,0:T(8,128)(2,1)S(1)}, u32[]{:S(2)}, u32[]{:S(2)}) %collective-permute-start.18) | collective-permute-done | bytes 262176 | tf_op jit(solution)/shard_map/ppermute | solution.py:27
  75.6 0.1 add_bitcast_fusion
  75.7 1.6 %collective-permute-start.19 = (bf16[1,128,512]{2,1,0:T(8,128)(2,1)S(1)}, bf16[1,128,512]{2,1,0:T(8,128)(2,1)S(1)}, u32[]{:S(2)}, u32[]{:S(2)}) collective-permute-start(bf16[1,128,512]{2,1,0:T(8,128)(2,1)S(1)} %fusion.4), channel_id=1, source_target_pairs={{0,2},{1,3},{2,0},{3,1},{4,6},{5,7},{6,4},{7,5},{8,10},{9,11},{10,... | collective-permute-start | bytes 393224 | tf_op jit(solution)/shard_map/ppermute | solution.py:27
  77.3 0.1 add_bitcast_fusion.1
  77.3 4.0 %collective-permute-done.19 = bf16[1,128,512]{2,1,0:T(8,128)(2,1)S(1)} collective-permute-done((bf16[1,128,512]{2,1,0:T(8,128)(2,1)S(1)}, bf16[1,128,512]{2,1,0:T(8,128)(2,1)S(1)}, u32[]{:S(2)}, u32[]{:S(2)}) %collective-permute-start.19) | collective-permute-done | bytes 131104 | tf_op jit(solution)/shard_map/ppermute | solution.py:27
  81.3 0.2 collective-permute-start.20
  81.5 0.1 add_bitcast_fusion.2
  81.6 3.8 %collective-permute-start.21 = (bf16[128,512]{1,0:T(8,128)(2,1)S(1)}, bf16[128,512]{1,0:T(8,128)(2,1)S(1)}, u32[]{:S(2)}, u32[]{:S(2)}) collective-permute-start(bf16[128,512]{1,0:T(8,128)(2,1)S(1)} %fusion.3.own_ref), channel_id=1, source_target_pairs={{0,4},{4,16},{8,12},{12,24},{16,20},{24,28},{1,5},{5,17},{9,13},{1... | collective-permute-start | bytes 393224 | tf_op jit(solution)/shard_map/ppermute | solution.py:35
  85.3 2.8 %collective-permute-done.20.before_ref = bf16[128,512]{1,0:T(8,128)(2,1)S(1)} collective-permute-done((bf16[128,512]{1,0:T(8,128)(2,1)S(1)}, bf16[128,512]{1,0:T(8,128)(2,1)S(1)}, u32[]{:S(2)}, u32[]{:S(2)}) %collective-permute-start.20) | collective-permute-done | bytes 131104 | tf_op jit(solution)/shard_map/ppermute | solution.py:33
  88.1 2.0 %collective-permute-start.22 = (bf16[128,512]{1,0:T(8,128)(2,1)S(1)}, bf16[128,512]{1,0:T(8,128)(2,1)S(1)}, u32[]{:S(2)}, u32[]{:S(2)}) collective-permute-start(bf16[128,512]{1,0:T(8,128)(2,1)S(1)} %collective-permute-done.20.before_ref), channel_id=1, source_target_pairs={{0,4},{1,5},{2,6},{3,7},{4,0},{5,1},{6,2},{7,3},{8,12},{9,13},{10,... | collective-permute-start | bytes 393224 | tf_op jit(solution)/shard_map/ppermute | solution.py:27
  90.1 1.4 %multiply_subtract_fusion = (f32[256,512]{1,0:T(8,128)}, f32[256,512]{1,0:T(8,128)}, f32[256,512]{1,0:T(8,128)}) fusion(f32[256,512]{1,0:T(8,128)S(1)} %copy-done.2, f32[256,256]{1,0:T(8,128)S(1)} %add_bitcast_fusion.1, f32[256,256]{1,0:T(8,128)S(1)} %add_bitcast_fusion.2, f32[256,512]{1,0:T(8,128)S(1)} %copy-done.3, f32[256,512]{1,0:T(8,128)S(1)} %copy-done.4), kind=kLoop, calls=%fused_computation.4 | loop fusion | flops 2097152 | bytes 3670016 | tf_op jit(solution)/shard_map/sub | solution.py:50
  91.5 0.7 weighted_values_early.1.early_ref
  92.2 0.0 collective-permute-done.21.leapt_ref
  92.2 0.9 collective-permute-done.22.relayed_ref
  93.1 1.6 %weighted_values.1 = bf16[1,128,4096]{2,1,0:T(8,128)(2,1)} custom-call(bf16[4,1024,512]{2,1,0:T(8,128)(2,1)S(1)} %attention_weights.1.w_ref, f32[4,1024,128]{2,1,0:T(8,128)S(1)} %weighted_values_early.1.early_ref, bf16[128,512]{1,0:T(8,128)(2,1)S(1)} %collective-permute-done.21.leapt_ref, bf16[128,512]{1,0:T(8,128)(2,1)S(1)} %collective-permute-done.22.relayed_ref), custom_call_target="tpu_custom_call" | custom-call | flops 268435456 | bytes 2097152 | tf_op jit(solution)/shard_map/weighted_values/pallas_call | solution.py:417
  (26 shorter events, 0.2 us)
Async XLA Ops:
  0.6 1.6 %copy-start = (bf16[8,256,512]{2,1,0:T(8,128)(2,1)S(1)}, bf16[8,256,512]{2,1,0:T(8,128)(2,1)}, u32[]{:S(2)}) copy-start(bf16[8,256,512]{2,1,0:T(8,128)(2,1)} %terms_ref.3) | copy-start | bytes 6291460
  2.2 8.2 %copy-start.1 = (bf16[8,256,512]{2,1,0:T(8,128)(2,1)S(1)}, bf16[8,256,512]{2,1,0:T(8,128)(2,1)}, u32[]{:S(2)}) copy-start(bf16[8,256,512]{2,1,0:T(8,128)(2,1)} %terms_ref.3) | copy-start | bytes 6291460
  2.4 14.9 %collective-permute-start = (bf16[4,256,256]{2,1,0:T(8,128)(2,1)S(1)}, bf16[4,256,256]{2,1,0:T(8,128)(2,1)S(1)}, u32[]{:S(2)}, u32[]{:S(2)}) collective-permute-start(bf16[4,256,256]{2,1,0:T(8,128)(2,1)S(1)} %get-tuple-element.35), channel_id=1, source_target_pairs={{0,4},{1,5},{2,6},{3,7},{4,0},{5,1},{6,2},{7,3},{8,12},{9,13},{10,... | collective-permute-start | bytes 1572872 | tf_op jit(solution)/shard_map/ppermute | solution.py:27
  5.4 13.4 %collective-permute-start.1 = (bf16[4,256,256]{2,1,0:T(8,128)(2,1)S(1)}, bf16[4,256,256]{2,1,0:T(8,128)(2,1)S(1)}, u32[]{:S(2)}, u32[]{:S(2)}) collective-permute-start(bf16[4,256,256]{2,1,0:T(8,128)(2,1)S(1)} %get-tuple-element.36), channel_id=1, source_target_pairs={{0,8},{1,9},{2,10},{3,11},{4,12},{5,13},{6,14},{7,15},{8,0},{9,1},... | collective-permute-start | bytes 1572872 | tf_op jit(solution)/shard_map/ppermute | solution.py:27
  7.0 1.6 %copy-start.5 = (bf16[1,128,8192]{2,1,0:T(8,128)(2,1)S(1)}, bf16[1,128,8192]{2,1,0:T(8,128)(2,1)}, u32[]{:S(2)}) copy-start(bf16[1,128,8192]{2,1,0:T(8,128)(2,1)} %param.15) | copy-start | bytes 6291460
  8.6 2.1 %copy-start.7 = (bf16[1,128,512]{2,1,0:T(8,128)(2,1)S(1)}, bf16[1,128,512]{2,1,0:T(8,128)(2,1)}, u32[]{:S(2)}) copy-start(bf16[1,128,512]{2,1,0:T(8,128)(2,1)} %key_ref.1) | copy-start | bytes 393220
  8.6 2.1 %copy-start.8 = (s32[1,128]{1,0:T(1,128)S(1)}, s32[1,128]{1,0:T(1,128)}, u32[]{:S(2)}) copy-start(s32[1,128]{1,0:T(1,128)} %seg_ref.1) | copy-start | bytes 1540
  8.9 28.9 %collective-permute-start.4 = (bf16[128,2048]{1,0:T(8,128)(2,1)S(1)}, bf16[128,2048]{1,0:T(8,128)(2,1)S(1)}, u32[]{:S(2)}, u32[]{:S(2)}) collective-permute-start(bf16[128,2048]{1,0:T(8,128)(2,1)S(1)} %get-tuple-element.38), channel_id=1, source_target_pairs={{0,2},{1,3},{2,0},{3,1},{4,6},{5,7},{6,4},{7,5},{8,10},{9,11},{10,... | collective-permute-start | bytes 1572872 | tf_op jit(solution)/shard_map/ppermute | solution.py:27
  18.8 6.9 %collective-permute-start.5 = (bf16[2,256,256]{2,1,0:T(8,128)(2,1)S(1)}, bf16[2,256,256]{2,1,0:T(8,128)(2,1)S(1)}, u32[]{:S(2)}, u32[]{:S(2)}) collective-permute-start(bf16[2,256,256]{2,1,0:T(8,128)(2,1)S(1)} %bitcast.25), channel_id=1, source_target_pairs={{0,4},{1,5},{2,6},{3,7},{4,0},{5,1},{6,2},{7,3},{8,12},{9,13},{10,... | collective-permute-start | bytes 786440 | tf_op jit(solution)/shard_map/ppermute | solution.py:27
  19.3 9.7 %copy-start.2 = (f32[256,512]{1,0:T(8,128)S(1)}, f32[256,512]{1,0:T(8,128)}, u32[]{:S(2)}) copy-start(f32[256,512]{1,0:T(8,128)} %refs_0_.1) | copy-start | bytes 1572868
  19.3 9.7 %copy-start.3 = (f32[256,512]{1,0:T(8,128)S(1)}, f32[256,512]{1,0:T(8,128)}, u32[]{:S(2)}) copy-start(f32[256,512]{1,0:T(8,128)} %refs_1_.1) | copy-start | bytes 1572868
  19.3 9.7 %copy-start.4 = (f32[256,512]{1,0:T(8,128)S(1)}, f32[256,512]{1,0:T(8,128)}, u32[]{:S(2)}) copy-start(f32[256,512]{1,0:T(8,128)} %refs_2_.1) | copy-start | bytes 1572868
  19.4 9.1 %collective-permute-start.2 = (bf16[2,256,256]{2,1,0:T(8,128)(2,1)S(1)}, bf16[2,256,256]{2,1,0:T(8,128)(2,1)S(1)}, u32[]{:S(2)}, u32[]{:S(2)}) collective-permute-start(bf16[2,256,256]{2,1,0:T(8,128)(2,1)S(1)} %bitcast.24), channel_id=1, source_target_pairs={{0,8},{1,9},{2,10},{3,11},{4,12},{5,13},{6,14},{7,15},{8,0},{9,1},... | collective-permute-start | bytes 786440 | tf_op jit(solution)/shard_map/ppermute | solution.py:27
  21.2 29.7 %collective-permute-start.8 = (bf16[128,2048]{1,0:T(8,128)(2,1)S(1)}, bf16[128,2048]{1,0:T(8,128)(2,1)S(1)}, u32[]{:S(2)}, u32[]{:S(2)}) collective-permute-start(bf16[128,2048]{1,0:T(8,128)(2,1)S(1)} %get-tuple-element.45), channel_id=1, source_target_pairs={{0,1},{1,0},{2,3},{3,2},{4,5},{5,4},{6,7},{7,6},{8,9},{9,8},{10,11... | collective-permute-start | bytes 1572872 | tf_op jit(solution)/shard_map/ppermute | solution.py:27
  25.8 11.6 %collective-permute-start.6 = (bf16[1,256,256]{2,1,0:T(8,128)(2,1)S(1)}, bf16[1,256,256]{2,1,0:T(8,128)(2,1)S(1)}, u32[]{:S(2)}, u32[]{:S(2)}) collective-permute-start(bf16[1,256,256]{2,1,0:T(8,128)(2,1)S(1)} %bitcast.27), channel_id=1, source_target_pairs={{0,16},{1,17},{2,18},{3,19},{4,20},{5,21},{6,22},{7,23},{8,24},{9,... | collective-permute-start | bytes 393224 | tf_op jit(solution)/shard_map/ppermute | solution.py:27
  28.5 11.2 %collective-permute-start.3 = (bf16[1,256,256]{2,1,0:T(8,128)(2,1)S(1)}, bf16[1,256,256]{2,1,0:T(8,128)(2,1)S(1)}, u32[]{:S(2)}, u32[]{:S(2)}) collective-permute-start(bf16[1,256,256]{2,1,0:T(8,128)(2,1)S(1)} %bitcast.26), channel_id=1, source_target_pairs={{0,16},{1,17},{2,18},{3,19},{4,20},{5,21},{6,22},{7,23},{8,24},{9,... | collective-permute-start | bytes 393224 | tf_op jit(solution)/shard_map/ppermute | solution.py:27
  29.0 30.0 %collective-permute-start.10 = (bf16[128,2048]{1,0:T(8,128)(2,1)S(1)}, bf16[128,2048]{1,0:T(8,128)(2,1)S(1)}, u32[]{:S(2)}, u32[]{:S(2)}) collective-permute-start(bf16[128,2048]{1,0:T(8,128)(2,1)S(1)} %get-tuple-element.47), channel_id=1, source_target_pairs={{0,3},{1,2},{2,1},{3,0},{4,7},{5,6},{6,5},{7,4},{8,11},{9,10},{10,... | collective-permute-start | bytes 1572872 | tf_op jit(solution)/shard_map/ppermute | solution.py:27
  37.7 13.0 %collective-permute-start.15 = (bf16[256,256]{1,0:T(8,128)(2,1)S(1)}, bf16[256,256]{1,0:T(8,128)(2,1)S(1)}, u32[]{:S(2)}, u32[]{:S(2)}) collective-permute-start(bf16[256,256]{1,0:T(8,128)(2,1)S(1)} %fresh_rows.3.first_ref), channel_id=1, source_target_pairs={{0,16},{1,17},{2,18},{3,19},{4,20},{5,21},{6,22},{7,23},{8,24},{9,... | collective-permute-start | bytes 393224 | tf_op jit(solution)/shard_map/ppermute | solution.py:27
  40.0 10.9 %collective-permute-start.7 = (bf16[256,256]{1,0:T(8,128)(2,1)S(1)}, bf16[256,256]{1,0:T(8,128)(2,1)S(1)}, u32[]{:S(2)}, u32[]{:S(2)}) collective-permute-start(bf16[256,256]{1,0:T(8,128)(2,1)S(1)} %fresh_rows.2.first_ref), channel_id=1, source_target_pairs={{0,16},{1,17},{2,18},{3,19},{4,20},{5,21},{6,22},{7,23},{8,24},{9,... | collective-permute-start | bytes 393224 | tf_op jit(solution)/shard_map/ppermute | solution.py:27
  41.0 13.9 %collective-permute-start.12 = (bf16[144,512]{1,0:T(8,128)(2,1)S(1)}, bf16[144,512]{1,0:T(8,128)(2,1)S(1)}, u32[]{:S(2)}, u32[]{:S(2)}) collective-permute-start(bf16[144,512]{1,0:T(8,128)(2,1)S(1)} %keys_and_numbers.1.rest_3_), channel_id=1, source_target_pairs={{0,8},{4,12},{8,16},{12,20},{16,24},{20,28},{1,9},{5,13},{9,17},{1... | collective-permute-start | bytes 442376 | tf_op jit(solution)/shard_map/ppermute | solution.py:33
  50.8 8.0 %collective-permute-start.16 = (bf16[512,256]{1,0:T(8,128)(2,1)S(1)}, bf16[512,256]{1,0:T(8,128)(2,1)S(1)}, u32[]{:S(2)}, u32[]{:S(2)}) collective-permute-start(bf16[512,256]{1,0:T(8,128)(2,1)S(1)} %one_below.6.first_ref), channel_id=1, source_target_pairs={{0,4},{1,5},{2,6},{3,7},{4,0},{5,1},{6,2},{7,3},{8,12},{9,13},{10,... | collective-permute-start | bytes 786440 | tf_op jit(solution)/shard_map/ppermute | solution.py:27
  50.9 11.0 %collective-permute-start.9 = (bf16[512,256]{1,0:T(8,128)(2,1)S(1)}, bf16[512,256]{1,0:T(8,128)(2,1)S(1)}, u32[]{:S(2)}, u32[]{:S(2)}) collective-permute-start(bf16[512,256]{1,0:T(8,128)(2,1)S(1)} %one_below.4.first_ref), channel_id=1, source_target_pairs={{0,8},{1,9},{2,10},{3,11},{4,12},{5,13},{6,14},{7,15},{8,0},{9,1},... | collective-permute-start | bytes 786440 | tf_op jit(solution)/shard_map/ppermute | solution.py:27
  51.9 7.5 %collective-permute-start.11 = (bf16[144,512]{1,0:T(8,128)(2,1)S(1)}, bf16[144,512]{1,0:T(8,128)(2,1)S(1)}, u32[]{:S(2)}, u32[]{:S(2)}) collective-permute-start(bf16[144,512]{1,0:T(8,128)(2,1)S(1)} %keys_and_numbers.1.rest_3_), channel_id=1, source_target_pairs={{0,4},{4,16},{8,12},{12,24},{16,20},{24,28},{1,5},{5,17},{9,13},{1... | collective-permute-start | bytes 442376 | tf_op jit(solution)/shard_map/ppermute | solution.py:35
  54.9 7.0 %collective-permute-start.13 = (bf16[144,512]{1,0:T(8,128)(2,1)S(1)}, bf16[144,512]{1,0:T(8,128)(2,1)S(1)}, u32[]{:S(2)}, u32[]{:S(2)}) collective-permute-start(bf16[144,512]{1,0:T(8,128)(2,1)S(1)} %collective-permute-done.12.rest_0_), channel_id=1, source_target_pairs={{0,4},{1,5},{2,6},{3,7},{4,0},{5,1},{6,2},{7,3},{8,12},{9,13},{10,... | collective-permute-start | bytes 442376 | tf_op jit(solution)/shard_map/ppermute | solution.py:27
  58.9 11.5 %collective-permute-start.17 = (bf16[1024,256]{1,0:T(8,128)(2,1)S(1)}, bf16[1024,256]{1,0:T(8,128)(2,1)S(1)}, u32[]{:S(2)}, u32[]{:S(2)}) collective-permute-start(bf16[1024,256]{1,0:T(8,128)(2,1)S(1)} %one_below.7.refs_5_), channel_id=1, source_target_pairs={{0,8},{1,9},{2,10},{3,11},{4,12},{5,13},{6,14},{7,15},{8,0},{9,1},... | collective-permute-start | bytes 1572872 | tf_op jit(solution)/shard_map/ppermute | solution.py:27
  62.0 11.3 %collective-permute-start.14 = (bf16[1024,256]{1,0:T(8,128)(2,1)S(1)}, bf16[1024,256]{1,0:T(8,128)(2,1)S(1)}, u32[]{:S(2)}, u32[]{:S(2)}) collective-permute-start(bf16[1024,256]{1,0:T(8,128)(2,1)S(1)} %one_below.5.refs_4_), channel_id=1, source_target_pairs={{0,4},{1,5},{2,6},{3,7},{4,0},{5,1},{6,2},{7,3},{8,12},{9,13},{10,... | collective-permute-start | bytes 1572872 | tf_op jit(solution)/shard_map/ppermute | solution.py:27
  64.9 1.2 %copy-start.6 = (bf16[1,128,4096]{2,1,0:T(8,128)(2,1)S(1)}, bf16[1,128,4096]{2,1,0:T(8,128)(2,1)}, u32[]{:S(2)}) copy-start(bf16[1,128,4096]{2,1,0:T(8,128)(2,1)} %q_ref.1) | copy-start | bytes 3145732
  74.0 1.6 %collective-permute-start.18 = (bf16[2,128,512]{2,1,0:T(8,128)(2,1)S(1)}, bf16[2,128,512]{2,1,0:T(8,128)(2,1)S(1)}, u32[]{:S(2)}, u32[]{:S(2)}) collective-permute-start(bf16[2,128,512]{2,1,0:T(8,128)(2,1)S(1)} %get-tuple-element.63), channel_id=1, source_target_pairs={{0,1},{1,0},{2,3},{3,2},{4,5},{5,4},{6,7},{7,6},{8,9},{9,8},{10,11... | collective-permute-start | bytes 786440 | tf_op jit(solution)/shard_map/ppermute | solution.py:27
  75.7 5.6 %collective-permute-start.19 = (bf16[1,128,512]{2,1,0:T(8,128)(2,1)S(1)}, bf16[1,128,512]{2,1,0:T(8,128)(2,1)S(1)}, u32[]{:S(2)}, u32[]{:S(2)}) collective-permute-start(bf16[1,128,512]{2,1,0:T(8,128)(2,1)S(1)} %fusion.4), channel_id=1, source_target_pairs={{0,2},{1,3},{2,0},{3,1},{4,6},{5,7},{6,4},{7,5},{8,10},{9,11},{10,... | collective-permute-start | bytes 393224 | tf_op jit(solution)/shard_map/ppermute | solution.py:27
  81.3 6.8 %collective-permute-start.20 = (bf16[128,512]{1,0:T(8,128)(2,1)S(1)}, bf16[128,512]{1,0:T(8,128)(2,1)S(1)}, u32[]{:S(2)}, u32[]{:S(2)}) collective-permute-start(bf16[128,512]{1,0:T(8,128)(2,1)S(1)} %fusion.3.own_ref), channel_id=1, source_target_pairs={{0,8},{4,12},{8,16},{12,20},{16,24},{20,28},{24,0},{28,4},{1,9},{5... | collective-permute-start | bytes 393224 | tf_op jit(solution)/shard_map/ppermute | solution.py:33
  81.6 10.6 %collective-permute-start.21 = (bf16[128,512]{1,0:T(8,128)(2,1)S(1)}, bf16[128,512]{1,0:T(8,128)(2,1)S(1)}, u32[]{:S(2)}, u32[]{:S(2)}) collective-permute-start(bf16[128,512]{1,0:T(8,128)(2,1)S(1)} %fusion.3.own_ref), channel_id=1, source_target_pairs={{0,4},{4,16},{8,12},{12,24},{16,20},{24,28},{1,5},{5,17},{9,13},{1... | collective-permute-start | bytes 393224 | tf_op jit(solution)/shard_map/ppermute | solution.py:35
  88.1 5.0 %collective-permute-start.22 = (bf16[128,512]{1,0:T(8,128)(2,1)S(1)}, bf16[128,512]{1,0:T(8,128)(2,1)S(1)}, u32[]{:S(2)}, u32[]{:S(2)}) collective-permute-start(bf16[128,512]{1,0:T(8,128)(2,1)S(1)} %collective-permute-done.20.before_ref), channel_id=1, source_target_pairs={{0,4},{1,5},{2,6},{3,7},{4,0},{5,1},{6,2},{7,3},{8,12},{9,13},{10,... | collective-permute-start | bytes 393224 | tf_op jit(solution)/shard_map/ppermute | solution.py:27

commit v7 on v6

--- a/solution.py
+++ b/solution.py
@@ -360,17 +360,25 @@
     )(packed_len, queries, *key_blocks)
 
 
-def weighted_values_early(weights, two_before, own):
+def weighted_values_early(weights, two_before, leapt, own):
     heads_kv, rows, _ = weights.shape
     tokens = own.shape[0]
 
-    def kernel(w_ref, before_ref, own_ref, out_ref):
+    def kernel(w_ref, before_ref, leapt_ref, own_ref, out_ref):
+        leapt_at = pl.multiple_of(lax.axis_index("dp") % 2 * 2 * tokens, tokens)
         for g in range(heads_kv):
             cut = slice(g * HD, (g + 1) * HD)
             picked = jnp.concatenate(
-                [w_ref[g, :, tokens : 2 * tokens], w_ref[g, :, 3 * tokens : 4 * tokens]], axis=1
+                [
+                    w_ref[g, :, tokens : 2 * tokens],
+                    w_ref[g, :, 3 * tokens : 4 * tokens],
+                    w_ref[g, :, pl.ds(leapt_at, tokens)],
+                ],
+                axis=1,
             )
-            values = jnp.concatenate([before_ref[:, cut], own_ref[:, cut]], axis=0)
+            values = jnp.concatenate(
+                [before_ref[:, cut], own_ref[:, cut], leapt_ref[:, cut]], axis=0
+            )
             out_ref[g] = jnp.dot(picked, values, preferred_element_type=jnp.float32)
 
     return pl.pallas_call(
@@ -383,25 +391,25 @@
             transcendentals=0,
         ),
         name="weighted_values_early",
-    )(weights, two_before, own)
-
-
-def weighted_values(weights, early, leapt, relayed):
+    )(weights, two_before, leapt, own)
+
+
+def weighted_values(weights, early, relayed):
     heads_kv, rows, _ = weights.shape
-    tokens = leapt.shape[0]
+    tokens = relayed.shape[0]
     groups = rows // tokens
     span = groups * HD
 
-    def kernel(w_ref, early_ref, leapt_ref, relayed_ref, out_ref, mixed_ref, sems):
+    def kernel(w_ref, early_ref, relayed_ref, out_ref, mixed_ref, sems):
+        relayed_at = pl.multiple_of((1 - lax.axis_index("dp") % 2) * 2 * tokens, tokens)
         copies = []
         for g in range(heads_kv):
             cut = slice(g * HD, (g + 1) * HD)
-            picked = jnp.concatenate(
-                [w_ref[g, :, 0:tokens], w_ref[g, :, 2 * tokens : 3 * tokens]], axis=1
+            mixed = early_ref[g] + jnp.dot(
+                w_ref[g, :, pl.ds(relayed_at, tokens)],
+                relayed_ref[:, cut],
+                preferred_element_type=jnp.float32,
             )
-            oldest, _, last, _ = in_order(None, leapt_ref[:, cut], relayed_ref[:, cut], None)
-            values = jnp.concatenate([oldest, last], axis=0)
-            mixed = early_ref[g] + jnp.dot(picked, values, preferred_element_type=jnp.float32)
             for j in range(groups):
                 mixed_ref[:, g * span + j * HD : g * span + (j + 1) * HD] = mixed[
                     j * tokens : (j + 1) * tokens, :
@@ -417,7 +425,7 @@
     return pl.pallas_call(
         kernel,
         out_shape=jax.ShapeDtypeStruct((1, tokens, heads_kv * span), jnp.bfloat16),
-        in_specs=[pl.BlockSpec(memory_space=pltpu.VMEM)] * 4,
+        in_specs=[pl.BlockSpec(memory_space=pltpu.VMEM)] * 3,
         out_specs=pl.BlockSpec(memory_space=pltpu.HBM),
         scratch_shapes=[
             pltpu.VMEM((tokens, heads_kv * span), jnp.bfloat16),
@@ -430,7 +438,7 @@
             transcendentals=0,
         ),
         name="weighted_values",
-    )(weights, early, leapt, relayed)
+    )(weights, early, relayed)
 
 
 def on_device(
@@ -514,8 +522,8 @@
         partial = partial[:, 0] + came.astype(jnp.float32)
     value = partial[0].astype(jnp.bfloat16)
     two_before, leapt, relayed = preceding(value, True)
-    early = weighted_values_early(weights, two_before, value)
-    attended = weighted_values(weights, early, leapt, relayed)
+    early = weighted_values_early(weights, two_before, leapt, value)
+    attended = weighted_values(weights, early, relayed)
     return (new_master, new_first, new_second, attended)
 
 

time: 95 us -> 94.7 us (level)
  no operation moved by 1% of the time
where the time goes in v7:
time: 94.7 us; the launch traced here: 94.4 us
  starting transfers between devices  40.2 us (42%)
  waiting for transfers between devices  37.4 us (39%)
  Pallas kernels  9.88 us (10%)
  local copies, waits for them, and re-layouts  3.71 us (4%)
  other arithmetic  1.62 us (2%)
  between operations  1.57 us (2%)
    ppermute x19, waiting for transfers between devices, swapped(): return lax.ppermute(block, ALL, [(i, i ^ mask) for i in range(total)])  34.2 us
    ppermute x19, starting transfers between devices, swapped(): return lax.ppermute(block, ALL, [(i, i ^ mask) for i in range(total)])  23.6 us
    ppermute x2, starting transfers between devices, preceding(): lax.ppermute(block, 'dp', [(i, (i + 2) % n_dp) for i in range(reach)])  9.88 us
    ppermute x2, starting transfers between devices, preceding(): lax.ppermute(block, 'dp', [leap for leap in leaps if leap[1] < n_dp])  6.77 us
    pallas_call x1, Pallas kernels, attention_weights(): pl.pallas_call(kernel, grid=(heads_kv,), out_shape=jax.ShapeDtypeStruct((...  4.25 us
    unnamed x18, local copies, waits for them, and re-layouts  3.69 us
    ppermute x2, waiting for transfers between devices, preceding(): lax.ppermute(block, 'dp', [(i, (i + 2) % n_dp) for i in range(reach)])  2.8 us
  transfers between devices with their start and end apart: 23, of which 12 were waited for; matrix products, arithmetic and copies ran while one was open for 2% of the time, Pallas kernels for 8%

profile of v7, /device:TPU:0, one launch (start us, length us, event | category | flops | bytes accessed | tf_op | source)
XLA Modules:
  0.0 94.4 jit_solution(10421189743098129611)
XLA Ops:
  0.6 1.6 %copy-done = bf16[8,256,512]{2,1,0:T(8,128)(2,1)S(1)} copy-done((bf16[8,256,512]{2,1,0:T(8,128)(2,1)S(1)}, bf16[8,256,512]{2,1,0:T(8,128)(2,1)}, u32[]{:S(2)}) %copy-start) | copy-done | bytes 2097176
  2.2 0.2 blocks_taken.3
  2.4 3.0 %collective-permute-start = (bf16[4,256,256]{2,1,0:T(8,128)(2,1)S(1)}, bf16[4,256,256]{2,1,0:T(8,128)(2,1)S(1)}, u32[]{:S(2)}, u32[]{:S(2)}) collective-permute-start(bf16[4,256,256]{2,1,0:T(8,128)(2,1)S(1)} %get-tuple-element.35), channel_id=1, source_target_pairs={{0,4},{1,5},{2,6},{3,7},{4,0},{5,1},{6,2},{7,3},{8,12},{9,13},{10,... | collective-permute-start | bytes 1572872 | tf_op jit(solution)/shard_map/ppermute | solution.py:27
  5.4 1.6 %collective-permute-start.1 = (bf16[4,256,256]{2,1,0:T(8,128)(2,1)S(1)}, bf16[4,256,256]{2,1,0:T(8,128)(2,1)S(1)}, u32[]{:S(2)}, u32[]{:S(2)}) collective-permute-start(bf16[4,256,256]{2,1,0:T(8,128)(2,1)S(1)} %get-tuple-element.36), channel_id=1, source_target_pairs={{0,8},{1,9},{2,10},{3,11},{4,12},{5,13},{6,14},{7,15},{8,0},{9,1},... | collective-permute-start | bytes 1572872 | tf_op jit(solution)/shard_map/ppermute | solution.py:27
  7.0 1.6 %copy-done.5 = bf16[1,128,8192]{2,1,0:T(8,128)(2,1)S(1)} copy-done((bf16[1,128,8192]{2,1,0:T(8,128)(2,1)S(1)}, bf16[1,128,8192]{2,1,0:T(8,128)(2,1)}, u32[]{:S(2)}) %copy-start.5) | copy-done | bytes 2097176
  8.6 0.3 pack_hidden.1
  8.9 1.6 %collective-permute-start.4 = (bf16[128,2048]{1,0:T(8,128)(2,1)S(1)}, bf16[128,2048]{1,0:T(8,128)(2,1)S(1)}, u32[]{:S(2)}, u32[]{:S(2)}) collective-permute-start(bf16[128,2048]{1,0:T(8,128)(2,1)S(1)} %get-tuple-element.38), channel_id=1, source_target_pairs={{0,2},{1,3},{2,0},{3,1},{4,6},{5,7},{6,4},{7,5},{8,10},{9,11},{10,... | collective-permute-start | bytes 1572872 | tf_op jit(solution)/shard_map/ppermute | solution.py:27
  10.5 0.2 blocks_taken.2
  10.7 6.7 %collective-permute-done.refs_1_ = bf16[4,256,256]{2,1,0:T(8,128)(2,1)S(1)} collective-permute-done((bf16[4,256,256]{2,1,0:T(8,128)(2,1)S(1)}, bf16[4,256,256]{2,1,0:T(8,128)(2,1)S(1)}, u32[]{:S(2)}, u32[]{:S(2)}) %collective-permute-start) | collective-permute-done | bytes 524320 | tf_op jit(solution)/shard_map/ppermute | solution.py:27
  17.3 1.5 %collective-permute-done.1.refs_1_ = bf16[4,256,256]{2,1,0:T(8,128)(2,1)S(1)} collective-permute-done((bf16[4,256,256]{2,1,0:T(8,128)(2,1)S(1)}, bf16[4,256,256]{2,1,0:T(8,128)(2,1)S(1)}, u32[]{:S(2)}, u32[]{:S(2)}) %collective-permute-start.1) | collective-permute-done | bytes 524320 | tf_op jit(solution)/shard_map/ppermute | solution.py:27
  18.8 0.1 first_half_sums.6
  18.8 0.4 collective-permute-start.5
  19.3 0.1 first_half_sums.4
  19.4 1.8 %collective-permute-start.2 = (bf16[2,256,256]{2,1,0:T(8,128)(2,1)S(1)}, bf16[2,256,256]{2,1,0:T(8,128)(2,1)S(1)}, u32[]{:S(2)}, u32[]{:S(2)}) collective-permute-start(bf16[2,256,256]{2,1,0:T(8,128)(2,1)S(1)} %bitcast.24), channel_id=1, source_target_pairs={{0,8},{1,9},{2,10},{3,11},{4,12},{5,13},{6,14},{7,15},{8,0},{9,1},... | collective-permute-start | bytes 786440 | tf_op jit(solution)/shard_map/ppermute | solution.py:27
  21.2 0.0 collective-permute-start.8
  21.2 4.6 %collective-permute-done.5.refs_2_ = bf16[2,256,256]{2,1,0:T(8,128)(2,1)S(1)} collective-permute-done((bf16[2,256,256]{2,1,0:T(8,128)(2,1)S(1)}, bf16[2,256,256]{2,1,0:T(8,128)(2,1)S(1)}, u32[]{:S(2)}, u32[]{:S(2)}) %collective-permute-start.5) | collective-permute-done | bytes 262176 | tf_op jit(solution)/shard_map/ppermute | solution.py:27
  25.8 0.1 first_half_sums.7
  25.8 2.7 %collective-permute-start.6 = (bf16[1,256,256]{2,1,0:T(8,128)(2,1)S(1)}, bf16[1,256,256]{2,1,0:T(8,128)(2,1)S(1)}, u32[]{:S(2)}, u32[]{:S(2)}) collective-permute-start(bf16[1,256,256]{2,1,0:T(8,128)(2,1)S(1)} %bitcast.27), channel_id=1, source_target_pairs={{0,16},{1,17},{2,18},{3,19},{4,20},{5,21},{6,22},{7,23},{8,24},{9,... | collective-permute-start | bytes 393224 | tf_op jit(solution)/shard_map/ppermute | solution.py:27
  28.5 0.0 collective-permute-done.2.refs_2_
  28.5 0.1 first_half_sums.5
  28.5 0.5 collective-permute-start.3
  29.0 0.0 collective-permute-start.10
  29.0 0.4 staged.1
  29.4 8.0 %collective-permute-done.6.refs_3_ = bf16[1,256,256]{2,1,0:T(8,128)(2,1)S(1)} collective-permute-done((bf16[1,256,256]{2,1,0:T(8,128)(2,1)S(1)}, bf16[1,256,256]{2,1,0:T(8,128)(2,1)S(1)}, u32[]{:S(2)}, u32[]{:S(2)}) %collective-permute-start.6) | collective-permute-done | bytes 131104 | tf_op jit(solution)/shard_map/ppermute | solution.py:27
  37.4 0.3 fresh_rows.3.first_ref
  37.7 0.1 collective-permute-start.15
  37.8 1.9 %collective-permute-done.3.refs_3_ = bf16[1,256,256]{2,1,0:T(8,128)(2,1)S(1)} collective-permute-done((bf16[1,256,256]{2,1,0:T(8,128)(2,1)S(1)}, bf16[1,256,256]{2,1,0:T(8,128)(2,1)S(1)}, u32[]{:S(2)}, u32[]{:S(2)}) %collective-permute-start.3) | collective-permute-done | bytes 131104 | tf_op jit(solution)/shard_map/ppermute | solution.py:27
  39.7 0.3 fresh_rows.2.first_ref
  40.0 1.0 %collective-permute-start.7 = (bf16[256,256]{1,0:T(8,128)(2,1)S(1)}, bf16[256,256]{1,0:T(8,128)(2,1)S(1)}, u32[]{:S(2)}, u32[]{:S(2)}) collective-permute-start(bf16[256,256]{1,0:T(8,128)(2,1)S(1)} %fresh_rows.2.first_ref), channel_id=1, source_target_pairs={{0,16},{1,17},{2,18},{3,19},{4,20},{5,21},{6,22},{7,23},{8,24},{9,... | collective-permute-start | bytes 393224 | tf_op jit(solution)/shard_map/ppermute | solution.py:27
  41.0 9.7 %collective-permute-start.12 = (bf16[144,512]{1,0:T(8,128)(2,1)S(1)}, bf16[144,512]{1,0:T(8,128)(2,1)S(1)}, u32[]{:S(2)}, u32[]{:S(2)}) collective-permute-start(bf16[144,512]{1,0:T(8,128)(2,1)S(1)} %keys_and_numbers.1.rest_3_), channel_id=1, source_target_pairs={{0,8},{4,12},{8,16},{12,20},{16,24},{20,28},{1,9},{5,13},{9,17},{1... | collective-permute-start | bytes 442376 | tf_op jit(solution)/shard_map/ppermute | solution.py:33
  50.8 0.0 collective-permute-done.15.second_ref
  50.8 0.1 collective-permute-start.16
  50.9 0.0 collective-permute-done.8.refs_1_
  50.9 1.0 %collective-permute-start.9 = (bf16[512,256]{1,0:T(8,128)(2,1)S(1)}, bf16[512,256]{1,0:T(8,128)(2,1)S(1)}, u32[]{:S(2)}, u32[]{:S(2)}) collective-permute-start(bf16[512,256]{1,0:T(8,128)(2,1)S(1)} %one_below.4.first_ref), channel_id=1, source_target_pairs={{0,8},{1,9},{2,10},{3,11},{4,12},{5,13},{6,14},{7,15},{8,0},{9,1},... | collective-permute-start | bytes 786440 | tf_op jit(solution)/shard_map/ppermute | solution.py:27
  51.9 3.0 %collective-permute-start.11 = (bf16[144,512]{1,0:T(8,128)(2,1)S(1)}, bf16[144,512]{1,0:T(8,128)(2,1)S(1)}, u32[]{:S(2)}, u32[]{:S(2)}) collective-permute-start(bf16[144,512]{1,0:T(8,128)(2,1)S(1)} %keys_and_numbers.1.rest_3_), channel_id=1, source_target_pairs={{0,4},{4,16},{8,12},{12,24},{16,20},{24,28},{1,5},{5,17},{9,13},{1... | collective-permute-start | bytes 442376 | tf_op jit(solution)/shard_map/ppermute | solution.py:35
  54.9 0.0 collective-permute-done.12.rest_0_
  54.9 3.9 %collective-permute-start.13 = (bf16[144,512]{1,0:T(8,128)(2,1)S(1)}, bf16[144,512]{1,0:T(8,128)(2,1)S(1)}, u32[]{:S(2)}, u32[]{:S(2)}) collective-permute-start(bf16[144,512]{1,0:T(8,128)(2,1)S(1)} %collective-permute-done.12.rest_0_), channel_id=1, source_target_pairs={{0,4},{1,5},{2,6},{3,7},{4,0},{5,1},{6,2},{7,3},{8,12},{9,13},{10,... | collective-permute-start | bytes 442376 | tf_op jit(solution)/shard_map/ppermute | solution.py:27
  58.9 0.1 collective-permute-start.17
  59.0 0.4 collective-permute-done.11.rest_1_
  59.4 2.5 %collective-permute-done.13.rest_2_ = bf16[144,512]{1,0:T(8,128)(2,1)S(1)} collective-permute-done((bf16[144,512]{1,0:T(8,128)(2,1)S(1)}, bf16[144,512]{1,0:T(8,128)(2,1)S(1)}, u32[]{:S(2)}, u32[]{:S(2)}) %collective-permute-start.13) | collective-permute-done | bytes 147488 | tf_op jit(solution)/shard_map/ppermute | solution.py:27
  62.0 2.3 %collective-permute-start.14 = (bf16[1024,256]{1,0:T(8,128)(2,1)S(1)}, bf16[1024,256]{1,0:T(8,128)(2,1)S(1)}, u32[]{:S(2)}, u32[]{:S(2)}) collective-permute-start(bf16[1024,256]{1,0:T(8,128)(2,1)S(1)} %one_below.5.refs_4_), channel_id=1, source_target_pairs={{0,4},{1,5},{2,6},{3,7},{4,0},{5,1},{6,2},{7,3},{8,12},{9,13},{10,... | collective-permute-start | bytes 1572872 | tf_op jit(solution)/shard_map/ppermute | solution.py:27
  64.9 0.0 copy-start.6
  64.9 0.7 projected_first.1.refs_4_
  65.6 0.5 copy-done.6
  66.1 4.2 %attention_weights.1.w_ref = bf16[4,1024,512]{2,1,0:T(8,128)(2,1)S(1)} custom-call(s32[1]{0:T(128)S(6)} %copy.13.used_ref, bf16[1,128,4096]{2,1,0:T(8,128)(2,1)S(1)} %copy-done.6, bf16[144,512]{1,0:T(8,128)(2,1)S(1)} %collective-permute-done.12.rest_0_, bf16[144,512]{1,0:T(8,128)(2,1)S(1)} %collective-permute-done.11.rest_1_, ...), custom_call_target="tpu_custom_call" | custom-call | flops 536870912 | bytes 5242880 | tf_op jit(solution)/shard_map/attention_weights/pallas_call | solution.py:343
  70.4 0.0 collective-permute-done.17.refs_6_
  70.4 2.8 %collective-permute-done.14.refs_5_ = bf16[1024,256]{1,0:T(8,128)(2,1)S(1)} collective-permute-done((bf16[1024,256]{1,0:T(8,128)(2,1)S(1)}, bf16[1024,256]{1,0:T(8,128)(2,1)S(1)}, u32[]{:S(2)}, u32[]{:S(2)}) %collective-permute-start.14) | collective-permute-done | bytes 524320 | tf_op jit(solution)/shard_map/ppermute | solution.py:27
  73.2 0.7 projected_last.1
  74.0 0.1 collective-permute-start.18
  74.1 1.5 %collective-permute-done.18 = bf16[2,128,512]{2,1,0:T(8,128)(2,1)S(1)} collective-permute-done((bf16[2,128,512]{2,1,0:T(8,128)(2,1)S(1)}, bf16[2,128,512]{2,1,0:T(8,128)(2,1)S(1)}, u32[]{:S(2)}, u32[]{:S(2)}) %collective-permute-start.18) | collective-permute-done | bytes 262176 | tf_op jit(solution)/shard_map/ppermute | solution.py:27
  75.6 0.1 add_bitcast_fusion
  75.7 1.6 %collective-permute-start.19 = (bf16[1,128,512]{2,1,0:T(8,128)(2,1)S(1)}, bf16[1,128,512]{2,1,0:T(8,128)(2,1)S(1)}, u32[]{:S(2)}, u32[]{:S(2)}) collective-permute-start(bf16[1,128,512]{2,1,0:T(8,128)(2,1)S(1)} %fusion.4), channel_id=1, source_target_pairs={{0,2},{1,3},{2,0},{3,1},{4,6},{5,7},{6,4},{7,5},{8,10},{9,11},{10,... | collective-permute-start | bytes 393224 | tf_op jit(solution)/shard_map/ppermute | solution.py:27
  77.3 0.1 add_bitcast_fusion.1
  77.3 4.0 %collective-permute-done.19 = bf16[1,128,512]{2,1,0:T(8,128)(2,1)S(1)} collective-permute-done((bf16[1,128,512]{2,1,0:T(8,128)(2,1)S(1)}, bf16[1,128,512]{2,1,0:T(8,128)(2,1)S(1)}, u32[]{:S(2)}, u32[]{:S(2)}) %collective-permute-start.19) | collective-permute-done | bytes 131104 | tf_op jit(solution)/shard_map/ppermute | solution.py:27
  81.3 0.2 collective-permute-start.20
  81.5 0.1 add_bitcast_fusion.2
  81.6 3.8 %collective-permute-start.21 = (bf16[128,512]{1,0:T(8,128)(2,1)S(1)}, bf16[128,512]{1,0:T(8,128)(2,1)S(1)}, u32[]{:S(2)}, u32[]{:S(2)}) collective-permute-start(bf16[128,512]{1,0:T(8,128)(2,1)S(1)} %fusion.3.own_ref), channel_id=1, source_target_pairs={{0,4},{4,16},{8,12},{12,24},{16,20},{24,28},{1,5},{5,17},{9,13},{1... | collective-permute-start | bytes 393224 | tf_op jit(solution)/shard_map/ppermute | solution.py:35
  85.3 2.8 %collective-permute-done.20.before_ref = bf16[128,512]{1,0:T(8,128)(2,1)S(1)} collective-permute-done((bf16[128,512]{1,0:T(8,128)(2,1)S(1)}, bf16[128,512]{1,0:T(8,128)(2,1)S(1)}, u32[]{:S(2)}, u32[]{:S(2)}) %collective-permute-start.20) | collective-permute-done | bytes 131104 | tf_op jit(solution)/shard_map/ppermute | solution.py:33
  88.1 2.0 %collective-permute-start.22 = (bf16[128,512]{1,0:T(8,128)(2,1)S(1)}, bf16[128,512]{1,0:T(8,128)(2,1)S(1)}, u32[]{:S(2)}, u32[]{:S(2)}) collective-permute-start(bf16[128,512]{1,0:T(8,128)(2,1)S(1)} %collective-permute-done.20.before_ref), channel_id=1, source_target_pairs={{0,4},{1,5},{2,6},{3,7},{4,0},{5,1},{6,2},{7,3},{8,12},{9,13},{10,... | collective-permute-start | bytes 393224 | tf_op jit(solution)/shard_map/ppermute | solution.py:27
  90.1 1.4 %multiply_subtract_fusion = (f32[256,512]{1,0:T(8,128)}, f32[256,512]{1,0:T(8,128)}, f32[256,512]{1,0:T(8,128)}) fusion(f32[256,512]{1,0:T(8,128)S(1)} %copy-done.2, f32[256,256]{1,0:T(8,128)S(1)} %add_bitcast_fusion.1, f32[256,256]{1,0:T(8,128)S(1)} %add_bitcast_fusion.2, f32[256,512]{1,0:T(8,128)S(1)} %copy-done.3, f32[256,512]{1,0:T(8,128)S(1)} %copy-done.4), kind=kLoop, calls=%fused_computation.4 | loop fusion | flops 2097152 | bytes 3670016 | tf_op jit(solution)/shard_map/sub | solution.py:50
  91.5 0.0 collective-permute-done.21.leapt_ref
  91.5 1.0 %weighted_values_early.1.early_ref = f32[4,1024,128]{2,1,0:T(8,128)S(1)} custom-call(bf16[4,1024,512]{2,1,0:T(8,128)(2,1)S(1)} %attention_weights.1.w_ref, bf16[128,512]{1,0:T(8,128)(2,1)S(1)} %collective-permute-done.20.before_ref, bf16[128,512]{1,0:T(8,128)(2,1)S(1)} %collective-permute-done.21.leapt_ref, bf16[128,512]{1,0:T(8,128)(2,1)S(1)} %fusion.3.own_ref), custom_call_target="tpu_custom_call" | custom-call | flops 268435456 | bytes 2097152 | tf_op jit(solution)/shard_map/weighted_values_early/pallas_call | solution.py:384
  92.5 0.6 collective-permute-done.22.relayed_ref
  93.1 1.3 %weighted_values.1 = bf16[1,128,4096]{2,1,0:T(8,128)(2,1)} custom-call(bf16[4,1024,512]{2,1,0:T(8,128)(2,1)S(1)} %attention_weights.1.w_ref, f32[4,1024,128]{2,1,0:T(8,128)S(1)} %weighted_values_early.1.early_ref, bf16[128,512]{1,0:T(8,128)(2,1)S(1)} %collective-permute-done.22.relayed_ref), custom_call_target="tpu_custom_call" | custom-call | flops 268435456 | bytes 2097152 | tf_op jit(solution)/shard_map/weighted_values/pallas_call | solution.py:425
  (26 shorter events, 0.2 us)
Async XLA Ops:
  0.6 1.6 %copy-start = (bf16[8,256,512]{2,1,0:T(8,128)(2,1)S(1)}, bf16[8,256,512]{2,1,0:T(8,128)(2,1)}, u32[]{:S(2)}) copy-start(bf16[8,256,512]{2,1,0:T(8,128)(2,1)} %terms_ref.3) | copy-start | bytes 6291460
  2.2 8.2 %copy-start.1 = (bf16[8,256,512]{2,1,0:T(8,128)(2,1)S(1)}, bf16[8,256,512]{2,1,0:T(8,128)(2,1)}, u32[]{:S(2)}) copy-start(bf16[8,256,512]{2,1,0:T(8,128)(2,1)} %terms_ref.3) | copy-start | bytes 6291460
  2.4 14.9 %collective-permute-start = (bf16[4,256,256]{2,1,0:T(8,128)(2,1)S(1)}, bf16[4,256,256]{2,1,0:T(8,128)(2,1)S(1)}, u32[]{:S(2)}, u32[]{:S(2)}) collective-permute-start(bf16[4,256,256]{2,1,0:T(8,128)(2,1)S(1)} %get-tuple-element.35), channel_id=1, source_target_pairs={{0,4},{1,5},{2,6},{3,7},{4,0},{5,1},{6,2},{7,3},{8,12},{9,13},{10,... | collective-permute-start | bytes 1572872 | tf_op jit(solution)/shard_map/ppermute | solution.py:27
  5.4 13.4 %collective-permute-start.1 = (bf16[4,256,256]{2,1,0:T(8,128)(2,1)S(1)}, bf16[4,256,256]{2,1,0:T(8,128)(2,1)S(1)}, u32[]{:S(2)}, u32[]{:S(2)}) collective-permute-start(bf16[4,256,256]{2,1,0:T(8,128)(2,1)S(1)} %get-tuple-element.36), channel_id=1, source_target_pairs={{0,8},{1,9},{2,10},{3,11},{4,12},{5,13},{6,14},{7,15},{8,0},{9,1},... | collective-permute-start | bytes 1572872 | tf_op jit(solution)/shard_map/ppermute | solution.py:27
  7.0 1.6 %copy-start.5 = (bf16[1,128,8192]{2,1,0:T(8,128)(2,1)S(1)}, bf16[1,128,8192]{2,1,0:T(8,128)(2,1)}, u32[]{:S(2)}) copy-start(bf16[1,128,8192]{2,1,0:T(8,128)(2,1)} %param.15) | copy-start | bytes 6291460
  8.6 2.1 %copy-start.7 = (bf16[1,128,512]{2,1,0:T(8,128)(2,1)S(1)}, bf16[1,128,512]{2,1,0:T(8,128)(2,1)}, u32[]{:S(2)}) copy-start(bf16[1,128,512]{2,1,0:T(8,128)(2,1)} %key_ref.1) | copy-start | bytes 393220
  8.6 2.1 %copy-start.8 = (s32[1,128]{1,0:T(1,128)S(1)}, s32[1,128]{1,0:T(1,128)}, u32[]{:S(2)}) copy-start(s32[1,128]{1,0:T(1,128)} %seg_ref.1) | copy-start | bytes 1540
  8.9 28.9 %collective-permute-start.4 = (bf16[128,2048]{1,0:T(8,128)(2,1)S(1)}, bf16[128,2048]{1,0:T(8,128)(2,1)S(1)}, u32[]{:S(2)}, u32[]{:S(2)}) collective-permute-start(bf16[128,2048]{1,0:T(8,128)(2,1)S(1)} %get-tuple-element.38), channel_id=1, source_target_pairs={{0,2},{1,3},{2,0},{3,1},{4,6},{5,7},{6,4},{7,5},{8,10},{9,11},{10,... | collective-permute-start | bytes 1572872 | tf_op jit(solution)/shard_map/ppermute | solution.py:27
  18.8 6.9 %collective-permute-start.5 = (bf16[2,256,256]{2,1,0:T(8,128)(2,1)S(1)}, bf16[2,256,256]{2,1,0:T(8,128)(2,1)S(1)}, u32[]{:S(2)}, u32[]{:S(2)}) collective-permute-start(bf16[2,256,256]{2,1,0:T(8,128)(2,1)S(1)} %bitcast.25), channel_id=1, source_target_pairs={{0,4},{1,5},{2,6},{3,7},{4,0},{5,1},{6,2},{7,3},{8,12},{9,13},{10,... | collective-permute-start | bytes 786440 | tf_op jit(solution)/shard_map/ppermute | solution.py:27
  19.3 9.7 %copy-start.2 = (f32[256,512]{1,0:T(8,128)S(1)}, f32[256,512]{1,0:T(8,128)}, u32[]{:S(2)}) copy-start(f32[256,512]{1,0:T(8,128)} %refs_0_.1) | copy-start | bytes 1572868
  19.3 9.7 %copy-start.3 = (f32[256,512]{1,0:T(8,128)S(1)}, f32[256,512]{1,0:T(8,128)}, u32[]{:S(2)}) copy-start(f32[256,512]{1,0:T(8,128)} %refs_1_.1) | copy-start | bytes 1572868
  19.3 9.7 %copy-start.4 = (f32[256,512]{1,0:T(8,128)S(1)}, f32[256,512]{1,0:T(8,128)}, u32[]{:S(2)}) copy-start(f32[256,512]{1,0:T(8,128)} %refs_2_.1) | copy-start | bytes 1572868
  19.4 9.1 %collective-permute-start.2 = (bf16[2,256,256]{2,1,0:T(8,128)(2,1)S(1)}, bf16[2,256,256]{2,1,0:T(8,128)(2,1)S(1)}, u32[]{:S(2)}, u32[]{:S(2)}) collective-permute-start(bf16[2,256,256]{2,1,0:T(8,128)(2,1)S(1)} %bitcast.24), channel_id=1, source_target_pairs={{0,8},{1,9},{2,10},{3,11},{4,12},{5,13},{6,14},{7,15},{8,0},{9,1},... | collective-permute-start | bytes 786440 | tf_op jit(solution)/shard_map/ppermute | solution.py:27
  21.2 29.7 %collective-permute-start.8 = (bf16[128,2048]{1,0:T(8,128)(2,1)S(1)}, bf16[128,2048]{1,0:T(8,128)(2,1)S(1)}, u32[]{:S(2)}, u32[]{:S(2)}) collective-permute-start(bf16[128,2048]{1,0:T(8,128)(2,1)S(1)} %get-tuple-element.45), channel_id=1, source_target_pairs={{0,1},{1,0},{2,3},{3,2},{4,5},{5,4},{6,7},{7,6},{8,9},{9,8},{10,11... | collective-permute-start | bytes 1572872 | tf_op jit(solution)/shard_map/ppermute | solution.py:27
  25.8 11.6 %collective-permute-start.6 = (bf16[1,256,256]{2,1,0:T(8,128)(2,1)S(1)}, bf16[1,256,256]{2,1,0:T(8,128)(2,1)S(1)}, u32[]{:S(2)}, u32[]{:S(2)}) collective-permute-start(bf16[1,256,256]{2,1,0:T(8,128)(2,1)S(1)} %bitcast.27), channel_id=1, source_target_pairs={{0,16},{1,17},{2,18},{3,19},{4,20},{5,21},{6,22},{7,23},{8,24},{9,... | collective-permute-start | bytes 393224 | tf_op jit(solution)/shard_map/ppermute | solution.py:27
  28.5 11.2 %collective-permute-start.3 = (bf16[1,256,256]{2,1,0:T(8,128)(2,1)S(1)}, bf16[1,256,256]{2,1,0:T(8,128)(2,1)S(1)}, u32[]{:S(2)}, u32[]{:S(2)}) collective-permute-start(bf16[1,256,256]{2,1,0:T(8,128)(2,1)S(1)} %bitcast.26), channel_id=1, source_target_pairs={{0,16},{1,17},{2,18},{3,19},{4,20},{5,21},{6,22},{7,23},{8,24},{9,... | collective-permute-start | bytes 393224 | tf_op jit(solution)/shard_map/ppermute | solution.py:27
  29.0 30.0 %collective-permute-start.10 = (bf16[128,2048]{1,0:T(8,128)(2,1)S(1)}, bf16[128,2048]{1,0:T(8,128)(2,1)S(1)}, u32[]{:S(2)}, u32[]{:S(2)}) collective-permute-start(bf16[128,2048]{1,0:T(8,128)(2,1)S(1)} %get-tuple-element.47), channel_id=1, source_target_pairs={{0,3},{1,2},{2,1},{3,0},{4,7},{5,6},{6,5},{7,4},{8,11},{9,10},{10,... | collective-permute-start | bytes 1572872 | tf_op jit(solution)/shard_map/ppermute | solution.py:27
  37.7 13.0 %collective-permute-start.15 = (bf16[256,256]{1,0:T(8,128)(2,1)S(1)}, bf16[256,256]{1,0:T(8,128)(2,1)S(1)}, u32[]{:S(2)}, u32[]{:S(2)}) collective-permute-start(bf16[256,256]{1,0:T(8,128)(2,1)S(1)} %fresh_rows.3.first_ref), channel_id=1, source_target_pairs={{0,16},{1,17},{2,18},{3,19},{4,20},{5,21},{6,22},{7,23},{8,24},{9,... | collective-permute-start | bytes 393224 | tf_op jit(solution)/shard_map/ppermute | solution.py:27
  40.0 10.9 %collective-permute-start.7 = (bf16[256,256]{1,0:T(8,128)(2,1)S(1)}, bf16[256,256]{1,0:T(8,128)(2,1)S(1)}, u32[]{:S(2)}, u32[]{:S(2)}) collective-permute-start(bf16[256,256]{1,0:T(8,128)(2,1)S(1)} %fresh_rows.2.first_ref), channel_id=1, source_target_pairs={{0,16},{1,17},{2,18},{3,19},{4,20},{5,21},{6,22},{7,23},{8,24},{9,... | collective-permute-start | bytes 393224 | tf_op jit(solution)/shard_map/ppermute | solution.py:27
  41.0 13.9 %collective-permute-start.12 = (bf16[144,512]{1,0:T(8,128)(2,1)S(1)}, bf16[144,512]{1,0:T(8,128)(2,1)S(1)}, u32[]{:S(2)}, u32[]{:S(2)}) collective-permute-start(bf16[144,512]{1,0:T(8,128)(2,1)S(1)} %keys_and_numbers.1.rest_3_), channel_id=1, source_target_pairs={{0,8},{4,12},{8,16},{12,20},{16,24},{20,28},{1,9},{5,13},{9,17},{1... | collective-permute-start | bytes 442376 | tf_op jit(solution)/shard_map/ppermute | solution.py:33
  50.8 8.0 %collective-permute-start.16 = (bf16[512,256]{1,0:T(8,128)(2,1)S(1)}, bf16[512,256]{1,0:T(8,128)(2,1)S(1)}, u32[]{:S(2)}, u32[]{:S(2)}) collective-permute-start(bf16[512,256]{1,0:T(8,128)(2,1)S(1)} %one_below.6.first_ref), channel_id=1, source_target_pairs={{0,4},{1,5},{2,6},{3,7},{4,0},{5,1},{6,2},{7,3},{8,12},{9,13},{10,... | collective-permute-start | bytes 786440 | tf_op jit(solution)/shard_map/ppermute | solution.py:27
  50.9 11.0 %collective-permute-start.9 = (bf16[512,256]{1,0:T(8,128)(2,1)S(1)}, bf16[512,256]{1,0:T(8,128)(2,1)S(1)}, u32[]{:S(2)}, u32[]{:S(2)}) collective-permute-start(bf16[512,256]{1,0:T(8,128)(2,1)S(1)} %one_below.4.first_ref), channel_id=1, source_target_pairs={{0,8},{1,9},{2,10},{3,11},{4,12},{5,13},{6,14},{7,15},{8,0},{9,1},... | collective-permute-start | bytes 786440 | tf_op jit(solution)/shard_map/ppermute | solution.py:27
  51.9 7.5 %collective-permute-start.11 = (bf16[144,512]{1,0:T(8,128)(2,1)S(1)}, bf16[144,512]{1,0:T(8,128)(2,1)S(1)}, u32[]{:S(2)}, u32[]{:S(2)}) collective-permute-start(bf16[144,512]{1,0:T(8,128)(2,1)S(1)} %keys_and_numbers.1.rest_3_), channel_id=1, source_target_pairs={{0,4},{4,16},{8,12},{12,24},{16,20},{24,28},{1,5},{5,17},{9,13},{1... | collective-permute-start | bytes 442376 | tf_op jit(solution)/shard_map/ppermute | solution.py:35
  54.9 7.0 %collective-permute-start.13 = (bf16[144,512]{1,0:T(8,128)(2,1)S(1)}, bf16[144,512]{1,0:T(8,128)(2,1)S(1)}, u32[]{:S(2)}, u32[]{:S(2)}) collective-permute-start(bf16[144,512]{1,0:T(8,128)(2,1)S(1)} %collective-permute-done.12.rest_0_), channel_id=1, source_target_pairs={{0,4},{1,5},{2,6},{3,7},{4,0},{5,1},{6,2},{7,3},{8,12},{9,13},{10,... | collective-permute-start | bytes 442376 | tf_op jit(solution)/shard_map/ppermute | solution.py:27
  58.9 11.5 %collective-permute-start.17 = (bf16[1024,256]{1,0:T(8,128)(2,1)S(1)}, bf16[1024,256]{1,0:T(8,128)(2,1)S(1)}, u32[]{:S(2)}, u32[]{:S(2)}) collective-permute-start(bf16[1024,256]{1,0:T(8,128)(2,1)S(1)} %one_below.7.refs_5_), channel_id=1, source_target_pairs={{0,8},{1,9},{2,10},{3,11},{4,12},{5,13},{6,14},{7,15},{8,0},{9,1},... | collective-permute-start | bytes 1572872 | tf_op jit(solution)/shard_map/ppermute | solution.py:27
  62.0 11.3 %collective-permute-start.14 = (bf16[1024,256]{1,0:T(8,128)(2,1)S(1)}, bf16[1024,256]{1,0:T(8,128)(2,1)S(1)}, u32[]{:S(2)}, u32[]{:S(2)}) collective-permute-start(bf16[1024,256]{1,0:T(8,128)(2,1)S(1)} %one_below.5.refs_4_), channel_id=1, source_target_pairs={{0,4},{1,5},{2,6},{3,7},{4,0},{5,1},{6,2},{7,3},{8,12},{9,13},{10,... | collective-permute-start | bytes 1572872 | tf_op jit(solution)/shard_map/ppermute | solution.py:27
  64.9 1.2 %copy-start.6 = (bf16[1,128,4096]{2,1,0:T(8,128)(2,1)S(1)}, bf16[1,128,4096]{2,1,0:T(8,128)(2,1)}, u32[]{:S(2)}) copy-start(bf16[1,128,4096]{2,1,0:T(8,128)(2,1)} %q_ref.1) | copy-start | bytes 3145732
  74.0 1.6 %collective-permute-start.18 = (bf16[2,128,512]{2,1,0:T(8,128)(2,1)S(1)}, bf16[2,128,512]{2,1,0:T(8,128)(2,1)S(1)}, u32[]{:S(2)}, u32[]{:S(2)}) collective-permute-start(bf16[2,128,512]{2,1,0:T(8,128)(2,1)S(1)} %get-tuple-element.63), channel_id=1, source_target_pairs={{0,1},{1,0},{2,3},{3,2},{4,5},{5,4},{6,7},{7,6},{8,9},{9,8},{10,11... | collective-permute-start | bytes 786440 | tf_op jit(solution)/shard_map/ppermute | solution.py:27
  75.7 5.6 %collective-permute-start.19 = (bf16[1,128,512]{2,1,0:T(8,128)(2,1)S(1)}, bf16[1,128,512]{2,1,0:T(8,128)(2,1)S(1)}, u32[]{:S(2)}, u32[]{:S(2)}) collective-permute-start(bf16[1,128,512]{2,1,0:T(8,128)(2,1)S(1)} %fusion.4), channel_id=1, source_target_pairs={{0,2},{1,3},{2,0},{3,1},{4,6},{5,7},{6,4},{7,5},{8,10},{9,11},{10,... | collective-permute-start | bytes 393224 | tf_op jit(solution)/shard_map/ppermute | solution.py:27
  81.3 6.8 %collective-permute-start.20 = (bf16[128,512]{1,0:T(8,128)(2,1)S(1)}, bf16[128,512]{1,0:T(8,128)(2,1)S(1)}, u32[]{:S(2)}, u32[]{:S(2)}) collective-permute-start(bf16[128,512]{1,0:T(8,128)(2,1)S(1)} %fusion.3.own_ref), channel_id=1, source_target_pairs={{0,8},{4,12},{8,16},{12,20},{16,24},{20,28},{24,0},{28,4},{1,9},{5... | collective-permute-start | bytes 393224 | tf_op jit(solution)/shard_map/ppermute | solution.py:33
  81.6 9.9 %collective-permute-start.21 = (bf16[128,512]{1,0:T(8,128)(2,1)S(1)}, bf16[128,512]{1,0:T(8,128)(2,1)S(1)}, u32[]{:S(2)}, u32[]{:S(2)}) collective-permute-start(bf16[128,512]{1,0:T(8,128)(2,1)S(1)} %fusion.3.own_ref), channel_id=1, source_target_pairs={{0,4},{4,16},{8,12},{12,24},{16,20},{24,28},{1,5},{5,17},{9,13},{1... | collective-permute-start | bytes 393224 | tf_op jit(solution)/shard_map/ppermute | solution.py:35
  88.1 5.0 %collective-permute-start.22 = (bf16[128,512]{1,0:T(8,128)(2,1)S(1)}, bf16[128,512]{1,0:T(8,128)(2,1)S(1)}, u32[]{:S(2)}, u32[]{:S(2)}) collective-permute-start(bf16[128,512]{1,0:T(8,128)(2,1)S(1)} %collective-permute-done.20.before_ref), channel_id=1, source_target_pairs={{0,4},{1,5},{2,6},{3,7},{4,0},{5,1},{6,2},{7,3},{8,12},{9,13},{10,... | collective-permute-start | bytes 393224 | tf_op jit(solution)/shard_map/ppermute | solution.py:27
